TPU v7x, 128 devices: a whole 4x4x4 slice. The times are simulated.
128 devices in a mesh: outer: 4 (over z_lo, core), inner: 32 (over z_hi, x, y).
Axes of the slice: x: 4, y: 4, z: 4 (z_hi: 2, z_lo: 2; z = z_hi * 2 + z_lo), core: 2. Of those that a mesh axis runs over, the one named last changes fastest.
Arguments:
- queries: bfloat16 [16384, 512], P(('outer', 'inner')), may hold values from -2 to 2
- keys: bfloat16 [16384, 128], P(('outer', 'inner')), may hold values from -2 to 2
- values: bfloat16 [16384, 128], P(('outer', 'inner')), may hold values from -6 to 6
- saved_out: bfloat16 [16384, 512], P(('outer', 'inner')), may hold values from -4 to 4
- out_grad: bfloat16 [16384, 512], P(('outer', 'inner')), may hold values from -6 to 6
- log_sums: float32 [16384, 4], P(('outer', 'inner')), as said below
- positions: int32 [16384], P(('outer', 'inner')), may hold values from 0 to 16383, as said below
- segments: int32 [16384], P(('outer', 'inner')), may hold values from 0 to 8, as said below
Outputs:
- grad_queries: float32 [16384, 512], P(('outer', 'inner'))
- grad_keys: float32 [16384, 128], P(('outer', 'inner'))
- grad_values: float32 [16384, 128], P(('outer', 'inner'))
Inputs may be any that keep to these rules, and one draw needn't show every extreme that they name: log_sums[i, h] is the log of the sum over allowed j of exp(scores_h[i, j]) for these queries, keys, positions and segments. A permutation of the positions; on every device the first 64 rows hold the consecutive positions of one block c of 64 positions, in order, and the last 64 rows those of block 255 - c. `segments`: document ids never fall as the position rises, position 0 has id 0, and each id from 0 to 8 occurs: nine documents.
All inputs are finite; a program needn't handle non-finite values.
Results may differ from a plain program's by a relative error of at most 0.0029.
Values may be sent and summed in bfloat16 or wider, within the bound.
No kernel may reach another device: no remote copies, remote signals or barrier semaphores. Data moves between devices by JAX's collectives and lax.ppermute only.
A program may use at most 192 MiB of HBM per device.

v0:
```python
import math

import jax
import jax.numpy as jnp
from jax import lax
from jax.experimental import pallas as pl
from jax.experimental.pallas import tpu as pltpu
from jax.sharding import PartitionSpec as P

HEAD = 128
QH = 4
ROWS = 128
BLOCK = 64
STATS = 16
PLANE = 16
DEPTH = 4
PIECES = 2 * DEPTH
QBLOCKS = 2 * PIECES
KBLOCKS = 2 * PLANE
STACK = QH * BLOCK
TILE = 256
TILE_BLOCKS = TILE // BLOCK
SLOTS = 40
TOGETHER = 2
FAR = 1.0e9
AXES = ("outer", "inner")
LOG2E = math.log2(math.e)


def place(index):
    outer, inner = divmod(index, 32)
    return (inner // 16) * 2 + outer // 2, outer % 2, inner % 16


def index_of(z, core, spot):
    return ((z % 2) * 2 + core) * 32 + (z // 2) * 16 + spot


def along_z(array, shift):
    pairs = []
    for source in range(128):
        z, core, spot = place(source)
        pairs.append((source, index_of((z + shift) % DEPTH, core, spot)))
    return lax.ppermute(array, AXES, pairs)


def to_partner(array):
    pairs = []
    for source in range(128):
        z, core, spot = place(source)
        pairs.append((source, index_of(z, 1 - core, spot)))
    return lax.ppermute(array, AXES, pairs)


def over_plane(array):
    groups = [list(range(first, first + PLANE)) for first in (0, PLANE)]
    return lax.all_to_all(array, "inner", 0, 0, axis_index_groups=groups, tiled=True)


def pack_kernel(q_hbm, g_hbm, o_hbm, k_hbm, v_hbm, lse_hbm, pos_hbm, seg_hbm, qmsg_ref, kvmsg_ref, *scratch):
    (q_ref, g_ref, o_ref, k_ref, v_ref, lse_ref, pos_ref, seg_ref, sems) = scratch
    sources = (lse_hbm, pos_hbm, seg_hbm, g_hbm, o_hbm, q_hbm, k_hbm, v_hbm)
    targets = (lse_ref, pos_ref, seg_ref, g_ref, o_ref, q_ref, k_ref, v_ref)
    copies = [pltpu.make_async_copy(s, t, sems.at[i]) for i, (s, t) in enumerate(zip(sources, targets))]
    for copy in copies:
        copy.start()
    for copy in copies:
        copy.wait()
    row = lax.broadcasted_iota(jnp.int32, (8, ROWS), 0)
    lane = lax.broadcasted_iota(jnp.int32, (8, ROWS), 1)
    block = jnp.right_shift(pos_ref[...], 6).astype(jnp.float32)
    seg = seg_ref[...].astype(jnp.float32)
    tops = []
    for h in range(QH):
        cols = slice(h * HEAD, (h + 1) * HEAD)
        prod = g_ref[:, cols].astype(jnp.float32) * o_ref[:, cols].astype(jnp.float32)
        dot = jnp.sum(prod.T, axis=0, keepdims=True)
        lse = lse_ref[h : h + 1, :] * LOG2E
        tops.append(
            jnp.where(
                row == 0,
                lse,
                jnp.where(row == 1, dot, jnp.where(row == 2, block, jnp.where(row == 3, seg, 0.0))),
            )
        )
        for b in range(2):
            to = slice(h * BLOCK, (h + 1) * BLOCK)
            frm = slice(b * BLOCK, (b + 1) * BLOCK)
            qmsg_ref[b, to, 0:HEAD] = q_ref[frm, cols]
            qmsg_ref[b, to, HEAD : 2 * HEAD] = g_ref[frm, cols]
    for pair in range(2):
        first, second = tops[2 * pair], tops[2 * pair + 1]
        halves = (
            jnp.where(lane < BLOCK, first, pltpu.roll(second, BLOCK, 1)),
            jnp.where(lane < BLOCK, pltpu.roll(first, BLOCK, 1), second),
        )
        for b in range(2):
            full = halves[b]
            high = full.astype(jnp.bfloat16).astype(jnp.float32)
            middle = (full - high).astype(jnp.bfloat16).astype(jnp.float32)
            low = full - high - middle
            upper = jnp.where(row < 4, high, pltpu.roll(middle, 4, 0))
            lower = jnp.where(row < 4, low, 0.0)
            qmsg_ref[b, STACK : STACK + STATS, pair * ROWS : (pair + 1) * ROWS] = jnp.concatenate(
                [upper, lower], axis=0
            ).astype(jnp.bfloat16)
    tail = jnp.where(row == 0, block, jnp.where(row == 1, seg, 0.0))
    tail = jnp.concatenate([tail, jnp.zeros_like(tail)], axis=0).astype(jnp.bfloat16)
    for d in range(PLANE):
        kvmsg_ref[d, 0:ROWS, 0:HEAD] = k_ref[...]
        kvmsg_ref[d, 0:ROWS, HEAD : 2 * HEAD] = v_ref[...]
        kvmsg_ref[d, ROWS : ROWS + STATS, 0:ROWS] = tail
        kvmsg_ref[d, ROWS : ROWS + STATS, ROWS : 2 * ROWS] = jnp.zeros_like(tail)


def pack(queries, out_grad, saved_out, keys, values, log_sums, positions, segments):
    wide = pltpu.VMEM((ROWS, QH * HEAD), jnp.bfloat16)
    narrow = pltpu.VMEM((ROWS, HEAD), jnp.bfloat16)
    line = pltpu.VMEM((1, ROWS), jnp.int32)
    return pl.pallas_call(
        pack_kernel,
        out_shape=(
            jax.ShapeDtypeStruct((2, STACK + STATS, 2 * HEAD), jnp.bfloat16),
            jax.ShapeDtypeStruct((PLANE, ROWS + STATS, 2 * HEAD), jnp.bfloat16),
        ),
        in_specs=[pl.BlockSpec(memory_space=pl.ANY)] * 8,
        out_specs=(pl.BlockSpec(memory_space=pltpu.VMEM),) * 2,
        scratch_shapes=[
            wide,
            wide,
            wide,
            narrow,
            narrow,
            pltpu.VMEM((QH, ROWS), jnp.float32),
            line,
            line,
            pltpu.SemaphoreType.DMA((8,)),
        ],
        compiler_params=pltpu.CompilerParams(vmem_limit_bytes=8 * 1024 * 1024),
        name="pack",
    )(
        queries,
        out_grad,
        saved_out,
        keys,
        values,
        log_sums.T,
        positions.reshape(1, ROWS),
        segments.reshape(1, ROWS),
    )


def grad_kernel(*refs):
    q_refs = refs[:PIECES]
    (kv_ref, dkv_ref, own_ref, other_ref) = refs[PIECES : PIECES + 4]
    (qs, rows, dk, dv, dq, ints, ints_s, jobs, sem) = refs[PIECES + 4 :]
    scale = HEAD ** (-0.5)

    tails = [kv_ref[d, ROWS : ROWS + STATS, 0:ROWS].astype(jnp.float32) for d in range(PLANE)]
    number = jnp.concatenate([tail[0:1] for tail in tails], axis=0)
    key_seg = jnp.concatenate([tail[1:2] for tail in tails], axis=0)
    column = jnp.concatenate([number[:, 0:1], number[:, BLOCK : BLOCK + 1]], axis=0)
    column = jnp.broadcast_to(column, (KBLOCKS, ROWS))
    pad = jnp.full((ROWS - KBLOCKS, ROWS), FAR, jnp.float32)
    line = jnp.concatenate([column, pad], axis=0).T
    rank = jnp.sum((column < line[0:KBLOCKS]).astype(jnp.float32), axis=0, keepdims=True)
    slot = lax.broadcasted_iota(jnp.int32, (SLOTS, ROWS), 0).astype(jnp.float32)
    lane = lax.broadcasted_iota(jnp.int32, (SLOTS, ROWS), 1)
    order = jnp.sum(
        jnp.where((rank == slot) & (lane < KBLOCKS), lane.astype(jnp.float32), 0.0),
        axis=1,
        keepdims=True,
    )
    below = [
        jnp.sum((key_seg < float(s)).astype(jnp.float32), axis=0, keepdims=True) for s in range(1, 9)
    ]
    below = jnp.sum(jnp.concatenate(below, axis=0), axis=1, keepdims=True)
    below = jnp.broadcast_to(below, (8, STACK))
    segment = (lax.broadcasted_iota(jnp.int32, (8, STACK), 0) + 1).astype(jnp.float32)

    within = jnp.bitwise_and(lax.broadcasted_iota(jnp.int32, (1, STACK), 1), BLOCK - 1)
    within = within.astype(jnp.float32) + 1.0
    numbers, begins = [], []
    stats = []
    for qi in range(QBLOCKS):
        tail = q_refs[qi // 2][qi % 2, STACK : STACK + STATS, :].astype(jnp.float32)
        stat = tail[0:4] + tail[4:8] + tail[8:12]
        begin = jnp.max(jnp.where(stat[3:4] >= segment, below, 0.0), axis=0, keepdims=True)
        stats.append((stat, begin))
        numbers.append(stat[2:3, 0:1])
        begins.append(begin[:, 0:1])
    numbers = jnp.concatenate(numbers, axis=0)
    before = jnp.sum((line[0:QBLOCKS] < numbers).astype(jnp.float32), axis=1, keepdims=True)
    same = jnp.sum((line[0:QBLOCKS] == numbers).astype(jnp.float32), axis=1, keepdims=True)
    low = jnp.floor(jnp.concatenate(begins, axis=0) * (1.0 / BLOCK))
    empty = jnp.zeros((SLOTS - QBLOCKS, 1), jnp.float32)
    low = jnp.concatenate([low, empty], axis=0)
    high = jnp.concatenate([before + same, empty], axis=0)
    ints[...] = jnp.where(lane == 0, order, jnp.where(lane == 1, low, high)).astype(jnp.int32)
    copy = pltpu.make_async_copy(ints, ints_s, sem)
    copy.start()

    for qi in range(QBLOCKS):
        stat, begin = stats[qi]
        rows[qi, 0:1, :] = stat[0:1]
        rows[qi, 1:2, :] = stat[1:2]
        rows[qi, 2:3, :] = begin
        rows[qi, 3:4, :] = before[qi : qi + 1] * float(BLOCK) + same[qi : qi + 1] * within
        qs[qi] = q_refs[qi // 2][qi % 2, 0:STACK, :]
    dk[...] = jnp.zeros_like(dk)
    dv[...] = jnp.zeros_like(dv)
    dq[...] = jnp.zeros_like(dq)
    copy.wait()

    def list_block(qi, count):
        lower = ints_s[qi, 1]
        steps = jnp.right_shift(jnp.maximum(ints_s[qi, 2] - lower, 0) + (TILE_BLOCKS - 1), 2)

        def put(step, count):
            jobs[count] = qi * 64 + lower + step * TILE_BLOCKS
            return count + 1

        return lax.fori_loop(0, steps, put, count)

    count = lax.fori_loop(0, QBLOCKS, list_block, 0)
    jobs[count] = KBLOCKS
    down = lax.broadcasted_iota(jnp.int32, (TILE, ROWS), 0).astype(jnp.float32)
    nt = (((1,), (1,)), ((), ()))
    tn = (((0,), (0,)), ((), ()))

    def products(job):
        qi = jnp.right_shift(job, 6)
        at = jnp.bitwise_and(job, 63)
        blocks = [ints_s[at + i, 0] for i in range(TILE_BLOCKS)]
        kv = jnp.concatenate(
            [
                kv_ref[
                    jnp.bitwise_and(j, PLANE - 1),
                    pl.ds(pl.multiple_of(jnp.right_shift(j, 4) * BLOCK, BLOCK), BLOCK),
                    :,
                ]
                for j in blocks
            ],
            axis=0,
        )
        k, v = kv[:, 0:HEAD], kv[:, HEAD : 2 * HEAD]
        q, g = qs[qi, :, 0:HEAD], qs[qi, :, HEAD : 2 * HEAD]
        s = lax.dot_general(k, q, nt, preferred_element_type=jnp.float32)
        gp = lax.dot_general(v, g, nt, preferred_element_type=jnp.float32)
        offset = (at * BLOCK).astype(jnp.float32)
        begin = rows[qi, 2:3, 0:ROWS] - offset
        end = rows[qi, 3:4, 0:ROWS] - offset
        seen = (down >= begin) & (down < end)
        seen = jnp.concatenate([seen, seen], axis=1)
        w = jnp.where(seen, jnp.exp2(s * (scale * LOG2E) - rows[qi, 0:1, :]), 0.0)
        ds = (w * (gp - rows[qi, 1:2, :]) * scale).astype(jnp.bfloat16)
        dv_part = jnp.dot(w.astype(jnp.bfloat16), g, preferred_element_type=jnp.float32)
        dk_part = jnp.dot(ds, q, preferred_element_type=jnp.float32)
        dq_part = lax.dot_general(ds, k, tn, preferred_element_type=jnp.float32)
        return qi, blocks, dq_part, dk_part, dv_part

    def jobs_step(step, carry):
        done = [products(jobs[step * TOGETHER + i]) for i in range(TOGETHER)]
        for qi, blocks, dq_part, dk_part, dv_part in done:
            dq[qi] += dq_part
            for i, j in enumerate(blocks):
                part = slice(i * BLOCK, (i + 1) * BLOCK)
                dk[j] += dk_part[part]
                dv[j] += dv_part[part]
        return carry

    lax.fori_loop(0, jnp.right_shift(count + TOGETHER - 1, 1), jobs_step, 0)

    for j in range(KBLOCKS):
        d, to = j % PLANE, slice((j // PLANE) * BLOCK, (j // PLANE + 1) * BLOCK)
        dkv_ref[d, to, 0:HEAD] = dk[j].astype(jnp.bfloat16)
        dkv_ref[d, to, HEAD : 2 * HEAD] = dv[j].astype(jnp.bfloat16)
    for qi in range(QBLOCKS // 2):
        own_ref[qi] = dq[qi]
        other_ref[qi] = dq[QBLOCKS // 2 + qi].astype(jnp.bfloat16)


def grads(pieces, kv):
    half = QBLOCKS // 2
    return pl.pallas_call(
        grad_kernel,
        out_shape=(
            jax.ShapeDtypeStruct((PLANE, ROWS, 2 * HEAD), jnp.bfloat16),
            jax.ShapeDtypeStruct((half, STACK, HEAD), jnp.float32),
            jax.ShapeDtypeStruct((half, STACK, HEAD), jnp.bfloat16),
        ),
        in_specs=[pl.BlockSpec(memory_space=pltpu.VMEM)] * (PIECES + 1),
        out_specs=(pl.BlockSpec(memory_space=pltpu.VMEM),) * 3,
        scratch_shapes=[
            pltpu.VMEM((QBLOCKS, STACK, 2 * HEAD), jnp.bfloat16),
            pltpu.VMEM((QBLOCKS, 8, STACK), jnp.float32),
            pltpu.VMEM((KBLOCKS, BLOCK, HEAD), jnp.float32),
            pltpu.VMEM((KBLOCKS, BLOCK, HEAD), jnp.float32),
            pltpu.VMEM((QBLOCKS, STACK, HEAD), jnp.float32),
            pltpu.VMEM((SLOTS, ROWS), jnp.int32),
            pltpu.SMEM((SLOTS, ROWS), jnp.int32),
            pltpu.SMEM((QBLOCKS * KBLOCKS // TILE_BLOCKS + 8,), jnp.int32),
            pltpu.SemaphoreType.DMA,
        ],
        compiler_params=pltpu.CompilerParams(vmem_limit_bytes=16 * 1024 * 1024),
        name="grads",
    )(*pieces, kv)


def unstack(array):
    return array.reshape(2, QH, BLOCK, HEAD).transpose(0, 2, 1, 3).reshape(ROWS, QH * HEAD)


def body(queries, keys, values, saved_out, out_grad, log_sums, positions, segments):
    qmsg, kvmsg = pack(queries, out_grad, saved_out, keys, values, log_sums, positions, segments)
    column = [qmsg] + [along_z(qmsg, shift) for shift in (1, 2, 3)]
    kv = over_plane(kvmsg)
    column = column + [to_partner(piece) for piece in column]
    dkv, own, other = grads(column, kv)
    total = (own + to_partner(other).astype(jnp.float32)).reshape(DEPTH, 2, STACK, HEAD)
    back = [along_z(total[shift].astype(jnp.bfloat16), -shift) for shift in (1, 2, 3)]
    parts = over_plane(dkv)
    grad_kv = jnp.sum(parts.astype(jnp.float32), axis=0)
    grad_queries = total[0]
    for part in back:
        grad_queries = grad_queries + part.astype(jnp.float32)
    return (unstack(grad_queries), grad_kv[:, :HEAD], grad_kv[:, HEAD:])


def solution(mesh):
    rows2, rows1 = P(AXES, None), P(AXES)
    return jax.shard_map(
        body,
        mesh=mesh,
        in_specs=(rows2,) * 6 + (rows1,) * 2,
        out_specs=(rows2,) * 3,
        check_vma=False,
    )
```

profile of v0, /device:TPU:0, one launch (start us, length us, event | category | flops | bytes accessed | tf_op | source)
XLA Modules:
  0.0 80.2 jit_solution(15732274727586796515)
XLA Ops:
  0.6 0.0 copy-start.8
  0.6 0.9 %copy-done.8 = bf16[128,512]{1,0:T(8,128)(2,1)S(1)} copy-done((bf16[128,512]{1,0:T(8,128)(2,1)S(1)}, bf16[128,512]{1,0:T(8,128)(2,1)}, u32[]{:S(2)}) %copy-start.8) | copy-done | bytes 131096
  1.5 0.0 copy-start.9
  1.5 0.9 %copy-done.9 = bf16[128,512]{1,0:T(8,128)(2,1)S(1)} copy-done((bf16[128,512]{1,0:T(8,128)(2,1)S(1)}, bf16[128,512]{1,0:T(8,128)(2,1)}, u32[]{:S(2)}) %copy-start.9) | copy-done | bytes 131096
  2.4 0.0 copy-start.10
  2.4 0.9 %copy-done.10 = bf16[128,512]{1,0:T(8,128)(2,1)S(1)} copy-done((bf16[128,512]{1,0:T(8,128)(2,1)S(1)}, bf16[128,512]{1,0:T(8,128)(2,1)}, u32[]{:S(2)}) %copy-start.10) | copy-done | bytes 131096
  3.3 0.0 copy-start.11
  3.4 0.8 copy-done.11
  4.1 0.0 copy-start.12
  4.1 0.8 copy-done.12
  4.9 0.0 copy-start.13
  4.9 0.7 copy-done.13
  5.5 0.0 copy-start.14
  5.5 0.7 copy-done.14
  6.2 0.0 copy-start.15
  6.2 0.7 copy-done.15
  6.9 2.0 %pack.1 = (bf16[2,272,256]{2,1,0:T(8,128)(2,1)S(1)}, bf16[16,144,256]{2,1,0:T(8,128)(2,1)}) custom-call(bf16[128,512]{1,0:T(8,128)(2,1)S(1)} %copy-done.8, bf16[128,512]{1,0:T(8,128)(2,1)S(1)} %copy-done.9, bf16[128,512]{1,0:T(8,128)(2,1)S(1)} %copy-done.10, bf16[128,128]{1,0:T(8,128)(2,1)S(1)} %copy-done.11, bf16[128,128]{1,0:T(8,128)(2,1)S(1)} %copy-done.12, ...), custom_call_target="tpu_custom_call" | custom-call | tf_op jit(solution)/shard_map/pack/pallas_call | solution.py:120
  8.9 7.1 %all-to-all-start = ((bf16[16,144,256]{2,1,0:T(8,128)(2,1)}), bf16[16,144,256]{2,1,0:T(8,128)(2,1)S(1)}, u32[]{:S(2)}, u32[]{:S(2)}) async-start(bf16[16,144,256]{2,1,0:T(8,128)(2,1)} %get-tuple-element.9), calls=%async_computation | async-start | bytes 2359296 | tf_op jit(solution)/shard_map/all_to_all | solution.py:57
  16.0 4.1 %collective-permute-start.2 = (bf16[2,272,256]{2,1,0:T(8,128)(2,1)S(1)}, bf16[2,272,256]{2,1,0:T(8,128)(2,1)S(1)}, u32[]{:S(2)}, u32[]{:S(2)}) collective-permute-start(bf16[2,272,256]{2,1,0:T(8,128)(2,1)S(1)} %get-tuple-element.8.refs_0_), channel_id=1, source_target_pairs={{0,80},{1,81},{2,82},{3,83},{4,84},{5,85},{6,86},{7,87},{8,88},{9,... | collective-permute-start | bytes 835592 | tf_op jit(solution)/shard_map/ppermute | solution.py:44
  20.1 0.0 collective-permute-start.1
  20.1 1.3 %collective-permute-start = (bf16[2,272,256]{2,1,0:T(8,128)(2,1)S(1)}, bf16[2,272,256]{2,1,0:T(8,128)(2,1)S(1)}, u32[]{:S(2)}, u32[]{:S(2)}) collective-permute-start(bf16[2,272,256]{2,1,0:T(8,128)(2,1)S(1)} %get-tuple-element.8.refs_0_), channel_id=1, source_target_pairs={{0,64},{1,65},{2,66},{3,67},{4,68},{5,69},{6,70},{7,71},{8,72},{9,... | collective-permute-start | bytes 835592 | tf_op jit(solution)/shard_map/ppermute | solution.py:44
  21.4 0.0 collective-permute-start.3
  21.4 10.3 %collective-permute-done.2.refs_3_ = bf16[2,272,256]{2,1,0:T(8,128)(2,1)S(1)} collective-permute-done((bf16[2,272,256]{2,1,0:T(8,128)(2,1)S(1)}, bf16[2,272,256]{2,1,0:T(8,128)(2,1)S(1)}, u32[]{:S(2)}, u32[]{:S(2)}) %collective-permute-start.2) | collective-permute-done | bytes 278560 | tf_op jit(solution)/shard_map/ppermute | solution.py:44
  31.7 0.0 collective-permute-start.6
  31.7 0.0 collective-permute-done.1.refs_2_
  31.7 0.5 collective-permute-start.5
  32.2 2.9 %collective-permute-done.refs_1_ = bf16[2,272,256]{2,1,0:T(8,128)(2,1)S(1)} collective-permute-done((bf16[2,272,256]{2,1,0:T(8,128)(2,1)S(1)}, bf16[2,272,256]{2,1,0:T(8,128)(2,1)S(1)}, u32[]{:S(2)}, u32[]{:S(2)}) %collective-permute-start) | collective-permute-done | bytes 278560 | tf_op jit(solution)/shard_map/ppermute | solution.py:44
  35.1 0.0 collective-permute-start.4
  35.1 0.0 collective-permute-done.3.refs_4_
  35.1 0.0 copy-start
  35.1 0.7 copy-done
  35.8 0.0 collective-permute-done.6.refs_7_
  35.8 0.7 copy-done.2
  36.5 0.0 collective-permute-done.5.refs_6_
  36.6 0.0 copy-start.4
  36.6 0.7 copy-done.4
  37.2 0.0 collective-permute-done.4.refs_5_
  37.3 0.0 copy-start.6
  37.3 0.7 copy-done.6
  38.0 0.0 all-to-all-done.refs_8_
  38.0 0.0 copy-start.1
  38.0 1.0 %copy-done.1 = bf16[2,272,256]{2,1,0:T(8,128)(2,1)S(1)} copy-done((bf16[2,272,256]{2,1,0:T(8,128)(2,1)S(1)}, bf16[2,272,256]{2,1,0:T(8,128)(2,1)}, u32[]{:S(2)}) %copy-start.1) | copy-done | bytes 278552
  38.9 0.0 copy-start.3
  38.9 1.0 %copy-done.3 = bf16[2,272,256]{2,1,0:T(8,128)(2,1)S(1)} copy-done((bf16[2,272,256]{2,1,0:T(8,128)(2,1)S(1)}, bf16[2,272,256]{2,1,0:T(8,128)(2,1)}, u32[]{:S(2)}) %copy-start.3) | copy-done | bytes 278552
  39.9 0.0 copy-start.5
  39.9 1.0 %copy-done.5 = bf16[2,272,256]{2,1,0:T(8,128)(2,1)S(1)} copy-done((bf16[2,272,256]{2,1,0:T(8,128)(2,1)S(1)}, bf16[2,272,256]{2,1,0:T(8,128)(2,1)}, u32[]{:S(2)}) %copy-start.5) | copy-done | bytes 278552
  40.9 1.0 %copy-done.7 = bf16[2,272,256]{2,1,0:T(8,128)(2,1)S(1)} copy-done((bf16[2,272,256]{2,1,0:T(8,128)(2,1)S(1)}, bf16[2,272,256]{2,1,0:T(8,128)(2,1)}, u32[]{:S(2)}) %copy-start.7) | copy-done | bytes 278552
  41.8 12.7 %grads.1 = (bf16[16,128,256]{2,1,0:T(8,128)(2,1)}, f32[8,256,128]{2,1,0:T(8,128)S(1)}, bf16[8,256,128]{2,1,0:T(8,128)(2,1)}) custom-call(bf16[2,272,256]{2,1,0:T(8,128)(2,1)S(1)} %get-tuple-element.8.refs_0_, bf16[2,272,256]{2,1,0:T(8,128)(2,1)S(1)} %collective-permute-done.refs_1_, bf16[2,272,256]{2,1,0:T(8,128)(2,1)S(1)} %collective-permute-done.1.refs_2_, ...), custom_call_target="tpu_custom_call" | custom-call | tf_op jit(solution)/shard_map/grads/pallas_call | solution.py:285
  54.5 0.1 collective-permute-start.7
  54.6 6.3 %all-to-all-start.1 = ((bf16[16,128,256]{2,1,0:T(8,128)(2,1)}), bf16[16,128,256]{2,1,0:T(8,128)(2,1)S(1)}, u32[]{:S(2)}, u32[]{:S(2)}) async-start(bf16[16,128,256]{2,1,0:T(8,128)(2,1)} %get-tuple-element.12), calls=%async_computation.1 | async-start | bytes 2097152 | tf_op jit(solution)/shard_map/all_to_all | solution.py:57
  60.9 0.0 collective-permute-done.7
  60.9 0.2 fusion.2
  61.1 0.1 collective-permute-start.8
  61.3 1.9 %collective-permute-start.10 = (bf16[2,256,128]{2,1,0:T(8,128)(2,1)S(1)}, bf16[2,256,128]{2,1,0:T(8,128)(2,1)S(1)}, u32[]{:S(2)}, u32[]{:S(2)}) collective-permute-start(bf16[2,256,128]{2,1,0:T(8,128)(2,1)S(1)} %get-tuple-element.16), channel_id=1, source_target_pairs={{0,64},{1,65},{2,66},{3,67},{4,68},{5,69},{6,70},{7,71},{8,72},{9,... | collective-permute-start | bytes 393224 | tf_op jit(solution)/shard_map/ppermute | solution.py:44
  63.2 0.8 %collective-permute-start.9 = (bf16[2,256,128]{2,1,0:T(8,128)(2,1)S(1)}, bf16[2,256,128]{2,1,0:T(8,128)(2,1)S(1)}, u32[]{:S(2)}, u32[]{:S(2)}) collective-permute-start(bf16[2,256,128]{2,1,0:T(8,128)(2,1)S(1)} %get-tuple-element.17), channel_id=1, source_target_pairs={{0,16},{1,17},{2,18},{3,19},{4,20},{5,21},{6,22},{7,23},{8,24},{9,... | collective-permute-start | bytes 393224 | tf_op jit(solution)/shard_map/ppermute | solution.py:44
  64.1 3.5 %collective-permute-done.8 = bf16[2,256,128]{2,1,0:T(8,128)(2,1)S(1)} collective-permute-done((bf16[2,256,128]{2,1,0:T(8,128)(2,1)S(1)}, bf16[2,256,128]{2,1,0:T(8,128)(2,1)S(1)}, u32[]{:S(2)}, u32[]{:S(2)}) %collective-permute-start.8) | collective-permute-done | bytes 131104 | tf_op jit(solution)/shard_map/ppermute | solution.py:44
  67.5 3.4 %collective-permute-done.10 = bf16[2,256,128]{2,1,0:T(8,128)(2,1)S(1)} collective-permute-done((bf16[2,256,128]{2,1,0:T(8,128)(2,1)S(1)}, bf16[2,256,128]{2,1,0:T(8,128)(2,1)S(1)}, u32[]{:S(2)}, u32[]{:S(2)}) %collective-permute-start.10) | collective-permute-done | bytes 131104 | tf_op jit(solution)/shard_map/ppermute | solution.py:44
  70.9 0.0 collective-permute-done.9
  70.9 0.1 fusion.1
  71.0 0.2 copy.11
  71.2 0.7 copy.14
  71.9 7.5 %all-to-all-done.1 = bf16[16,128,256]{2,1,0:T(8,128)(2,1)S(1)} async-done(((bf16[16,128,256]{2,1,0:T(8,128)(2,1)}), bf16[16,128,256]{2,1,0:T(8,128)(2,1)S(1)}, u32[]{:S(2)}, u32[]{:S(2)}) %all-to-all-start.1) | async-done | bytes 1048608 | tf_op jit(solution)/shard_map/all_to_all | solution.py:57
  79.4 0.1 convert_reduce_fusion
  79.5 0.7 fusion.4
  (3 shorter events, 0.0 us)
Async XLA Ops:
  0.6 0.9 %copy-start.8 = (bf16[128,512]{1,0:T(8,128)(2,1)S(1)}, bf16[128,512]{1,0:T(8,128)(2,1)}, u32[]{:S(2)}) copy-start(bf16[128,512]{1,0:T(8,128)(2,1)} %q_hbm.1) | copy-start | bytes 393220
  1.5 0.9 %copy-start.9 = (bf16[128,512]{1,0:T(8,128)(2,1)S(1)}, bf16[128,512]{1,0:T(8,128)(2,1)}, u32[]{:S(2)}) copy-start(bf16[128,512]{1,0:T(8,128)(2,1)} %g_hbm.1) | copy-start | bytes 393220
  2.4 0.9 %copy-start.10 = (bf16[128,512]{1,0:T(8,128)(2,1)S(1)}, bf16[128,512]{1,0:T(8,128)(2,1)}, u32[]{:S(2)}) copy-start(bf16[128,512]{1,0:T(8,128)(2,1)} %o_hbm.1) | copy-start | bytes 393220
  3.3 0.8 copy-start.11
  4.1 0.8 copy-start.12
  4.9 0.7 copy-start.13
  5.5 0.7 copy-start.14
  6.2 0.7 copy-start.15
  8.9 29.1 %all-to-all-start = ((bf16[16,144,256]{2,1,0:T(8,128)(2,1)}), bf16[16,144,256]{2,1,0:T(8,128)(2,1)S(1)}, u32[]{:S(2)}, u32[]{:S(2)}) async-start(bf16[16,144,256]{2,1,0:T(8,128)(2,1)} %get-tuple-element.9), calls=%async_computation | async-start | bytes 2359296 | tf_op jit(solution)/shard_map/all_to_all | solution.py:57
  16.0 15.7 %collective-permute-start.2 = (bf16[2,272,256]{2,1,0:T(8,128)(2,1)S(1)}, bf16[2,272,256]{2,1,0:T(8,128)(2,1)S(1)}, u32[]{:S(2)}, u32[]{:S(2)}) collective-permute-start(bf16[2,272,256]{2,1,0:T(8,128)(2,1)S(1)} %get-tuple-element.8.refs_0_), channel_id=1, source_target_pairs={{0,80},{1,81},{2,82},{3,83},{4,84},{5,85},{6,86},{7,87},{8,88},{9,... | collective-permute-start | bytes 835592 | tf_op jit(solution)/shard_map/ppermute | solution.py:44
  20.1 11.6 %collective-permute-start.1 = (bf16[2,272,256]{2,1,0:T(8,128)(2,1)S(1)}, bf16[2,272,256]{2,1,0:T(8,128)(2,1)S(1)}, u32[]{:S(2)}, u32[]{:S(2)}) collective-permute-start(bf16[2,272,256]{2,1,0:T(8,128)(2,1)S(1)} %get-tuple-element.8.refs_0_), channel_id=1, source_target_pairs={{0,16},{1,17},{2,18},{3,19},{4,20},{5,21},{6,22},{7,23},{8,24},{9,... | collective-permute-start | bytes 835592 | tf_op jit(solution)/shard_map/ppermute | solution.py:44
  20.1 15.0 %collective-permute-start = (bf16[2,272,256]{2,1,0:T(8,128)(2,1)S(1)}, bf16[2,272,256]{2,1,0:T(8,128)(2,1)S(1)}, u32[]{:S(2)}, u32[]{:S(2)}) collective-permute-start(bf16[2,272,256]{2,1,0:T(8,128)(2,1)S(1)} %get-tuple-element.8.refs_0_), channel_id=1, source_target_pairs={{0,64},{1,65},{2,66},{3,67},{4,68},{5,69},{6,70},{7,71},{8,72},{9,... | collective-permute-start | bytes 835592 | tf_op jit(solution)/shard_map/ppermute | solution.py:44
  21.4 13.8 %collective-permute-start.3 = (bf16[2,272,256]{2,1,0:T(8,128)(2,1)S(1)}, bf16[2,272,256]{2,1,0:T(8,128)(2,1)S(1)}, u32[]{:S(2)}, u32[]{:S(2)}) collective-permute-start(bf16[2,272,256]{2,1,0:T(8,128)(2,1)S(1)} %get-tuple-element.8.refs_0_), channel_id=1, source_target_pairs={{0,32},{1,33},{2,34},{3,35},{4,36},{5,37},{6,38},{7,39},{8,40},{9,... | collective-permute-start | bytes 835592 | tf_op jit(solution)/shard_map/ppermute | solution.py:52
  31.7 4.1 %collective-permute-start.6 = (bf16[2,272,256]{2,1,0:T(8,128)(2,1)S(1)}, bf16[2,272,256]{2,1,0:T(8,128)(2,1)S(1)}, u32[]{:S(2)}, u32[]{:S(2)}) collective-permute-start(bf16[2,272,256]{2,1,0:T(8,128)(2,1)S(1)} %collective-permute-done.2.refs_3_), channel_id=1, source_target_pairs={{0,32},{1,33},{2,34},{3,35},{4,36},{5,37},{6,38},{7,39},{8,40},{9,... | collective-permute-start | bytes 835592 | tf_op jit(solution)/shard_map/ppermute | solution.py:52
  31.7 4.8 %collective-permute-start.5 = (bf16[2,272,256]{2,1,0:T(8,128)(2,1)S(1)}, bf16[2,272,256]{2,1,0:T(8,128)(2,1)S(1)}, u32[]{:S(2)}, u32[]{:S(2)}) collective-permute-start(bf16[2,272,256]{2,1,0:T(8,128)(2,1)S(1)} %collective-permute-done.1.refs_2_), channel_id=1, source_target_pairs={{0,32},{1,33},{2,34},{3,35},{4,36},{5,37},{6,38},{7,39},{8,40},{9,... | collective-permute-start | bytes 835592 | tf_op jit(solution)/shard_map/ppermute | solution.py:52
  35.1 2.1 %collective-permute-start.4 = (bf16[2,272,256]{2,1,0:T(8,128)(2,1)S(1)}, bf16[2,272,256]{2,1,0:T(8,128)(2,1)S(1)}, u32[]{:S(2)}, u32[]{:S(2)}) collective-permute-start(bf16[2,272,256]{2,1,0:T(8,128)(2,1)S(1)} %collective-permute-done.refs_1_), channel_id=1, source_target_pairs={{0,32},{1,33},{2,34},{3,35},{4,36},{5,37},{6,38},{7,39},{8,40},{9,... | collective-permute-start | bytes 835592 | tf_op jit(solution)/shard_map/ppermute | solution.py:52
  35.1 0.7 copy-start
  35.8 0.7 copy-start.2
  36.6 0.7 copy-start.4
  37.3 0.7 copy-start.6
  38.0 1.0 %copy-start.1 = (bf16[2,272,256]{2,1,0:T(8,128)(2,1)S(1)}, bf16[2,272,256]{2,1,0:T(8,128)(2,1)}, u32[]{:S(2)}) copy-start(bf16[2,272,256]{2,1,0:T(8,128)(2,1)} %copy-done) | copy-start | bytes 835588
  38.9 1.0 %copy-start.3 = (bf16[2,272,256]{2,1,0:T(8,128)(2,1)S(1)}, bf16[2,272,256]{2,1,0:T(8,128)(2,1)}, u32[]{:S(2)}) copy-start(bf16[2,272,256]{2,1,0:T(8,128)(2,1)} %copy-done.2) | copy-start | bytes 835588
  39.9 1.0 %copy-start.5 = (bf16[2,272,256]{2,1,0:T(8,128)(2,1)S(1)}, bf16[2,272,256]{2,1,0:T(8,128)(2,1)}, u32[]{:S(2)}) copy-start(bf16[2,272,256]{2,1,0:T(8,128)(2,1)} %copy-done.4) | copy-start | bytes 835588
  40.8 1.0 %copy-start.7 = (bf16[2,272,256]{2,1,0:T(8,128)(2,1)S(1)}, bf16[2,272,256]{2,1,0:T(8,128)(2,1)}, u32[]{:S(2)}) copy-start(bf16[2,272,256]{2,1,0:T(8,128)(2,1)} %copy-done.6) | copy-start | bytes 835588
  54.5 6.4 %collective-permute-start.7 = (bf16[8,256,128]{2,1,0:T(8,128)(2,1)}, bf16[8,256,128]{2,1,0:T(8,128)(2,1)S(1)}, u32[]{:S(2)}, u32[]{:S(2)}) collective-permute-start(bf16[8,256,128]{2,1,0:T(8,128)(2,1)} %get-tuple-element.11), channel_id=1, source_target_pairs={{0,32},{1,33},{2,34},{3,35},{4,36},{5,37},{6,38},{7,39},{8,40},{9,... | collective-permute-start | bytes 1572872 | tf_op jit(solution)/shard_map/ppermute | solution.py:52
  54.6 24.7 %all-to-all-start.1 = ((bf16[16,128,256]{2,1,0:T(8,128)(2,1)}), bf16[16,128,256]{2,1,0:T(8,128)(2,1)S(1)}, u32[]{:S(2)}, u32[]{:S(2)}) async-start(bf16[16,128,256]{2,1,0:T(8,128)(2,1)} %get-tuple-element.12), calls=%async_computation.1 | async-start | bytes 2097152 | tf_op jit(solution)/shard_map/all_to_all | solution.py:57
  61.1 6.4 %collective-permute-start.8 = (bf16[2,256,128]{2,1,0:T(8,128)(2,1)S(1)}, bf16[2,256,128]{2,1,0:T(8,128)(2,1)S(1)}, u32[]{:S(2)}, u32[]{:S(2)}) collective-permute-start(bf16[2,256,128]{2,1,0:T(8,128)(2,1)S(1)} %get-tuple-element.15), channel_id=1, source_target_pairs={{0,80},{1,81},{2,82},{3,83},{4,84},{5,85},{6,86},{7,87},{8,88},{9,... | collective-permute-start | bytes 393224 | tf_op jit(solution)/shard_map/ppermute | solution.py:44
  61.3 9.6 %collective-permute-start.10 = (bf16[2,256,128]{2,1,0:T(8,128)(2,1)S(1)}, bf16[2,256,128]{2,1,0:T(8,128)(2,1)S(1)}, u32[]{:S(2)}, u32[]{:S(2)}) collective-permute-start(bf16[2,256,128]{2,1,0:T(8,128)(2,1)S(1)} %get-tuple-element.16), channel_id=1, source_target_pairs={{0,64},{1,65},{2,66},{3,67},{4,68},{5,69},{6,70},{7,71},{8,72},{9,... | collective-permute-start | bytes 393224 | tf_op jit(solution)/shard_map/ppermute | solution.py:44
  63.2 7.7 %collective-permute-start.9 = (bf16[2,256,128]{2,1,0:T(8,128)(2,1)S(1)}, bf16[2,256,128]{2,1,0:T(8,128)(2,1)S(1)}, u32[]{:S(2)}, u32[]{:S(2)}) collective-permute-start(bf16[2,256,128]{2,1,0:T(8,128)(2,1)S(1)} %get-tuple-element.17), channel_id=1, source_target_pairs={{0,16},{1,17},{2,18},{3,19},{4,20},{5,21},{6,22},{7,23},{8,24},{9,... | collective-permute-start | bytes 393224 | tf_op jit(solution)/shard_map/ppermute | solution.py:44
where the time goes:
time: 81.5 us; the launch traced here: 80.2 us
  waiting for transfers between devices  27.6 us (34%)
  starting transfers between devices  22.3 us (27%)
  Pallas kernels  14.7 us (18%)
  local copies, waits for them, and re-layouts  14.4 us (18%)
    ppermute x6, waiting for transfers between devices, along_z(): return lax.ppermute(array, AXES, pairs)  20.1 us
    unnamed x33, local copies, waits for them, and re-layouts  13.6 us
    all_to_all x2, starting transfers between devices, over_plane(): lax.all_to_all(array, 'inner', 0, 0, axis_index_groups=groups, tiled=True)  13.4 us
    pallas_call x1, Pallas kernels, grads(): pl.pallas_call(grad_kernel, out_shape=(jax.ShapeDtypeStruct((PLANE, ROWS,...  12.7 us
    ppermute x6, starting transfers between devices, along_z(): return lax.ppermute(array, AXES, pairs)  8.3 us
    all_to_all x2, waiting for transfers between devices, over_plane(): lax.all_to_all(array, 'inner', 0, 0, axis_index_groups=groups, tiled=True)  7.49 us
    pallas_call x1, Pallas kernels, pack(): pl.pallas_call(pack_kernel, out_shape=(jax.ShapeDtypeStruct((2, STACK + S...  1.99 us
  transfers between devices with their start and end apart: 13, of which 5 were waited for; matrix products, arithmetic and copies ran while one was open for 1% of the time, Pallas kernels for 0%

commit v1 on v0

--- a/solution.py
+++ b/solution.py
@@ -21,7 +21,7 @@
 TILE = 256
 TILE_BLOCKS = TILE // BLOCK
 SLOTS = 40
-TOGETHER = 2
+TOGETHER = 4
 FAR = 1.0e9
 AXES = ("outer", "inner")
 LOG2E = math.log2(math.e)
@@ -123,7 +123,7 @@
             jax.ShapeDtypeStruct((2, STACK + STATS, 2 * HEAD), jnp.bfloat16),
             jax.ShapeDtypeStruct((PLANE, ROWS + STATS, 2 * HEAD), jnp.bfloat16),
         ),
-        in_specs=[pl.BlockSpec(memory_space=pl.ANY)] * 8,
+        in_specs=[pl.BlockSpec(memory_space=pltpu.HBM)] * 8,
         out_specs=(pl.BlockSpec(memory_space=pltpu.VMEM),) * 2,
         scratch_shapes=[
             wide,
@@ -153,7 +153,15 @@
 def grad_kernel(*refs):
     q_refs = refs[:PIECES]
     (kv_ref, dkv_ref, own_ref, other_ref) = refs[PIECES : PIECES + 4]
-    (qs, rows, dk, dv, dq, ints, ints_s, jobs, sem) = refs[PIECES + 4 :]
+    (qs, rows, dk, dv, dq, ints, ints_s, jobs, sem, q_sems) = refs[PIECES + 4 :]
+    q_copies = [
+        pltpu.make_async_copy(q_refs[p], qs.at[pl.ds(2 * p, 2)], q_sems.at[p]) for p in range(PIECES)
+    ]
+    for copy in q_copies:
+        copy.start()
+    dk[...] = jnp.zeros_like(dk)
+    dv[...] = jnp.zeros_like(dv)
+    dq[...] = jnp.zeros_like(dq)
     scale = HEAD ** (-0.5)
 
     tails = [kv_ref[d, ROWS : ROWS + STATS, 0:ROWS].astype(jnp.float32) for d in range(PLANE)]
@@ -183,7 +191,9 @@
     numbers, begins = [], []
     stats = []
     for qi in range(QBLOCKS):
-        tail = q_refs[qi // 2][qi % 2, STACK : STACK + STATS, :].astype(jnp.float32)
+        if qi % 2 == 0:
+            q_copies[qi // 2].wait()
+        tail = qs[qi, STACK : STACK + STATS, :].astype(jnp.float32)
         stat = tail[0:4] + tail[4:8] + tail[8:12]
         begin = jnp.max(jnp.where(stat[3:4] >= segment, below, 0.0), axis=0, keepdims=True)
         stats.append((stat, begin))
@@ -206,10 +216,6 @@
         rows[qi, 1:2, :] = stat[1:2]
         rows[qi, 2:3, :] = begin
         rows[qi, 3:4, :] = before[qi : qi + 1] * float(BLOCK) + same[qi : qi + 1] * within
-        qs[qi] = q_refs[qi // 2][qi % 2, 0:STACK, :]
-    dk[...] = jnp.zeros_like(dk)
-    dv[...] = jnp.zeros_like(dv)
-    dq[...] = jnp.zeros_like(dq)
     copy.wait()
 
     def list_block(qi, count):
@@ -223,7 +229,8 @@
         return lax.fori_loop(0, steps, put, count)
 
     count = lax.fori_loop(0, QBLOCKS, list_block, 0)
-    jobs[count] = KBLOCKS
+    for i in range(TOGETHER - 1):
+        jobs[count + i] = KBLOCKS
     down = lax.broadcasted_iota(jnp.int32, (TILE, ROWS), 0).astype(jnp.float32)
     nt = (((1,), (1,)), ((), ()))
     tn = (((0,), (0,)), ((), ()))
@@ -244,7 +251,7 @@
             axis=0,
         )
         k, v = kv[:, 0:HEAD], kv[:, HEAD : 2 * HEAD]
-        q, g = qs[qi, :, 0:HEAD], qs[qi, :, HEAD : 2 * HEAD]
+        q, g = qs[qi, 0:STACK, 0:HEAD], qs[qi, 0:STACK, HEAD : 2 * HEAD]
         s = lax.dot_general(k, q, nt, preferred_element_type=jnp.float32)
         gp = lax.dot_general(v, g, nt, preferred_element_type=jnp.float32)
         offset = (at * BLOCK).astype(jnp.float32)
@@ -256,7 +263,7 @@
         ds = (w * (gp - rows[qi, 1:2, :]) * scale).astype(jnp.bfloat16)
         dv_part = jnp.dot(w.astype(jnp.bfloat16), g, preferred_element_type=jnp.float32)
         dk_part = jnp.dot(ds, q, preferred_element_type=jnp.float32)
-        dq_part = lax.dot_general(ds, k, tn, preferred_element_type=jnp.float32)
+        dq_part = lax.dot_general(k, ds, tn, preferred_element_type=jnp.float32)
         return qi, blocks, dq_part, dk_part, dv_part
 
     def jobs_step(step, carry):
@@ -269,15 +276,15 @@
                 dv[j] += dv_part[part]
         return carry
 
-    lax.fori_loop(0, jnp.right_shift(count + TOGETHER - 1, 1), jobs_step, 0)
+    lax.fori_loop(0, jnp.right_shift(count + TOGETHER - 1, 2), jobs_step, 0)
 
     for j in range(KBLOCKS):
         d, to = j % PLANE, slice((j // PLANE) * BLOCK, (j // PLANE + 1) * BLOCK)
         dkv_ref[d, to, 0:HEAD] = dk[j].astype(jnp.bfloat16)
         dkv_ref[d, to, HEAD : 2 * HEAD] = dv[j].astype(jnp.bfloat16)
     for qi in range(QBLOCKS // 2):
-        own_ref[qi] = dq[qi]
-        other_ref[qi] = dq[QBLOCKS // 2 + qi].astype(jnp.bfloat16)
+        own_ref[qi] = dq[qi].T
+        other_ref[qi] = dq[QBLOCKS // 2 + qi].T.astype(jnp.bfloat16)
 
 
 def grads(pieces, kv):
@@ -289,18 +296,20 @@
             jax.ShapeDtypeStruct((half, STACK, HEAD), jnp.float32),
             jax.ShapeDtypeStruct((half, STACK, HEAD), jnp.bfloat16),
         ),
-        in_specs=[pl.BlockSpec(memory_space=pltpu.VMEM)] * (PIECES + 1),
+        in_specs=[pl.BlockSpec(memory_space=pltpu.HBM)] * PIECES
+        + [pl.BlockSpec(memory_space=pltpu.VMEM)],
         out_specs=(pl.BlockSpec(memory_space=pltpu.VMEM),) * 3,
         scratch_shapes=[
-            pltpu.VMEM((QBLOCKS, STACK, 2 * HEAD), jnp.bfloat16),
+            pltpu.VMEM((QBLOCKS, STACK + STATS, 2 * HEAD), jnp.bfloat16),
             pltpu.VMEM((QBLOCKS, 8, STACK), jnp.float32),
             pltpu.VMEM((KBLOCKS, BLOCK, HEAD), jnp.float32),
             pltpu.VMEM((KBLOCKS, BLOCK, HEAD), jnp.float32),
-            pltpu.VMEM((QBLOCKS, STACK, HEAD), jnp.float32),
+            pltpu.VMEM((QBLOCKS, HEAD, STACK), jnp.float32),
             pltpu.VMEM((SLOTS, ROWS), jnp.int32),
             pltpu.SMEM((SLOTS, ROWS), jnp.int32),
             pltpu.SMEM((QBLOCKS * KBLOCKS // TILE_BLOCKS + 8,), jnp.int32),
             pltpu.SemaphoreType.DMA,
+            pltpu.SemaphoreType.DMA((PIECES,)),
         ],
         compiler_params=pltpu.CompilerParams(vmem_limit_bytes=16 * 1024 * 1024),
         name="grads",

time: 81.5 us -> 81 us (level); the launches traced: 80.2 us -> 81.1 us
  starting transfers between devices: 22.3 us -> 26 us
  Pallas kernels: 14.7 us -> 11.6 us
    pallas_call x1, Pallas kernels: 12.7 us -> 9.58 us  [grads(): pl.pallas_call(grad_kernel, out_shape=(jax.ShapeDtypeStruct((PLANE, ROWS,...]
    all_to_all x2, starting transfers between devices: 13.4 us -> 16.3 us  [over_plane(): lax.all_to_all(array, 'inner', 0, 0, axis_index_groups=groups, tiled=True)]
    ppermute x5, starting transfers between devices: 0.6 us -> 2.27 us  [to_partner(): return lax.ppermute(array, AXES, pairs)]
    ppermute x6, starting transfers between devices: 8.3 us -> 7.46 us  [along_z(): return lax.ppermute(array, AXES, pairs)]
where the time goes in v1:
time: 81 us; the launch traced here: 81.1 us
  waiting for transfers between devices  28 us (35%)
  starting transfers between devices  26 us (32%)
  local copies, waits for them, and re-layouts  14.4 us (18%)
  Pallas kernels  11.6 us (14%)
    ppermute x6, waiting for transfers between devices, along_z(): return lax.ppermute(array, AXES, pairs)  20.5 us
    all_to_all x2, starting transfers between devices, over_plane(): lax.all_to_all(array, 'inner', 0, 0, axis_index_groups=groups, tiled=True)  16.3 us
    unnamed x33, local copies, waits for them, and re-layouts  13.6 us
    pallas_call x1, Pallas kernels, grads(): pl.pallas_call(grad_kernel, out_shape=(jax.ShapeDtypeStruct((PLANE, ROWS,...  9.58 us
    all_to_all x2, waiting for transfers between devices, over_plane(): lax.all_to_all(array, 'inner', 0, 0, axis_index_groups=groups, tiled=True)  7.5 us
    ppermute x6, starting transfers between devices, along_z(): return lax.ppermute(array, AXES, pairs)  7.46 us
    ppermute x5, starting transfers between devices, to_partner(): return lax.ppermute(array, AXES, pairs)  2.27 us
    pallas_call x1, Pallas kernels, pack(): pl.pallas_call(pack_kernel, out_shape=(jax.ShapeDtypeStruct((2, STACK + S...  1.99 us
  transfers between devices with their start and end apart: 13, of which 5 were waited for; matrix products, arithmetic and copies ran while one was open for 1% of the time, Pallas kernels for 0%

profile of v1, /device:TPU:0, one launch (start us, length us, event | category | flops | bytes accessed | tf_op | source)
XLA Modules:
  0.0 81.1 jit_solution(8934589139584384958)
XLA Ops:
  0.6 0.0 copy-start.8
  0.6 0.9 %copy-done.8 = bf16[128,512]{1,0:T(8,128)(2,1)S(1)} copy-done((bf16[128,512]{1,0:T(8,128)(2,1)S(1)}, bf16[128,512]{1,0:T(8,128)(2,1)}, u32[]{:S(2)}) %copy-start.8) | copy-done | bytes 131096
  1.5 0.0 copy-start.9
  1.5 0.9 %copy-done.9 = bf16[128,512]{1,0:T(8,128)(2,1)S(1)} copy-done((bf16[128,512]{1,0:T(8,128)(2,1)S(1)}, bf16[128,512]{1,0:T(8,128)(2,1)}, u32[]{:S(2)}) %copy-start.9) | copy-done | bytes 131096
  2.4 0.0 copy-start.10
  2.4 0.9 %copy-done.10 = bf16[128,512]{1,0:T(8,128)(2,1)S(1)} copy-done((bf16[128,512]{1,0:T(8,128)(2,1)S(1)}, bf16[128,512]{1,0:T(8,128)(2,1)}, u32[]{:S(2)}) %copy-start.10) | copy-done | bytes 131096
  3.3 0.0 copy-start.11
  3.4 0.8 copy-done.11
  4.1 0.0 copy-start.12
  4.1 0.8 copy-done.12
  4.9 0.0 copy-start.13
  4.9 0.7 copy-done.13
  5.5 0.0 copy-start.14
  5.5 0.7 copy-done.14
  6.2 0.0 copy-start.15
  6.2 0.7 copy-done.15
  6.9 2.0 %pack.1 = (bf16[2,272,256]{2,1,0:T(8,128)(2,1)S(1)}, bf16[16,144,256]{2,1,0:T(8,128)(2,1)}) custom-call(bf16[128,512]{1,0:T(8,128)(2,1)S(1)} %copy-done.8, bf16[128,512]{1,0:T(8,128)(2,1)S(1)} %copy-done.9, bf16[128,512]{1,0:T(8,128)(2,1)S(1)} %copy-done.10, bf16[128,128]{1,0:T(8,128)(2,1)S(1)} %copy-done.11, bf16[128,128]{1,0:T(8,128)(2,1)S(1)} %copy-done.12, ...), custom_call_target="tpu_custom_call" | custom-call | tf_op jit(solution)/shard_map/pack/pallas_call | solution.py:120
  8.9 7.1 %all-to-all-start = ((bf16[16,144,256]{2,1,0:T(8,128)(2,1)}), bf16[16,144,256]{2,1,0:T(8,128)(2,1)S(1)}, u32[]{:S(2)}, u32[]{:S(2)}) async-start(bf16[16,144,256]{2,1,0:T(8,128)(2,1)} %get-tuple-element.9), calls=%async_computation | async-start | bytes 2359296 | tf_op jit(solution)/shard_map/all_to_all | solution.py:57
  16.0 4.1 %collective-permute-start.2 = (bf16[2,272,256]{2,1,0:T(8,128)(2,1)S(1)}, bf16[2,272,256]{2,1,0:T(8,128)(2,1)S(1)}, u32[]{:S(2)}, u32[]{:S(2)}) collective-permute-start(bf16[2,272,256]{2,1,0:T(8,128)(2,1)S(1)} %get-tuple-element.8.refs_0_), channel_id=1, source_target_pairs={{0,80},{1,81},{2,82},{3,83},{4,84},{5,85},{6,86},{7,87},{8,88},{9,... | collective-permute-start | bytes 835592 | tf_op jit(solution)/shard_map/ppermute | solution.py:44
  20.1 0.0 collective-permute-start.1
  20.1 1.3 %collective-permute-start = (bf16[2,272,256]{2,1,0:T(8,128)(2,1)S(1)}, bf16[2,272,256]{2,1,0:T(8,128)(2,1)S(1)}, u32[]{:S(2)}, u32[]{:S(2)}) collective-permute-start(bf16[2,272,256]{2,1,0:T(8,128)(2,1)S(1)} %get-tuple-element.8.refs_0_), channel_id=1, source_target_pairs={{0,64},{1,65},{2,66},{3,67},{4,68},{5,69},{6,70},{7,71},{8,72},{9,... | collective-permute-start | bytes 835592 | tf_op jit(solution)/shard_map/ppermute | solution.py:44
  21.4 0.0 collective-permute-start.3
  21.4 10.3 %collective-permute-done.2.refs_3_ = bf16[2,272,256]{2,1,0:T(8,128)(2,1)S(1)} collective-permute-done((bf16[2,272,256]{2,1,0:T(8,128)(2,1)S(1)}, bf16[2,272,256]{2,1,0:T(8,128)(2,1)S(1)}, u32[]{:S(2)}, u32[]{:S(2)}) %collective-permute-start.2) | collective-permute-done | bytes 278560 | tf_op jit(solution)/shard_map/ppermute | solution.py:44
  31.7 0.0 collective-permute-start.6
  31.7 0.0 collective-permute-done.1.refs_2_
  31.7 0.5 collective-permute-start.5
  32.2 2.9 %collective-permute-done.refs_1_ = bf16[2,272,256]{2,1,0:T(8,128)(2,1)S(1)} collective-permute-done((bf16[2,272,256]{2,1,0:T(8,128)(2,1)S(1)}, bf16[2,272,256]{2,1,0:T(8,128)(2,1)S(1)}, u32[]{:S(2)}, u32[]{:S(2)}) %collective-permute-start) | collective-permute-done | bytes 278560 | tf_op jit(solution)/shard_map/ppermute | solution.py:44
  35.1 0.0 collective-permute-start.4
  35.1 0.0 collective-permute-done.3.refs_4_
  35.1 0.0 copy-start
  35.1 0.7 copy-done
  35.8 0.0 collective-permute-done.6.refs_7_
  35.8 0.0 copy-start.2
  35.8 0.7 copy-done.2
  36.5 0.0 collective-permute-done.5.refs_6_
  36.6 0.0 copy-start.4
  36.6 0.7 copy-done.4
  37.2 0.0 collective-permute-done.4.refs_5_
  37.3 0.0 copy-start.6
  37.3 0.7 copy-done.6
  38.0 0.0 all-to-all-done.refs_8_
  38.0 0.0 copy-start.1
  38.0 1.0 %copy-done.1 = bf16[2,272,256]{2,1,0:T(8,128)(2,1)S(1)} copy-done((bf16[2,272,256]{2,1,0:T(8,128)(2,1)S(1)}, bf16[2,272,256]{2,1,0:T(8,128)(2,1)}, u32[]{:S(2)}) %copy-start.1) | copy-done | bytes 278552
  38.9 0.0 copy-start.3
  38.9 1.0 %copy-done.3 = bf16[2,272,256]{2,1,0:T(8,128)(2,1)S(1)} copy-done((bf16[2,272,256]{2,1,0:T(8,128)(2,1)S(1)}, bf16[2,272,256]{2,1,0:T(8,128)(2,1)}, u32[]{:S(2)}) %copy-start.3) | copy-done | bytes 278552
  39.9 1.0 %copy-done.5 = bf16[2,272,256]{2,1,0:T(8,128)(2,1)S(1)} copy-done((bf16[2,272,256]{2,1,0:T(8,128)(2,1)S(1)}, bf16[2,272,256]{2,1,0:T(8,128)(2,1)}, u32[]{:S(2)}) %copy-start.5) | copy-done | bytes 278552
  40.9 1.0 %copy-done.7 = bf16[2,272,256]{2,1,0:T(8,128)(2,1)S(1)} copy-done((bf16[2,272,256]{2,1,0:T(8,128)(2,1)S(1)}, bf16[2,272,256]{2,1,0:T(8,128)(2,1)}, u32[]{:S(2)}) %copy-start.7) | copy-done | bytes 278552
  41.8 9.6 %grads.1 = (bf16[16,128,256]{2,1,0:T(8,128)(2,1)}, f32[8,256,128]{2,1,0:T(8,128)S(1)}, bf16[8,256,128]{2,1,0:T(8,128)(2,1)}) custom-call(bf16[2,272,256]{2,1,0:T(8,128)(2,1)S(1)} %get-tuple-element.8.refs_0_, bf16[2,272,256]{2,1,0:T(8,128)(2,1)S(1)} %collective-permute-done.refs_1_, bf16[2,272,256]{2,1,0:T(8,128)(2,1)S(1)} %collective-permute-done.1.refs_2_, ...), custom_call_target="tpu_custom_call" | custom-call | tf_op jit(solution)/shard_map/grads/pallas_call | solution.py:292
  51.4 1.8 %collective-permute-start.7 = (bf16[8,256,128]{2,1,0:T(8,128)(2,1)}, bf16[8,256,128]{2,1,0:T(8,128)(2,1)S(1)}, u32[]{:S(2)}, u32[]{:S(2)}) collective-permute-start(bf16[8,256,128]{2,1,0:T(8,128)(2,1)} %get-tuple-element.11), channel_id=1, source_target_pairs={{0,32},{1,33},{2,34},{3,35},{4,36},{5,37},{6,38},{7,39},{8,40},{9,... | collective-permute-start | bytes 1572872 | tf_op jit(solution)/shard_map/ppermute | solution.py:52
  53.1 9.1 %all-to-all-start.1 = ((bf16[16,128,256]{2,1,0:T(8,128)(2,1)}), bf16[16,128,256]{2,1,0:T(8,128)(2,1)S(1)}, u32[]{:S(2)}, u32[]{:S(2)}) async-start(bf16[16,128,256]{2,1,0:T(8,128)(2,1)} %get-tuple-element.12), calls=%async_computation.1 | async-start | bytes 2097152 | tf_op jit(solution)/shard_map/all_to_all | solution.py:57
  62.3 0.0 collective-permute-done.7
  62.3 0.2 fusion.2
  62.5 0.1 collective-permute-start.8
  62.6 2.0 %collective-permute-start.10 = (bf16[2,256,128]{2,1,0:T(8,128)(2,1)S(1)}, bf16[2,256,128]{2,1,0:T(8,128)(2,1)S(1)}, u32[]{:S(2)}, u32[]{:S(2)}) collective-permute-start(bf16[2,256,128]{2,1,0:T(8,128)(2,1)S(1)} %get-tuple-element.16), channel_id=1, source_target_pairs={{0,64},{1,65},{2,66},{3,67},{4,68},{5,69},{6,70},{7,71},{8,72},{9,... | collective-permute-start | bytes 393224 | tf_op jit(solution)/shard_map/ppermute | solution.py:44
  64.6 0.0 collective-permute-start.9
  64.6 4.1 %collective-permute-done.8 = bf16[2,256,128]{2,1,0:T(8,128)(2,1)S(1)} collective-permute-done((bf16[2,256,128]{2,1,0:T(8,128)(2,1)S(1)}, bf16[2,256,128]{2,1,0:T(8,128)(2,1)S(1)}, u32[]{:S(2)}, u32[]{:S(2)}) %collective-permute-start.8) | collective-permute-done | bytes 131104 | tf_op jit(solution)/shard_map/ppermute | solution.py:44
  68.7 3.1 %collective-permute-done.10 = bf16[2,256,128]{2,1,0:T(8,128)(2,1)S(1)} collective-permute-done((bf16[2,256,128]{2,1,0:T(8,128)(2,1)S(1)}, bf16[2,256,128]{2,1,0:T(8,128)(2,1)S(1)}, u32[]{:S(2)}, u32[]{:S(2)}) %collective-permute-start.10) | collective-permute-done | bytes 131104 | tf_op jit(solution)/shard_map/ppermute | solution.py:44
  71.8 0.0 collective-permute-done.9
  71.8 0.1 fusion.1
  71.9 0.2 copy.11
  72.1 0.7 copy.14
  72.8 7.5 %all-to-all-done.1 = bf16[16,128,256]{2,1,0:T(8,128)(2,1)S(1)} async-done(((bf16[16,128,256]{2,1,0:T(8,128)(2,1)}), bf16[16,128,256]{2,1,0:T(8,128)(2,1)S(1)}, u32[]{:S(2)}, u32[]{:S(2)}) %all-to-all-start.1) | async-done | bytes 1048608 | tf_op jit(solution)/shard_map/all_to_all | solution.py:57
  80.3 0.1 convert_reduce_fusion
  80.4 0.7 fusion.4
  (3 shorter events, 0.0 us)
Async XLA Ops:
  0.6 0.9 %copy-start.8 = (bf16[128,512]{1,0:T(8,128)(2,1)S(1)}, bf16[128,512]{1,0:T(8,128)(2,1)}, u32[]{:S(2)}) copy-start(bf16[128,512]{1,0:T(8,128)(2,1)} %q_hbm.1) | copy-start | bytes 393220
  1.5 0.9 %copy-start.9 = (bf16[128,512]{1,0:T(8,128)(2,1)S(1)}, bf16[128,512]{1,0:T(8,128)(2,1)}, u32[]{:S(2)}) copy-start(bf16[128,512]{1,0:T(8,128)(2,1)} %g_hbm.1) | copy-start | bytes 393220
  2.4 0.9 %copy-start.10 = (bf16[128,512]{1,0:T(8,128)(2,1)S(1)}, bf16[128,512]{1,0:T(8,128)(2,1)}, u32[]{:S(2)}) copy-start(bf16[128,512]{1,0:T(8,128)(2,1)} %o_hbm.1) | copy-start | bytes 393220
  3.3 0.8 copy-start.11
  4.1 0.8 copy-start.12
  4.9 0.7 copy-start.13
  5.5 0.7 copy-start.14
  6.2 0.7 copy-start.15
  8.9 29.1 %all-to-all-start = ((bf16[16,144,256]{2,1,0:T(8,128)(2,1)}), bf16[16,144,256]{2,1,0:T(8,128)(2,1)S(1)}, u32[]{:S(2)}, u32[]{:S(2)}) async-start(bf16[16,144,256]{2,1,0:T(8,128)(2,1)} %get-tuple-element.9), calls=%async_computation | async-start | bytes 2359296 | tf_op jit(solution)/shard_map/all_to_all | solution.py:57
  16.0 15.7 %collective-permute-start.2 = (bf16[2,272,256]{2,1,0:T(8,128)(2,1)S(1)}, bf16[2,272,256]{2,1,0:T(8,128)(2,1)S(1)}, u32[]{:S(2)}, u32[]{:S(2)}) collective-permute-start(bf16[2,272,256]{2,1,0:T(8,128)(2,1)S(1)} %get-tuple-element.8.refs_0_), channel_id=1, source_target_pairs={{0,80},{1,81},{2,82},{3,83},{4,84},{5,85},{6,86},{7,87},{8,88},{9,... | collective-permute-start | bytes 835592 | tf_op jit(solution)/shard_map/ppermute | solution.py:44
  20.1 11.6 %collective-permute-start.1 = (bf16[2,272,256]{2,1,0:T(8,128)(2,1)S(1)}, bf16[2,272,256]{2,1,0:T(8,128)(2,1)S(1)}, u32[]{:S(2)}, u32[]{:S(2)}) collective-permute-start(bf16[2,272,256]{2,1,0:T(8,128)(2,1)S(1)} %get-tuple-element.8.refs_0_), channel_id=1, source_target_pairs={{0,16},{1,17},{2,18},{3,19},{4,20},{5,21},{6,22},{7,23},{8,24},{9,... | collective-permute-start | bytes 835592 | tf_op jit(solution)/shard_map/ppermute | solution.py:44
  20.1 15.0 %collective-permute-start = (bf16[2,272,256]{2,1,0:T(8,128)(2,1)S(1)}, bf16[2,272,256]{2,1,0:T(8,128)(2,1)S(1)}, u32[]{:S(2)}, u32[]{:S(2)}) collective-permute-start(bf16[2,272,256]{2,1,0:T(8,128)(2,1)S(1)} %get-tuple-element.8.refs_0_), channel_id=1, source_target_pairs={{0,64},{1,65},{2,66},{3,67},{4,68},{5,69},{6,70},{7,71},{8,72},{9,... | collective-permute-start | bytes 835592 | tf_op jit(solution)/shard_map/ppermute | solution.py:44
  21.4 13.8 %collective-permute-start.3 = (bf16[2,272,256]{2,1,0:T(8,128)(2,1)S(1)}, bf16[2,272,256]{2,1,0:T(8,128)(2,1)S(1)}, u32[]{:S(2)}, u32[]{:S(2)}) collective-permute-start(bf16[2,272,256]{2,1,0:T(8,128)(2,1)S(1)} %get-tuple-element.8.refs_0_), channel_id=1, source_target_pairs={{0,32},{1,33},{2,34},{3,35},{4,36},{5,37},{6,38},{7,39},{8,40},{9,... | collective-permute-start | bytes 835592 | tf_op jit(solution)/shard_map/ppermute | solution.py:52
  31.7 4.1 %collective-permute-start.6 = (bf16[2,272,256]{2,1,0:T(8,128)(2,1)S(1)}, bf16[2,272,256]{2,1,0:T(8,128)(2,1)S(1)}, u32[]{:S(2)}, u32[]{:S(2)}) collective-permute-start(bf16[2,272,256]{2,1,0:T(8,128)(2,1)S(1)} %collective-permute-done.2.refs_3_), channel_id=1, source_target_pairs={{0,32},{1,33},{2,34},{3,35},{4,36},{5,37},{6,38},{7,39},{8,40},{9,... | collective-permute-start | bytes 835592 | tf_op jit(solution)/shard_map/ppermute | solution.py:52
  31.7 4.8 %collective-permute-start.5 = (bf16[2,272,256]{2,1,0:T(8,128)(2,1)S(1)}, bf16[2,272,256]{2,1,0:T(8,128)(2,1)S(1)}, u32[]{:S(2)}, u32[]{:S(2)}) collective-permute-start(bf16[2,272,256]{2,1,0:T(8,128)(2,1)S(1)} %collective-permute-done.1.refs_2_), channel_id=1, source_target_pairs={{0,32},{1,33},{2,34},{3,35},{4,36},{5,37},{6,38},{7,39},{8,40},{9,... | collective-permute-start | bytes 835592 | tf_op jit(solution)/shard_map/ppermute | solution.py:52
  35.1 2.1 %collective-permute-start.4 = (bf16[2,272,256]{2,1,0:T(8,128)(2,1)S(1)}, bf16[2,272,256]{2,1,0:T(8,128)(2,1)S(1)}, u32[]{:S(2)}, u32[]{:S(2)}) collective-permute-start(bf16[2,272,256]{2,1,0:T(8,128)(2,1)S(1)} %collective-permute-done.refs_1_), channel_id=1, source_target_pairs={{0,32},{1,33},{2,34},{3,35},{4,36},{5,37},{6,38},{7,39},{8,40},{9,... | collective-permute-start | bytes 835592 | tf_op jit(solution)/shard_map/ppermute | solution.py:52
  35.1 0.7 copy-start
  35.8 0.7 copy-start.2
  36.6 0.7 copy-start.4
  37.3 0.7 copy-start.6
  38.0 1.0 %copy-start.1 = (bf16[2,272,256]{2,1,0:T(8,128)(2,1)S(1)}, bf16[2,272,256]{2,1,0:T(8,128)(2,1)}, u32[]{:S(2)}) copy-start(bf16[2,272,256]{2,1,0:T(8,128)(2,1)} %copy-done) | copy-start | bytes 835588
  38.9 1.0 %copy-start.3 = (bf16[2,272,256]{2,1,0:T(8,128)(2,1)S(1)}, bf16[2,272,256]{2,1,0:T(8,128)(2,1)}, u32[]{:S(2)}) copy-start(bf16[2,272,256]{2,1,0:T(8,128)(2,1)} %copy-done.2) | copy-start | bytes 835588
  39.9 1.0 %copy-start.5 = (bf16[2,272,256]{2,1,0:T(8,128)(2,1)S(1)}, bf16[2,272,256]{2,1,0:T(8,128)(2,1)}, u32[]{:S(2)}) copy-start(bf16[2,272,256]{2,1,0:T(8,128)(2,1)} %copy-done.4) | copy-start | bytes 835588
  40.8 1.0 %copy-start.7 = (bf16[2,272,256]{2,1,0:T(8,128)(2,1)S(1)}, bf16[2,272,256]{2,1,0:T(8,128)(2,1)}, u32[]{:S(2)}) copy-start(bf16[2,272,256]{2,1,0:T(8,128)(2,1)} %copy-done.6) | copy-start | bytes 835588
  51.4 10.9 %collective-permute-start.7 = (bf16[8,256,128]{2,1,0:T(8,128)(2,1)}, bf16[8,256,128]{2,1,0:T(8,128)(2,1)S(1)}, u32[]{:S(2)}, u32[]{:S(2)}) collective-permute-start(bf16[8,256,128]{2,1,0:T(8,128)(2,1)} %get-tuple-element.11), channel_id=1, source_target_pairs={{0,32},{1,33},{2,34},{3,35},{4,36},{5,37},{6,38},{7,39},{8,40},{9,... | collective-permute-start | bytes 1572872 | tf_op jit(solution)/shard_map/ppermute | solution.py:52
  53.1 27.1 %all-to-all-start.1 = ((bf16[16,128,256]{2,1,0:T(8,128)(2,1)}), bf16[16,128,256]{2,1,0:T(8,128)(2,1)S(1)}, u32[]{:S(2)}, u32[]{:S(2)}) async-start(bf16[16,128,256]{2,1,0:T(8,128)(2,1)} %get-tuple-element.12), calls=%async_computation.1 | async-start | bytes 2097152 | tf_op jit(solution)/shard_map/all_to_all | solution.py:57
  62.5 6.2 %collective-permute-start.8 = (bf16[2,256,128]{2,1,0:T(8,128)(2,1)S(1)}, bf16[2,256,128]{2,1,0:T(8,128)(2,1)S(1)}, u32[]{:S(2)}, u32[]{:S(2)}) collective-permute-start(bf16[2,256,128]{2,1,0:T(8,128)(2,1)S(1)} %get-tuple-element.15), channel_id=1, source_target_pairs={{0,80},{1,81},{2,82},{3,83},{4,84},{5,85},{6,86},{7,87},{8,88},{9,... | collective-permute-start | bytes 393224 | tf_op jit(solution)/shard_map/ppermute | solution.py:44
  62.6 9.2 %collective-permute-start.10 = (bf16[2,256,128]{2,1,0:T(8,128)(2,1)S(1)}, bf16[2,256,128]{2,1,0:T(8,128)(2,1)S(1)}, u32[]{:S(2)}, u32[]{:S(2)}) collective-permute-start(bf16[2,256,128]{2,1,0:T(8,128)(2,1)S(1)} %get-tuple-element.16), channel_id=1, source_target_pairs={{0,64},{1,65},{2,66},{3,67},{4,68},{5,69},{6,70},{7,71},{8,72},{9,... | collective-permute-start | bytes 393224 | tf_op jit(solution)/shard_map/ppermute | solution.py:44
  64.6 7.2 %collective-permute-start.9 = (bf16[2,256,128]{2,1,0:T(8,128)(2,1)S(1)}, bf16[2,256,128]{2,1,0:T(8,128)(2,1)S(1)}, u32[]{:S(2)}, u32[]{:S(2)}) collective-permute-start(bf16[2,256,128]{2,1,0:T(8,128)(2,1)S(1)} %get-tuple-element.17), channel_id=1, source_target_pairs={{0,16},{1,17},{2,18},{3,19},{4,20},{5,21},{6,22},{7,23},{8,24},{9,... | collective-permute-start | bytes 393224 | tf_op jit(solution)/shard_map/ppermute | solution.py:44

commit v2 on v1

--- a/solution.py
+++ b/solution.py
@@ -136,7 +136,7 @@
             line,
             pltpu.SemaphoreType.DMA((8,)),
         ],
-        compiler_params=pltpu.CompilerParams(vmem_limit_bytes=8 * 1024 * 1024),
+        compiler_params=pltpu.CompilerParams(vmem_limit_bytes=56 * 1024 * 1024),
         name="pack",
     )(
         queries,
@@ -311,7 +311,7 @@
             pltpu.SemaphoreType.DMA,
             pltpu.SemaphoreType.DMA((PIECES,)),
         ],
-        compiler_params=pltpu.CompilerParams(vmem_limit_bytes=16 * 1024 * 1024),
+        compiler_params=pltpu.CompilerParams(vmem_limit_bytes=50 * 1024 * 1024),
         name="grads",
     )(*pieces, kv)
 
@@ -329,11 +329,12 @@
     total = (own + to_partner(other).astype(jnp.float32)).reshape(DEPTH, 2, STACK, HEAD)
     back = [along_z(total[shift].astype(jnp.bfloat16), -shift) for shift in (1, 2, 3)]
     parts = over_plane(dkv)
-    grad_kv = jnp.sum(parts.astype(jnp.float32), axis=0)
+    grad_keys = jnp.sum(parts[:, :, :HEAD].astype(jnp.float32), axis=0)
+    grad_values = jnp.sum(parts[:, :, HEAD:].astype(jnp.float32), axis=0)
     grad_queries = total[0]
     for part in back:
         grad_queries = grad_queries + part.astype(jnp.float32)
-    return (unstack(grad_queries), grad_kv[:, :HEAD], grad_kv[:, HEAD:])
+    return (unstack(grad_queries), grad_keys, grad_values)
 
 
 def solution(mesh):

time: 81 us -> 70.6 us (0.87)
  local copies, waits for them, and re-layouts: 14.4 us -> 0.93 us
  Pallas kernels: 11.6 us -> 14.7 us
  starting transfers between devices: 26 us -> 25 us
  waiting for transfers between devices: 28 us -> 29 us
    unnamed x33 -> x5, local copies, waits for them, and re-layouts: 13.6 us -> 0.73 us
    pallas_call x1, Pallas kernels: 9.58 us -> 12.1 us  [grads(): pl.pallas_call(grad_kernel, out_shape=(jax.ShapeDtypeStruct((PLANE, ROWS,...]
    ppermute x5, starting transfers between devices: 2.27 us -> 0.6 us  [to_partner(): return lax.ppermute(array, AXES, pairs)]
    ppermute x5, waiting for transfers between devices: 0.01 us -> 1.55 us  [to_partner(): return lax.ppermute(array, AXES, pairs)]
    all_to_all x2, waiting for transfers between devices: 7.5 us -> 6.54 us  [over_plane(): lax.all_to_all(array, 'inner', 0, 0, axis_index_groups=groups, tiled=True)]
  transfers between devices with their start and end apart: 13 -> 13, of which waited for: 5 -> 6; matrix products, arithmetic and copies ran while one was open for 1% -> 2% of each run, Pallas kernels for 0% -> 0%
where the time goes in v2:
time: 70.6 us; the launch traced here: 71.4 us
  waiting for transfers between devices  29 us (41%)
  starting transfers between devices  25 us (35%)
  Pallas kernels  14.7 us (21%)
  other arithmetic  1.01 us (1%)
  local copies, waits for them, and re-layouts  0.93 us (1%)
  between operations  0.76 us (1%)
    ppermute x6, waiting for transfers between devices, along_z(): return lax.ppermute(array, AXES, pairs)  20.9 us
    all_to_all x2, starting transfers between devices, over_plane(): lax.all_to_all(array, 'inner', 0, 0, axis_index_groups=groups, tiled=True)  16.3 us
    pallas_call x1, Pallas kernels, grads(): pl.pallas_call(grad_kernel, out_shape=(jax.ShapeDtypeStruct((PLANE, ROWS,...  12.1 us
    ppermute x6, starting transfers between devices, along_z(): return lax.ppermute(array, AXES, pairs)  8.09 us
    all_to_all x2, waiting for transfers between devices, over_plane(): lax.all_to_all(array, 'inner', 0, 0, axis_index_groups=groups, tiled=True)  6.54 us
    pallas_call x1, Pallas kernels, pack(): pl.pallas_call(pack_kernel, out_shape=(jax.ShapeDtypeStruct((2, STACK + S...  2.58 us
    ppermute x5, waiting for transfers between devices, to_partner(): return lax.ppermute(array, AXES, pairs)  1.55 us
  transfers between devices with their start and end apart: 13, of which 6 were waited for; matrix products, arithmetic and copies ran while one was open for 2% of the time, Pallas kernels for 0%

profile of v2, /device:TPU:0, one launch (start us, length us, event | category | flops | bytes accessed | tf_op | source)
XLA Modules:
  0.0 71.4 jit_solution(8228938222383731258)
XLA Ops:
  0.6 2.6 %pack.1 = (bf16[2,272,256]{2,1,0:T(8,128)(2,1)}, bf16[16,144,256]{2,1,0:T(8,128)(2,1)}) custom-call(bf16[128,512]{1,0:T(8,128)(2,1)} %q_hbm.1, bf16[128,512]{1,0:T(8,128)(2,1)} %g_hbm.1, bf16[128,512]{1,0:T(8,128)(2,1)} %o_hbm.1, bf16[128,128]{1,0:T(8,128)(2,1)} %k_hbm.1, bf16[128,128]{1,0:T(8,128)(2,1)} %v_hbm.1, f32[4,128]{1,0:T(4,128)} %bitcast.14, ...), custom_call_target="tpu_custom_call" | custom-call | tf_op jit(solution)/shard_map/pack/pallas_call | solution.py:120
  3.2 0.0 copy-start
  3.2 7.3 %all-to-all-start = ((bf16[16,144,256]{2,1,0:T(8,128)(2,1)}), bf16[16,144,256]{2,1,0:T(8,128)(2,1)}, u32[]{:S(2)}, u32[]{:S(2)}) async-start(bf16[16,144,256]{2,1,0:T(8,128)(2,1)} %get-tuple-element.9), calls=%async_computation | async-start | bytes 2359296 | tf_op jit(solution)/shard_map/all_to_all | solution.py:57
  10.5 0.0 copy-done
  10.6 4.1 %collective-permute-start.2 = (bf16[2,272,256]{2,1,0:T(8,128)(2,1)S(1)}, bf16[2,272,256]{2,1,0:T(8,128)(2,1)S(1)}, u32[]{:S(2)}, u32[]{:S(2)}) collective-permute-start(bf16[2,272,256]{2,1,0:T(8,128)(2,1)S(1)} %copy-done), channel_id=1, source_target_pairs={{0,80},{1,81},{2,82},{3,83},{4,84},{5,85},{6,86},{7,87},{8,88},{9,... | collective-permute-start | bytes 835592 | tf_op jit(solution)/shard_map/ppermute | solution.py:44
  14.7 0.0 collective-permute-start.1
  14.7 1.3 %collective-permute-start = (bf16[2,272,256]{2,1,0:T(8,128)(2,1)S(1)}, bf16[2,272,256]{2,1,0:T(8,128)(2,1)S(1)}, u32[]{:S(2)}, u32[]{:S(2)}) collective-permute-start(bf16[2,272,256]{2,1,0:T(8,128)(2,1)S(1)} %copy-done), channel_id=1, source_target_pairs={{0,64},{1,65},{2,66},{3,67},{4,68},{5,69},{6,70},{7,71},{8,72},{9,... | collective-permute-start | bytes 835592 | tf_op jit(solution)/shard_map/ppermute | solution.py:44
  15.9 0.0 collective-permute-start.3
  15.9 10.3 %collective-permute-done.2.refs_3_ = bf16[2,272,256]{2,1,0:T(8,128)(2,1)S(1)} collective-permute-done((bf16[2,272,256]{2,1,0:T(8,128)(2,1)S(1)}, bf16[2,272,256]{2,1,0:T(8,128)(2,1)S(1)}, u32[]{:S(2)}, u32[]{:S(2)}) %collective-permute-start.2) | collective-permute-done | bytes 278560 | tf_op jit(solution)/shard_map/ppermute | solution.py:44
  26.3 0.0 collective-permute-start.6
  26.3 0.0 collective-permute-done.1.refs_2_
  26.3 0.5 collective-permute-start.5
  26.8 2.9 %collective-permute-done.refs_1_ = bf16[2,272,256]{2,1,0:T(8,128)(2,1)S(1)} collective-permute-done((bf16[2,272,256]{2,1,0:T(8,128)(2,1)S(1)}, bf16[2,272,256]{2,1,0:T(8,128)(2,1)S(1)}, u32[]{:S(2)}, u32[]{:S(2)}) %collective-permute-start) | collective-permute-done | bytes 278560 | tf_op jit(solution)/shard_map/ppermute | solution.py:44
  29.7 0.0 collective-permute-start.4
  29.7 0.0 collective-permute-done.3.refs_4_
  29.7 0.0 collective-permute-done.6.refs_7_
  29.7 0.0 collective-permute-done.5.refs_6_
  29.7 1.5 %collective-permute-done.4.refs_5_ = bf16[2,272,256]{2,1,0:T(8,128)(2,1)S(1)} collective-permute-done((bf16[2,272,256]{2,1,0:T(8,128)(2,1)S(1)}, bf16[2,272,256]{2,1,0:T(8,128)(2,1)S(1)}, u32[]{:S(2)}, u32[]{:S(2)}) %collective-permute-start.4) | collective-permute-done | bytes 278560 | tf_op jit(solution)/shard_map/ppermute | solution.py:52
  31.2 0.0 all-to-all-done.refs_8_
  31.2 12.1 %grads.1 = (bf16[16,128,256]{2,1,0:T(8,128)(2,1)}, f32[8,256,128]{2,1,0:T(8,128)}, bf16[8,256,128]{2,1,0:T(8,128)(2,1)S(1)}) custom-call(bf16[2,272,256]{2,1,0:T(8,128)(2,1)S(1)} %copy-done, bf16[2,272,256]{2,1,0:T(8,128)(2,1)S(1)} %collective-permute-done.refs_1_, bf16[2,272,256]{2,1,0:T(8,128)(2,1)S(1)} %collective-permute-done.1.refs_2_, ...), custom_call_target="tpu_custom_call" | custom-call | tf_op jit(solution)/shard_map/grads/pallas_call | solution.py:292
  43.4 0.0 copy-start.1
  43.4 0.1 collective-permute-start.7
  43.5 9.0 %all-to-all-start.1 = ((bf16[16,128,256]{2,1,0:T(8,128)(2,1)}), bf16[16,128,256]{2,1,0:T(8,128)(2,1)S(1)}, u32[]{:S(2)}, u32[]{:S(2)}) async-start(bf16[16,128,256]{2,1,0:T(8,128)(2,1)} %get-tuple-element.12), calls=%async_computation.1 | async-start | bytes 2097152 | tf_op jit(solution)/shard_map/all_to_all | solution.py:57
  52.5 0.0 collective-permute-done.7
  52.5 0.0 copy-done.1
  52.5 0.2 fusion.2
  52.7 1.2 %collective-permute-start.8 = (bf16[2,256,128]{2,1,0:T(8,128)(2,1)S(1)}, bf16[2,256,128]{2,1,0:T(8,128)(2,1)S(1)}, u32[]{:S(2)}, u32[]{:S(2)}) collective-permute-start(bf16[2,256,128]{2,1,0:T(8,128)(2,1)S(1)} %get-tuple-element.17), channel_id=1, source_target_pairs={{0,80},{1,81},{2,82},{3,83},{4,84},{5,85},{6,86},{7,87},{8,88},{9,... | collective-permute-start | bytes 393224 | tf_op jit(solution)/shard_map/ppermute | solution.py:44
  53.9 0.9 %collective-permute-start.10 = (bf16[2,256,128]{2,1,0:T(8,128)(2,1)S(1)}, bf16[2,256,128]{2,1,0:T(8,128)(2,1)S(1)}, u32[]{:S(2)}, u32[]{:S(2)}) collective-permute-start(bf16[2,256,128]{2,1,0:T(8,128)(2,1)S(1)} %get-tuple-element.18), channel_id=1, source_target_pairs={{0,64},{1,65},{2,66},{3,67},{4,68},{5,69},{6,70},{7,71},{8,72},{9,... | collective-permute-start | bytes 393224 | tf_op jit(solution)/shard_map/ppermute | solution.py:44
  54.8 0.6 collective-permute-start.9
  55.5 2.6 %collective-permute-done.8 = bf16[2,256,128]{2,1,0:T(8,128)(2,1)S(1)} collective-permute-done((bf16[2,256,128]{2,1,0:T(8,128)(2,1)S(1)}, bf16[2,256,128]{2,1,0:T(8,128)(2,1)S(1)}, u32[]{:S(2)}, u32[]{:S(2)}) %collective-permute-start.8) | collective-permute-done | bytes 131104 | tf_op jit(solution)/shard_map/ppermute | solution.py:44
  58.1 5.0 %collective-permute-done.10 = bf16[2,256,128]{2,1,0:T(8,128)(2,1)S(1)} collective-permute-done((bf16[2,256,128]{2,1,0:T(8,128)(2,1)S(1)}, bf16[2,256,128]{2,1,0:T(8,128)(2,1)S(1)}, u32[]{:S(2)}, u32[]{:S(2)}) %collective-permute-start.10) | collective-permute-done | bytes 131104 | tf_op jit(solution)/shard_map/ppermute | solution.py:44
  63.1 0.0 collective-permute-done.9
  63.1 0.1 fusion.1
  63.2 0.2 copy.11
  63.4 0.7 %copy.14 = f32[16,8,4,128]{3,1,2,0:T(8,128)} copy(f32[16,8,4,128]{3,2,1,0:T(4,128)S(1)} %bitcast.12) | data formatting | bytes 524288
  64.1 6.5 %all-to-all-done.1 = bf16[16,128,256]{2,1,0:T(8,128)(2,1)S(1)} async-done(((bf16[16,128,256]{2,1,0:T(8,128)(2,1)}), bf16[16,128,256]{2,1,0:T(8,128)(2,1)S(1)}, u32[]{:S(2)}, u32[]{:S(2)}) %all-to-all-start.1) | async-done | bytes 1048608 | tf_op jit(solution)/shard_map/all_to_all | solution.py:57
  70.6 0.8 %convert_reduce_fusion = (f32[128,128]{1,0:T(8,128)}, f32[128,128]{1,0:T(8,128)}) fusion(bf16[16,128,256]{2,1,0:T(8,128)(2,1)S(1)} %all-to-all-done.1), kind=kLoop, calls=%fused_computation | loop fusion | flops 1015808 | bytes 1179648 | tf_op jit(solution)/shard_map/reduce_sum | solution.py:333
  (1 shorter events, 0.0 us)
Async XLA Ops:
  3.2 7.3 %copy-start = (bf16[2,272,256]{2,1,0:T(8,128)(2,1)S(1)}, bf16[2,272,256]{2,1,0:T(8,128)(2,1)}, u32[]{:S(2)}) copy-start(bf16[2,272,256]{2,1,0:T(8,128)(2,1)} %get-tuple-element.8.refs_0_) | copy-start | bytes 835588
  3.2 28.0 %all-to-all-start = ((bf16[16,144,256]{2,1,0:T(8,128)(2,1)}), bf16[16,144,256]{2,1,0:T(8,128)(2,1)}, u32[]{:S(2)}, u32[]{:S(2)}) async-start(bf16[16,144,256]{2,1,0:T(8,128)(2,1)} %get-tuple-element.9), calls=%async_computation | async-start | bytes 2359296 | tf_op jit(solution)/shard_map/all_to_all | solution.py:57
  10.6 15.7 %collective-permute-start.2 = (bf16[2,272,256]{2,1,0:T(8,128)(2,1)S(1)}, bf16[2,272,256]{2,1,0:T(8,128)(2,1)S(1)}, u32[]{:S(2)}, u32[]{:S(2)}) collective-permute-start(bf16[2,272,256]{2,1,0:T(8,128)(2,1)S(1)} %copy-done), channel_id=1, source_target_pairs={{0,80},{1,81},{2,82},{3,83},{4,84},{5,85},{6,86},{7,87},{8,88},{9,... | collective-permute-start | bytes 835592 | tf_op jit(solution)/shard_map/ppermute | solution.py:44
  14.7 11.6 %collective-permute-start.1 = (bf16[2,272,256]{2,1,0:T(8,128)(2,1)S(1)}, bf16[2,272,256]{2,1,0:T(8,128)(2,1)S(1)}, u32[]{:S(2)}, u32[]{:S(2)}) collective-permute-start(bf16[2,272,256]{2,1,0:T(8,128)(2,1)S(1)} %copy-done), channel_id=1, source_target_pairs={{0,16},{1,17},{2,18},{3,19},{4,20},{5,21},{6,22},{7,23},{8,24},{9,... | collective-permute-start | bytes 835592 | tf_op jit(solution)/shard_map/ppermute | solution.py:44
  14.7 15.0 %collective-permute-start = (bf16[2,272,256]{2,1,0:T(8,128)(2,1)S(1)}, bf16[2,272,256]{2,1,0:T(8,128)(2,1)S(1)}, u32[]{:S(2)}, u32[]{:S(2)}) collective-permute-start(bf16[2,272,256]{2,1,0:T(8,128)(2,1)S(1)} %copy-done), channel_id=1, source_target_pairs={{0,64},{1,65},{2,66},{3,67},{4,68},{5,69},{6,70},{7,71},{8,72},{9,... | collective-permute-start | bytes 835592 | tf_op jit(solution)/shard_map/ppermute | solution.py:44
  15.9 13.8 %collective-permute-start.3 = (bf16[2,272,256]{2,1,0:T(8,128)(2,1)S(1)}, bf16[2,272,256]{2,1,0:T(8,128)(2,1)S(1)}, u32[]{:S(2)}, u32[]{:S(2)}) collective-permute-start(bf16[2,272,256]{2,1,0:T(8,128)(2,1)S(1)} %copy-done), channel_id=1, source_target_pairs={{0,32},{1,33},{2,34},{3,35},{4,36},{5,37},{6,38},{7,39},{8,40},{9,... | collective-permute-start | bytes 835592 | tf_op jit(solution)/shard_map/ppermute | solution.py:52
  26.3 3.4 %collective-permute-start.6 = (bf16[2,272,256]{2,1,0:T(8,128)(2,1)S(1)}, bf16[2,272,256]{2,1,0:T(8,128)(2,1)S(1)}, u32[]{:S(2)}, u32[]{:S(2)}) collective-permute-start(bf16[2,272,256]{2,1,0:T(8,128)(2,1)S(1)} %collective-permute-done.2.refs_3_), channel_id=1, source_target_pairs={{0,32},{1,33},{2,34},{3,35},{4,36},{5,37},{6,38},{7,39},{8,40},{9,... | collective-permute-start | bytes 835592 | tf_op jit(solution)/shard_map/ppermute | solution.py:52
  26.3 3.4 %collective-permute-start.5 = (bf16[2,272,256]{2,1,0:T(8,128)(2,1)S(1)}, bf16[2,272,256]{2,1,0:T(8,128)(2,1)S(1)}, u32[]{:S(2)}, u32[]{:S(2)}) collective-permute-start(bf16[2,272,256]{2,1,0:T(8,128)(2,1)S(1)} %collective-permute-done.1.refs_2_), channel_id=1, source_target_pairs={{0,32},{1,33},{2,34},{3,35},{4,36},{5,37},{6,38},{7,39},{8,40},{9,... | collective-permute-start | bytes 835592 | tf_op jit(solution)/shard_map/ppermute | solution.py:52
  29.7 1.6 %collective-permute-start.4 = (bf16[2,272,256]{2,1,0:T(8,128)(2,1)S(1)}, bf16[2,272,256]{2,1,0:T(8,128)(2,1)S(1)}, u32[]{:S(2)}, u32[]{:S(2)}) collective-permute-start(bf16[2,272,256]{2,1,0:T(8,128)(2,1)S(1)} %collective-permute-done.refs_1_), channel_id=1, source_target_pairs={{0,32},{1,33},{2,34},{3,35},{4,36},{5,37},{6,38},{7,39},{8,40},{9,... | collective-permute-start | bytes 835592 | tf_op jit(solution)/shard_map/ppermute | solution.py:52
  43.4 9.1 %copy-start.1 = (f32[8,256,128]{2,1,0:T(8,128)S(1)}, f32[8,256,128]{2,1,0:T(8,128)}, u32[]{:S(2)}) copy-start(f32[8,256,128]{2,1,0:T(8,128)} %get-tuple-element.10) | copy-start | bytes 3145732
  43.4 9.1 %collective-permute-start.7 = (bf16[8,256,128]{2,1,0:T(8,128)(2,1)S(1)}, bf16[8,256,128]{2,1,0:T(8,128)(2,1)S(1)}, u32[]{:S(2)}, u32[]{:S(2)}) collective-permute-start(bf16[8,256,128]{2,1,0:T(8,128)(2,1)S(1)} %get-tuple-element.11), channel_id=1, source_target_pairs={{0,32},{1,33},{2,34},{3,35},{4,36},{5,37},{6,38},{7,39},{8,40},{9,... | collective-permute-start | bytes 1572872 | tf_op jit(solution)/shard_map/ppermute | solution.py:52
  43.5 27.1 %all-to-all-start.1 = ((bf16[16,128,256]{2,1,0:T(8,128)(2,1)}), bf16[16,128,256]{2,1,0:T(8,128)(2,1)S(1)}, u32[]{:S(2)}, u32[]{:S(2)}) async-start(bf16[16,128,256]{2,1,0:T(8,128)(2,1)} %get-tuple-element.12), calls=%async_computation.1 | async-start | bytes 2097152 | tf_op jit(solution)/shard_map/all_to_all | solution.py:57
  52.7 5.3 %collective-permute-start.8 = (bf16[2,256,128]{2,1,0:T(8,128)(2,1)S(1)}, bf16[2,256,128]{2,1,0:T(8,128)(2,1)S(1)}, u32[]{:S(2)}, u32[]{:S(2)}) collective-permute-start(bf16[2,256,128]{2,1,0:T(8,128)(2,1)S(1)} %get-tuple-element.17), channel_id=1, source_target_pairs={{0,80},{1,81},{2,82},{3,83},{4,84},{5,85},{6,86},{7,87},{8,88},{9,... | collective-permute-start | bytes 393224 | tf_op jit(solution)/shard_map/ppermute | solution.py:44
  53.9 9.2 %collective-permute-start.10 = (bf16[2,256,128]{2,1,0:T(8,128)(2,1)S(1)}, bf16[2,256,128]{2,1,0:T(8,128)(2,1)S(1)}, u32[]{:S(2)}, u32[]{:S(2)}) collective-permute-start(bf16[2,256,128]{2,1,0:T(8,128)(2,1)S(1)} %get-tuple-element.18), channel_id=1, source_target_pairs={{0,64},{1,65},{2,66},{3,67},{4,68},{5,69},{6,70},{7,71},{8,72},{9,... | collective-permute-start | bytes 393224 | tf_op jit(solution)/shard_map/ppermute | solution.py:44
  54.8 8.3 %collective-permute-start.9 = (bf16[2,256,128]{2,1,0:T(8,128)(2,1)S(1)}, bf16[2,256,128]{2,1,0:T(8,128)(2,1)S(1)}, u32[]{:S(2)}, u32[]{:S(2)}) collective-permute-start(bf16[2,256,128]{2,1,0:T(8,128)(2,1)S(1)} %get-tuple-element.19), channel_id=1, source_target_pairs={{0,16},{1,17},{2,18},{3,19},{4,20},{5,21},{6,22},{7,23},{8,24},{9,... | collective-permute-start | bytes 393224 | tf_op jit(solution)/shard_map/ppermute | solution.py:44

commit v3 on v0

--- a/solution.py
+++ b/solution.py
@@ -20,8 +20,8 @@
 STACK = QH * BLOCK
 TILE = 256
 TILE_BLOCKS = TILE // BLOCK
-SLOTS = 40
-TOGETHER = 2
+JOBS = 256
+TOGETHER = 6
 FAR = 1.0e9
 AXES = ("outer", "inner")
 LOG2E = math.log2(math.e)
@@ -123,7 +123,7 @@
             jax.ShapeDtypeStruct((2, STACK + STATS, 2 * HEAD), jnp.bfloat16),
             jax.ShapeDtypeStruct((PLANE, ROWS + STATS, 2 * HEAD), jnp.bfloat16),
         ),
-        in_specs=[pl.BlockSpec(memory_space=pl.ANY)] * 8,
+        in_specs=[pl.BlockSpec(memory_space=pltpu.HBM)] * 8,
         out_specs=(pl.BlockSpec(memory_space=pltpu.VMEM),) * 2,
         scratch_shapes=[
             wide,
@@ -136,7 +136,7 @@
             line,
             pltpu.SemaphoreType.DMA((8,)),
         ],
-        compiler_params=pltpu.CompilerParams(vmem_limit_bytes=8 * 1024 * 1024),
+        compiler_params=pltpu.CompilerParams(vmem_limit_bytes=56 * 1024 * 1024),
         name="pack",
     )(
         queries,
@@ -153,8 +153,9 @@
 def grad_kernel(*refs):
     q_refs = refs[:PIECES]
     (kv_ref, dkv_ref, own_ref, other_ref) = refs[PIECES : PIECES + 4]
-    (qs, rows, dk, dv, dq, ints, ints_s, jobs, sem) = refs[PIECES + 4 :]
+    (qs, rows, dk, dv, dq, ints, ints_s, sem) = refs[PIECES + 4 :]
     scale = HEAD ** (-0.5)
+    half = QBLOCKS // 2
 
     tails = [kv_ref[d, ROWS : ROWS + STATS, 0:ROWS].astype(jnp.float32) for d in range(PLANE)]
     number = jnp.concatenate([tail[0:1] for tail in tails], axis=0)
@@ -163,13 +164,11 @@
     column = jnp.broadcast_to(column, (KBLOCKS, ROWS))
     pad = jnp.full((ROWS - KBLOCKS, ROWS), FAR, jnp.float32)
     line = jnp.concatenate([column, pad], axis=0).T
-    rank = jnp.sum((column < line[0:KBLOCKS]).astype(jnp.float32), axis=0, keepdims=True)
-    slot = lax.broadcasted_iota(jnp.int32, (SLOTS, ROWS), 0).astype(jnp.float32)
-    lane = lax.broadcasted_iota(jnp.int32, (SLOTS, ROWS), 1)
+    rank = jnp.sum((line[0:KBLOCKS] < column).astype(jnp.float32), axis=1, keepdims=True)
+    lane = lax.broadcasted_iota(jnp.int32, (KBLOCKS, ROWS), 1).astype(jnp.float32)
+    below_number = lax.broadcasted_iota(jnp.int32, (KBLOCKS, ROWS), 0).astype(jnp.float32)
     order = jnp.sum(
-        jnp.where((rank == slot) & (lane < KBLOCKS), lane.astype(jnp.float32), 0.0),
-        axis=1,
-        keepdims=True,
+        jnp.where(rank == lane, below_number, 0.0), axis=0, keepdims=True
     )
     below = [
         jnp.sum((key_seg < float(s)).astype(jnp.float32), axis=0, keepdims=True) for s in range(1, 9)
@@ -193,10 +192,22 @@
     before = jnp.sum((line[0:QBLOCKS] < numbers).astype(jnp.float32), axis=1, keepdims=True)
     same = jnp.sum((line[0:QBLOCKS] == numbers).astype(jnp.float32), axis=1, keepdims=True)
     low = jnp.floor(jnp.concatenate(begins, axis=0) * (1.0 / BLOCK))
-    empty = jnp.zeros((SLOTS - QBLOCKS, 1), jnp.float32)
-    low = jnp.concatenate([low, empty], axis=0)
-    high = jnp.concatenate([before + same, empty], axis=0)
-    ints[...] = jnp.where(lane == 0, order, jnp.where(lane == 1, low, high)).astype(jnp.int32)
+    steps = jnp.maximum(before + same - low, 0.0)
+    steps = jnp.floor((steps + (TILE_BLOCKS - 1)) * (1.0 / TILE_BLOCKS))
+    steps = jnp.broadcast_to(steps, (QBLOCKS, JOBS))
+    row = lax.broadcasted_iota(jnp.int32, (QBLOCKS, JOBS), 0)
+    done = steps
+    for shift in (1, 2, 4, 8):
+        done = done + jnp.where(row >= shift, pltpu.roll(done, shift, 0), 0.0)
+    job = lax.broadcasted_iota(jnp.int32, (QBLOCKS, JOBS), 1).astype(jnp.float32)
+    mine = (job < done) & (job >= done - steps)
+    code = row.astype(jnp.float32) * 64.0 + low + (job - (done - steps)) * TILE_BLOCKS
+    code = jnp.sum(jnp.where(mine, code, 0.0), axis=0, keepdims=True)
+    count = done[QBLOCKS - 1 : QBLOCKS]
+    code = jnp.where(job[0:1] < count, code, float(KBLOCKS))
+    ints[0:1, :] = code.astype(jnp.int32)
+    ints[1:2, 0:ROWS] = order.astype(jnp.int32)
+    ints[2:3, :] = count.astype(jnp.int32)
     copy = pltpu.make_async_copy(ints, ints_s, sem)
     copy.start()
 
@@ -205,25 +216,14 @@
         rows[qi, 0:1, :] = stat[0:1]
         rows[qi, 1:2, :] = stat[1:2]
         rows[qi, 2:3, :] = begin
+        qs[qi] = q_refs[qi // 2][qi % 2, 0:STACK, :]
         rows[qi, 3:4, :] = before[qi : qi + 1] * float(BLOCK) + same[qi : qi + 1] * within
-        qs[qi] = q_refs[qi // 2][qi % 2, 0:STACK, :]
     dk[...] = jnp.zeros_like(dk)
     dv[...] = jnp.zeros_like(dv)
     dq[...] = jnp.zeros_like(dq)
     copy.wait()
 
-    def list_block(qi, count):
-        lower = ints_s[qi, 1]
-        steps = jnp.right_shift(jnp.maximum(ints_s[qi, 2] - lower, 0) + (TILE_BLOCKS - 1), 2)
-
-        def put(step, count):
-            jobs[count] = qi * 64 + lower + step * TILE_BLOCKS
-            return count + 1
-
-        return lax.fori_loop(0, steps, put, count)
-
-    count = lax.fori_loop(0, QBLOCKS, list_block, 0)
-    jobs[count] = KBLOCKS
+    count = ints_s[2, 0]
     down = lax.broadcasted_iota(jnp.int32, (TILE, ROWS), 0).astype(jnp.float32)
     nt = (((1,), (1,)), ((), ()))
     tn = (((0,), (0,)), ((), ()))
@@ -231,7 +231,7 @@
     def products(job):
         qi = jnp.right_shift(job, 6)
         at = jnp.bitwise_and(job, 63)
-        blocks = [ints_s[at + i, 0] for i in range(TILE_BLOCKS)]
+        blocks = [ints_s[1, at + i] for i in range(TILE_BLOCKS)]
         kv = jnp.concatenate(
             [
                 kv_ref[
@@ -256,11 +256,11 @@
         ds = (w * (gp - rows[qi, 1:2, :]) * scale).astype(jnp.bfloat16)
         dv_part = jnp.dot(w.astype(jnp.bfloat16), g, preferred_element_type=jnp.float32)
         dk_part = jnp.dot(ds, q, preferred_element_type=jnp.float32)
-        dq_part = lax.dot_general(ds, k, tn, preferred_element_type=jnp.float32)
+        dq_part = lax.dot_general(k, ds, tn, preferred_element_type=jnp.float32)
         return qi, blocks, dq_part, dk_part, dv_part
 
     def jobs_step(step, carry):
-        done = [products(jobs[step * TOGETHER + i]) for i in range(TOGETHER)]
+        done = [products(ints_s[0, step * TOGETHER + i]) for i in range(TOGETHER)]
         for qi, blocks, dq_part, dk_part, dv_part in done:
             dq[qi] += dq_part
             for i, j in enumerate(blocks):
@@ -269,15 +269,15 @@
                 dv[j] += dv_part[part]
         return carry
 
-    lax.fori_loop(0, jnp.right_shift(count + TOGETHER - 1, 1), jobs_step, 0)
+    lax.fori_loop(0, lax.div(count + TOGETHER - 1, TOGETHER), jobs_step, 0)
 
     for j in range(KBLOCKS):
         d, to = j % PLANE, slice((j // PLANE) * BLOCK, (j // PLANE + 1) * BLOCK)
         dkv_ref[d, to, 0:HEAD] = dk[j].astype(jnp.bfloat16)
         dkv_ref[d, to, HEAD : 2 * HEAD] = dv[j].astype(jnp.bfloat16)
-    for qi in range(QBLOCKS // 2):
-        own_ref[qi] = dq[qi]
-        other_ref[qi] = dq[QBLOCKS // 2 + qi].astype(jnp.bfloat16)
+    for qi in range(half):
+        own_ref[qi] = dq[qi].astype(jnp.bfloat16).T
+        other_ref[qi] = dq[half + qi].astype(jnp.bfloat16).T
 
 
 def grads(pieces, kv):
@@ -286,7 +286,7 @@
         grad_kernel,
         out_shape=(
             jax.ShapeDtypeStruct((PLANE, ROWS, 2 * HEAD), jnp.bfloat16),
-            jax.ShapeDtypeStruct((half, STACK, HEAD), jnp.float32),
+            jax.ShapeDtypeStruct((half, STACK, HEAD), jnp.bfloat16),
             jax.ShapeDtypeStruct((half, STACK, HEAD), jnp.bfloat16),
         ),
         in_specs=[pl.BlockSpec(memory_space=pltpu.VMEM)] * (PIECES + 1),
@@ -296,13 +296,12 @@
             pltpu.VMEM((QBLOCKS, 8, STACK), jnp.float32),
             pltpu.VMEM((KBLOCKS, BLOCK, HEAD), jnp.float32),
             pltpu.VMEM((KBLOCKS, BLOCK, HEAD), jnp.float32),
-            pltpu.VMEM((QBLOCKS, STACK, HEAD), jnp.float32),
-            pltpu.VMEM((SLOTS, ROWS), jnp.int32),
-            pltpu.SMEM((SLOTS, ROWS), jnp.int32),
-            pltpu.SMEM((QBLOCKS * KBLOCKS // TILE_BLOCKS + 8,), jnp.int32),
+            pltpu.VMEM((QBLOCKS, HEAD, STACK), jnp.float32),
+            pltpu.VMEM((8, JOBS), jnp.int32),
+            pltpu.SMEM((8, JOBS), jnp.int32),
             pltpu.SemaphoreType.DMA,
         ],
-        compiler_params=pltpu.CompilerParams(vmem_limit_bytes=16 * 1024 * 1024),
+        compiler_params=pltpu.CompilerParams(vmem_limit_bytes=49 * 1024 * 1024),
         name="grads",
     )(*pieces, kv)
 
@@ -317,14 +316,16 @@
     kv = over_plane(kvmsg)
     column = column + [to_partner(piece) for piece in column]
     dkv, own, other = grads(column, kv)
-    total = (own + to_partner(other).astype(jnp.float32)).reshape(DEPTH, 2, STACK, HEAD)
+    total = own.astype(jnp.float32) + to_partner(other).astype(jnp.float32)
+    total = total.reshape(DEPTH, 2, STACK, HEAD)
     back = [along_z(total[shift].astype(jnp.bfloat16), -shift) for shift in (1, 2, 3)]
     parts = over_plane(dkv)
-    grad_kv = jnp.sum(parts.astype(jnp.float32), axis=0)
+    grad_keys = jnp.sum(parts[:, :, :HEAD].astype(jnp.float32), axis=0)
+    grad_values = jnp.sum(parts[:, :, HEAD:].astype(jnp.float32), axis=0)
     grad_queries = total[0]
     for part in back:
         grad_queries = grad_queries + part.astype(jnp.float32)
-    return (unstack(grad_queries), grad_kv[:, :HEAD], grad_kv[:, HEAD:])
+    return (unstack(grad_queries), grad_keys, grad_values)
 
 
 def solution(mesh):

time: 81.5 us -> 67.8 us (0.83)
  local copies, waits for them, and re-layouts: 14.4 us -> 0.93 us
  Pallas kernels: 14.7 us -> 11.5 us
  starting transfers between devices: 22.3 us -> 24.4 us
  waiting for transfers between devices: 27.6 us -> 28.5 us
    unnamed x33 -> x3, local copies, waits for them, and re-layouts: 13.6 us -> 0.73 us
    pallas_call x1, Pallas kernels: 12.7 us -> 8.95 us  [grads(): pl.pallas_call(grad_kernel, out_shape=(jax.ShapeDtypeStruct((PLANE, ROWS,...]
    all_to_all x2, starting transfers between devices: 13.4 us -> 15.2 us  [over_plane(): lax.all_to_all(array, 'inner', 0, 0, axis_index_groups=groups, tiled=True)]
    ppermute x5, waiting for transfers between devices: 0.01 us -> 1.55 us  [to_partner(): return lax.ppermute(array, AXES, pairs)]
  transfers between devices with their start and end apart: 13 -> 13, of which waited for: 5 -> 7; matrix products, arithmetic and copies ran while one was open for 1% -> 2% of each run, Pallas kernels for 0% -> 0%
where the time goes in v3:
time: 67.8 us; the launch traced here: 67.1 us
  waiting for transfers between devices  28.5 us (42%)
  starting transfers between devices  24.4 us (36%)
  Pallas kernels  11.5 us (17%)
  other arithmetic  1.01 us (1%)
  local copies, waits for them, and re-layouts  0.93 us (1%)
  between operations  0.74 us (1%)
    ppermute x6, waiting for transfers between devices, along_z(): return lax.ppermute(array, AXES, pairs)  19.5 us
    all_to_all x2, starting transfers between devices, over_plane(): lax.all_to_all(array, 'inner', 0, 0, axis_index_groups=groups, tiled=True)  15.2 us
    pallas_call x1, Pallas kernels, grads(): pl.pallas_call(grad_kernel, out_shape=(jax.ShapeDtypeStruct((PLANE, ROWS,...  8.95 us
    ppermute x6, starting transfers between devices, along_z(): return lax.ppermute(array, AXES, pairs)  8.5 us
    all_to_all x2, waiting for transfers between devices, over_plane(): lax.all_to_all(array, 'inner', 0, 0, axis_index_groups=groups, tiled=True)  7.46 us
    pallas_call x1, Pallas kernels, pack(): pl.pallas_call(pack_kernel, out_shape=(jax.ShapeDtypeStruct((2, STACK + S...  2.58 us
    ppermute x5, waiting for transfers between devices, to_partner(): return lax.ppermute(array, AXES, pairs)  1.55 us
  transfers between devices with their start and end apart: 13, of which 7 were waited for; matrix products, arithmetic and copies ran while one was open for 2% of the time, Pallas kernels for 0%

profile of v3, /device:TPU:0, one launch (start us, length us, event | category | flops | bytes accessed | tf_op | source)
XLA Modules:
  0.0 67.1 jit_solution(2476827003744281060)
XLA Ops:
  0.6 2.6 %pack.1 = (bf16[2,272,256]{2,1,0:T(8,128)(2,1)}, bf16[16,144,256]{2,1,0:T(8,128)(2,1)}) custom-call(bf16[128,512]{1,0:T(8,128)(2,1)} %q_hbm.1, bf16[128,512]{1,0:T(8,128)(2,1)} %g_hbm.1, bf16[128,512]{1,0:T(8,128)(2,1)} %o_hbm.1, bf16[128,128]{1,0:T(8,128)(2,1)} %k_hbm.1, bf16[128,128]{1,0:T(8,128)(2,1)} %v_hbm.1, f32[4,128]{1,0:T(4,128)} %bitcast.14, ...), custom_call_target="tpu_custom_call" | custom-call | tf_op jit(solution)/shard_map/pack/pallas_call | solution.py:120
  3.2 0.0 copy-start
  3.2 7.3 %all-to-all-start = ((bf16[16,144,256]{2,1,0:T(8,128)(2,1)}), bf16[16,144,256]{2,1,0:T(8,128)(2,1)}, u32[]{:S(2)}, u32[]{:S(2)}) async-start(bf16[16,144,256]{2,1,0:T(8,128)(2,1)} %get-tuple-element.9), calls=%async_computation | async-start | bytes 2359296 | tf_op jit(solution)/shard_map/all_to_all | solution.py:57
  10.5 0.0 copy-done
  10.6 4.1 %collective-permute-start.2 = (bf16[2,272,256]{2,1,0:T(8,128)(2,1)S(1)}, bf16[2,272,256]{2,1,0:T(8,128)(2,1)S(1)}, u32[]{:S(2)}, u32[]{:S(2)}) collective-permute-start(bf16[2,272,256]{2,1,0:T(8,128)(2,1)S(1)} %copy-done), channel_id=1, source_target_pairs={{0,80},{1,81},{2,82},{3,83},{4,84},{5,85},{6,86},{7,87},{8,88},{9,... | collective-permute-start | bytes 835592 | tf_op jit(solution)/shard_map/ppermute | solution.py:44
  14.7 0.0 collective-permute-start.1
  14.7 1.3 %collective-permute-start = (bf16[2,272,256]{2,1,0:T(8,128)(2,1)S(1)}, bf16[2,272,256]{2,1,0:T(8,128)(2,1)S(1)}, u32[]{:S(2)}, u32[]{:S(2)}) collective-permute-start(bf16[2,272,256]{2,1,0:T(8,128)(2,1)S(1)} %copy-done), channel_id=1, source_target_pairs={{0,64},{1,65},{2,66},{3,67},{4,68},{5,69},{6,70},{7,71},{8,72},{9,... | collective-permute-start | bytes 835592 | tf_op jit(solution)/shard_map/ppermute | solution.py:44
  15.9 0.0 collective-permute-start.3
  15.9 10.3 %collective-permute-done.2.refs_3_ = bf16[2,272,256]{2,1,0:T(8,128)(2,1)S(1)} collective-permute-done((bf16[2,272,256]{2,1,0:T(8,128)(2,1)S(1)}, bf16[2,272,256]{2,1,0:T(8,128)(2,1)S(1)}, u32[]{:S(2)}, u32[]{:S(2)}) %collective-permute-start.2) | collective-permute-done | bytes 278560 | tf_op jit(solution)/shard_map/ppermute | solution.py:44
  26.3 0.0 collective-permute-start.6
  26.3 0.0 collective-permute-done.1.refs_2_
  26.3 0.5 collective-permute-start.5
  26.8 2.9 %collective-permute-done.refs_1_ = bf16[2,272,256]{2,1,0:T(8,128)(2,1)S(1)} collective-permute-done((bf16[2,272,256]{2,1,0:T(8,128)(2,1)S(1)}, bf16[2,272,256]{2,1,0:T(8,128)(2,1)S(1)}, u32[]{:S(2)}, u32[]{:S(2)}) %collective-permute-start) | collective-permute-done | bytes 278560 | tf_op jit(solution)/shard_map/ppermute | solution.py:44
  29.7 0.0 collective-permute-start.4
  29.7 0.0 collective-permute-done.3.refs_4_
  29.7 0.0 collective-permute-done.6.refs_7_
  29.7 0.0 collective-permute-done.5.refs_6_
  29.7 1.5 %collective-permute-done.4.refs_5_ = bf16[2,272,256]{2,1,0:T(8,128)(2,1)S(1)} collective-permute-done((bf16[2,272,256]{2,1,0:T(8,128)(2,1)S(1)}, bf16[2,272,256]{2,1,0:T(8,128)(2,1)S(1)}, u32[]{:S(2)}, u32[]{:S(2)}) %collective-permute-start.4) | collective-permute-done | bytes 278560 | tf_op jit(solution)/shard_map/ppermute | solution.py:52
  31.2 0.0 all-to-all-done.refs_8_
  31.2 9.0 %grads.1 = (bf16[16,128,256]{2,1,0:T(8,128)(2,1)}, bf16[8,256,128]{2,1,0:T(8,128)(2,1)S(1)}, bf16[8,256,128]{2,1,0:T(8,128)(2,1)S(1)}) custom-call(bf16[2,272,256]{2,1,0:T(8,128)(2,1)S(1)} %copy-done, bf16[2,272,256]{2,1,0:T(8,128)(2,1)S(1)} %collective-permute-done.refs_1_, bf16[2,272,256]{2,1,0:T(8,128)(2,1)S(1)} %collective-permute-done.1.refs_2_, ...), custom_call_target="tpu_custom_call" | custom-call | tf_op jit(solution)/shard_map/grads/pallas_call | solution.py:285
  40.2 0.2 collective-permute-start.7
  40.4 7.9 %all-to-all-start.1 = ((bf16[16,128,256]{2,1,0:T(8,128)(2,1)}), bf16[16,128,256]{2,1,0:T(8,128)(2,1)S(1)}, u32[]{:S(2)}, u32[]{:S(2)}) async-start(bf16[16,128,256]{2,1,0:T(8,128)(2,1)} %get-tuple-element.12), calls=%async_computation.1 | async-start | bytes 2097152 | tf_op jit(solution)/shard_map/all_to_all | solution.py:57
  48.3 0.0 collective-permute-done.7
  48.4 0.2 fusion.2
  48.6 0.1 collective-permute-start.8
  48.6 2.0 %collective-permute-start.10 = (bf16[2,256,128]{2,1,0:T(8,128)(2,1)S(1)}, bf16[2,256,128]{2,1,0:T(8,128)(2,1)S(1)}, u32[]{:S(2)}, u32[]{:S(2)}) collective-permute-start(bf16[2,256,128]{2,1,0:T(8,128)(2,1)S(1)} %get-tuple-element.18), channel_id=1, source_target_pairs={{0,64},{1,65},{2,66},{3,67},{4,68},{5,69},{6,70},{7,71},{8,72},{9,... | collective-permute-start | bytes 393224 | tf_op jit(solution)/shard_map/ppermute | solution.py:44
  50.7 1.0 %collective-permute-start.9 = (bf16[2,256,128]{2,1,0:T(8,128)(2,1)S(1)}, bf16[2,256,128]{2,1,0:T(8,128)(2,1)S(1)}, u32[]{:S(2)}, u32[]{:S(2)}) collective-permute-start(bf16[2,256,128]{2,1,0:T(8,128)(2,1)S(1)} %get-tuple-element.19), channel_id=1, source_target_pairs={{0,16},{1,17},{2,18},{3,19},{4,20},{5,21},{6,22},{7,23},{8,24},{9,... | collective-permute-start | bytes 393224 | tf_op jit(solution)/shard_map/ppermute | solution.py:44
  51.7 3.0 %collective-permute-done.8 = bf16[2,256,128]{2,1,0:T(8,128)(2,1)S(1)} collective-permute-done((bf16[2,256,128]{2,1,0:T(8,128)(2,1)S(1)}, bf16[2,256,128]{2,1,0:T(8,128)(2,1)S(1)}, u32[]{:S(2)}, u32[]{:S(2)}) %collective-permute-start.8) | collective-permute-done | bytes 131104 | tf_op jit(solution)/shard_map/ppermute | solution.py:44
  54.7 1.4 %collective-permute-done.10 = bf16[2,256,128]{2,1,0:T(8,128)(2,1)S(1)} collective-permute-done((bf16[2,256,128]{2,1,0:T(8,128)(2,1)S(1)}, bf16[2,256,128]{2,1,0:T(8,128)(2,1)S(1)}, u32[]{:S(2)}, u32[]{:S(2)}) %collective-permute-start.10) | collective-permute-done | bytes 131104 | tf_op jit(solution)/shard_map/ppermute | solution.py:44
  56.2 1.7 %collective-permute-done.9 = bf16[2,256,128]{2,1,0:T(8,128)(2,1)S(1)} collective-permute-done((bf16[2,256,128]{2,1,0:T(8,128)(2,1)S(1)}, bf16[2,256,128]{2,1,0:T(8,128)(2,1)S(1)}, u32[]{:S(2)}, u32[]{:S(2)}) %collective-permute-start.9) | collective-permute-done | bytes 131104 | tf_op jit(solution)/shard_map/ppermute | solution.py:44
  57.9 0.1 fusion.1
  58.0 0.2 copy.11
  58.2 0.7 %copy.14 = f32[16,8,4,128]{3,1,2,0:T(8,128)} copy(f32[16,8,4,128]{3,2,1,0:T(4,128)S(1)} %bitcast.12) | data formatting | bytes 524288
  58.9 7.5 %all-to-all-done.1 = bf16[16,128,256]{2,1,0:T(8,128)(2,1)S(1)} async-done(((bf16[16,128,256]{2,1,0:T(8,128)(2,1)}), bf16[16,128,256]{2,1,0:T(8,128)(2,1)S(1)}, u32[]{:S(2)}, u32[]{:S(2)}) %all-to-all-start.1) | async-done | bytes 1048608 | tf_op jit(solution)/shard_map/all_to_all | solution.py:57
  66.3 0.8 %convert_reduce_fusion = (f32[128,128]{1,0:T(8,128)}, f32[128,128]{1,0:T(8,128)}) fusion(bf16[16,128,256]{2,1,0:T(8,128)(2,1)S(1)} %all-to-all-done.1), kind=kLoop, calls=%fused_computation | loop fusion | flops 1015808 | bytes 1179648 | tf_op jit(solution)/shard_map/reduce_sum | solution.py:324
  (1 shorter events, 0.0 us)
Async XLA Ops:
  3.2 7.3 %copy-start = (bf16[2,272,256]{2,1,0:T(8,128)(2,1)S(1)}, bf16[2,272,256]{2,1,0:T(8,128)(2,1)}, u32[]{:S(2)}) copy-start(bf16[2,272,256]{2,1,0:T(8,128)(2,1)} %get-tuple-element.8.refs_0_) | copy-start | bytes 835588
  3.2 28.0 %all-to-all-start = ((bf16[16,144,256]{2,1,0:T(8,128)(2,1)}), bf16[16,144,256]{2,1,0:T(8,128)(2,1)}, u32[]{:S(2)}, u32[]{:S(2)}) async-start(bf16[16,144,256]{2,1,0:T(8,128)(2,1)} %get-tuple-element.9), calls=%async_computation | async-start | bytes 2359296 | tf_op jit(solution)/shard_map/all_to_all | solution.py:57
  10.6 15.7 %collective-permute-start.2 = (bf16[2,272,256]{2,1,0:T(8,128)(2,1)S(1)}, bf16[2,272,256]{2,1,0:T(8,128)(2,1)S(1)}, u32[]{:S(2)}, u32[]{:S(2)}) collective-permute-start(bf16[2,272,256]{2,1,0:T(8,128)(2,1)S(1)} %copy-done), channel_id=1, source_target_pairs={{0,80},{1,81},{2,82},{3,83},{4,84},{5,85},{6,86},{7,87},{8,88},{9,... | collective-permute-start | bytes 835592 | tf_op jit(solution)/shard_map/ppermute | solution.py:44
  14.7 11.6 %collective-permute-start.1 = (bf16[2,272,256]{2,1,0:T(8,128)(2,1)S(1)}, bf16[2,272,256]{2,1,0:T(8,128)(2,1)S(1)}, u32[]{:S(2)}, u32[]{:S(2)}) collective-permute-start(bf16[2,272,256]{2,1,0:T(8,128)(2,1)S(1)} %copy-done), channel_id=1, source_target_pairs={{0,16},{1,17},{2,18},{3,19},{4,20},{5,21},{6,22},{7,23},{8,24},{9,... | collective-permute-start | bytes 835592 | tf_op jit(solution)/shard_map/ppermute | solution.py:44
  14.7 15.0 %collective-permute-start = (bf16[2,272,256]{2,1,0:T(8,128)(2,1)S(1)}, bf16[2,272,256]{2,1,0:T(8,128)(2,1)S(1)}, u32[]{:S(2)}, u32[]{:S(2)}) collective-permute-start(bf16[2,272,256]{2,1,0:T(8,128)(2,1)S(1)} %copy-done), channel_id=1, source_target_pairs={{0,64},{1,65},{2,66},{3,67},{4,68},{5,69},{6,70},{7,71},{8,72},{9,... | collective-permute-start | bytes 835592 | tf_op jit(solution)/shard_map/ppermute | solution.py:44
  15.9 13.8 %collective-permute-start.3 = (bf16[2,272,256]{2,1,0:T(8,128)(2,1)S(1)}, bf16[2,272,256]{2,1,0:T(8,128)(2,1)S(1)}, u32[]{:S(2)}, u32[]{:S(2)}) collective-permute-start(bf16[2,272,256]{2,1,0:T(8,128)(2,1)S(1)} %copy-done), channel_id=1, source_target_pairs={{0,32},{1,33},{2,34},{3,35},{4,36},{5,37},{6,38},{7,39},{8,40},{9,... | collective-permute-start | bytes 835592 | tf_op jit(solution)/shard_map/ppermute | solution.py:52
  26.3 3.4 %collective-permute-start.6 = (bf16[2,272,256]{2,1,0:T(8,128)(2,1)S(1)}, bf16[2,272,256]{2,1,0:T(8,128)(2,1)S(1)}, u32[]{:S(2)}, u32[]{:S(2)}) collective-permute-start(bf16[2,272,256]{2,1,0:T(8,128)(2,1)S(1)} %collective-permute-done.2.refs_3_), channel_id=1, source_target_pairs={{0,32},{1,33},{2,34},{3,35},{4,36},{5,37},{6,38},{7,39},{8,40},{9,... | collective-permute-start | bytes 835592 | tf_op jit(solution)/shard_map/ppermute | solution.py:52
  26.3 3.4 %collective-permute-start.5 = (bf16[2,272,256]{2,1,0:T(8,128)(2,1)S(1)}, bf16[2,272,256]{2,1,0:T(8,128)(2,1)S(1)}, u32[]{:S(2)}, u32[]{:S(2)}) collective-permute-start(bf16[2,272,256]{2,1,0:T(8,128)(2,1)S(1)} %collective-permute-done.1.refs_2_), channel_id=1, source_target_pairs={{0,32},{1,33},{2,34},{3,35},{4,36},{5,37},{6,38},{7,39},{8,40},{9,... | collective-permute-start | bytes 835592 | tf_op jit(solution)/shard_map/ppermute | solution.py:52
  29.7 1.6 %collective-permute-start.4 = (bf16[2,272,256]{2,1,0:T(8,128)(2,1)S(1)}, bf16[2,272,256]{2,1,0:T(8,128)(2,1)S(1)}, u32[]{:S(2)}, u32[]{:S(2)}) collective-permute-start(bf16[2,272,256]{2,1,0:T(8,128)(2,1)S(1)} %collective-permute-done.refs_1_), channel_id=1, source_target_pairs={{0,32},{1,33},{2,34},{3,35},{4,36},{5,37},{6,38},{7,39},{8,40},{9,... | collective-permute-start | bytes 835592 | tf_op jit(solution)/shard_map/ppermute | solution.py:52
  40.2 8.1 %collective-permute-start.7 = (bf16[8,256,128]{2,1,0:T(8,128)(2,1)S(1)}, bf16[8,256,128]{2,1,0:T(8,128)(2,1)S(1)}, u32[]{:S(2)}, u32[]{:S(2)}) collective-permute-start(bf16[8,256,128]{2,1,0:T(8,128)(2,1)S(1)} %get-tuple-element.11), channel_id=1, source_target_pairs={{0,32},{1,33},{2,34},{3,35},{4,36},{5,37},{6,38},{7,39},{8,40},{9,... | collective-permute-start | bytes 1572872 | tf_op jit(solution)/shard_map/ppermute | solution.py:52
  40.4 25.9 %all-to-all-start.1 = ((bf16[16,128,256]{2,1,0:T(8,128)(2,1)}), bf16[16,128,256]{2,1,0:T(8,128)(2,1)S(1)}, u32[]{:S(2)}, u32[]{:S(2)}) async-start(bf16[16,128,256]{2,1,0:T(8,128)(2,1)} %get-tuple-element.12), calls=%async_computation.1 | async-start | bytes 2097152 | tf_op jit(solution)/shard_map/all_to_all | solution.py:57
  48.6 6.2 %collective-permute-start.8 = (bf16[2,256,128]{2,1,0:T(8,128)(2,1)S(1)}, bf16[2,256,128]{2,1,0:T(8,128)(2,1)S(1)}, u32[]{:S(2)}, u32[]{:S(2)}) collective-permute-start(bf16[2,256,128]{2,1,0:T(8,128)(2,1)S(1)} %get-tuple-element.17), channel_id=1, source_target_pairs={{0,80},{1,81},{2,82},{3,83},{4,84},{5,85},{6,86},{7,87},{8,88},{9,... | collective-permute-start | bytes 393224 | tf_op jit(solution)/shard_map/ppermute | solution.py:44
  48.6 7.5 %collective-permute-start.10 = (bf16[2,256,128]{2,1,0:T(8,128)(2,1)S(1)}, bf16[2,256,128]{2,1,0:T(8,128)(2,1)S(1)}, u32[]{:S(2)}, u32[]{:S(2)}) collective-permute-start(bf16[2,256,128]{2,1,0:T(8,128)(2,1)S(1)} %get-tuple-element.18), channel_id=1, source_target_pairs={{0,64},{1,65},{2,66},{3,67},{4,68},{5,69},{6,70},{7,71},{8,72},{9,... | collective-permute-start | bytes 393224 | tf_op jit(solution)/shard_map/ppermute | solution.py:44
  50.7 7.3 %collective-permute-start.9 = (bf16[2,256,128]{2,1,0:T(8,128)(2,1)S(1)}, bf16[2,256,128]{2,1,0:T(8,128)(2,1)S(1)}, u32[]{:S(2)}, u32[]{:S(2)}) collective-permute-start(bf16[2,256,128]{2,1,0:T(8,128)(2,1)S(1)} %get-tuple-element.19), channel_id=1, source_target_pairs={{0,16},{1,17},{2,18},{3,19},{4,20},{5,21},{6,22},{7,23},{8,24},{9,... | collective-permute-start | bytes 393224 | tf_op jit(solution)/shard_map/ppermute | solution.py:44

commit v4 on v3

--- a/solution.py
+++ b/solution.py
@@ -20,7 +20,8 @@
 STACK = QH * BLOCK
 TILE = 256
 TILE_BLOCKS = TILE // BLOCK
-JOBS = 256
+SLOTS = 40
+JOBS = 128
 TOGETHER = 6
 FAR = 1.0e9
 AXES = ("outer", "inner")
@@ -153,7 +154,7 @@
 def grad_kernel(*refs):
     q_refs = refs[:PIECES]
     (kv_ref, dkv_ref, own_ref, other_ref) = refs[PIECES : PIECES + 4]
-    (qs, rows, dk, dv, dq, ints, ints_s, sem) = refs[PIECES + 4 :]
+    (qs, rows, dk, dv, dq, jobs) = refs[PIECES + 4 :]
     scale = HEAD ** (-0.5)
     half = QBLOCKS // 2
 
@@ -170,6 +171,7 @@
     order = jnp.sum(
         jnp.where(rank == lane, below_number, 0.0), axis=0, keepdims=True
     )
+    order = jnp.broadcast_to(order, (ROWS, ROWS)).T[0:SLOTS]
     below = [
         jnp.sum((key_seg < float(s)).astype(jnp.float32), axis=0, keepdims=True) for s in range(1, 9)
     ]
@@ -205,11 +207,20 @@
     code = jnp.sum(jnp.where(mine, code, 0.0), axis=0, keepdims=True)
     count = done[QBLOCKS - 1 : QBLOCKS]
     code = jnp.where(job[0:1] < count, code, float(KBLOCKS))
-    ints[0:1, :] = code.astype(jnp.int32)
-    ints[1:2, 0:ROWS] = order.astype(jnp.int32)
-    ints[2:3, :] = count.astype(jnp.int32)
-    copy = pltpu.make_async_copy(ints, ints_s, sem)
-    copy.start()
+    query = jnp.floor(code * (1.0 / 64.0))
+    at = code - query * 64.0
+    slot = lax.broadcasted_iota(jnp.int32, (SLOTS, JOBS), 0).astype(jnp.float32)
+    members = [
+        jnp.sum(jnp.where(slot == at + float(i), order, 0.0), axis=0, keepdims=True)
+        for i in range(TILE_BLOCKS)
+    ]
+    members = jnp.concatenate([query, at] + members + [jnp.zeros((2, JOBS), jnp.float32)], axis=0)
+    pad = jnp.zeros((JOBS - 8, JOBS), jnp.float32)
+    jobs[0:JOBS, :] = jnp.concatenate([members, pad], axis=0).T.astype(jnp.int32)
+    jobs[JOBS : JOBS + 16, :] = jnp.where(
+        lax.broadcasted_iota(jnp.int32, (16, ROWS), 1) == 1, KBLOCKS, 0
+    )
+    count = jnp.max(count).astype(jnp.int32)
 
     for qi in range(QBLOCKS):
         stat, begin = stats[qi]
@@ -221,17 +232,13 @@
     dk[...] = jnp.zeros_like(dk)
     dv[...] = jnp.zeros_like(dv)
     dq[...] = jnp.zeros_like(dq)
-    copy.wait()
-
-    count = ints_s[2, 0]
+
     down = lax.broadcasted_iota(jnp.int32, (TILE, ROWS), 0).astype(jnp.float32)
     nt = (((1,), (1,)), ((), ()))
     tn = (((0,), (0,)), ((), ()))
 
-    def products(job):
-        qi = jnp.right_shift(job, 6)
-        at = jnp.bitwise_and(job, 63)
-        blocks = [ints_s[1, at + i] for i in range(TILE_BLOCKS)]
+    def products(record):
+        qi, at, blocks = record[0], record[1], record[2:]
         kv = jnp.concatenate(
             [
                 kv_ref[
@@ -259,17 +266,22 @@
         dq_part = lax.dot_general(k, ds, tn, preferred_element_type=jnp.float32)
         return qi, blocks, dq_part, dk_part, dv_part
 
+    def records(step):
+        found = jobs[pl.ds(step * TOGETHER, 8), :]
+        return [[found[i, r] for r in range(2 + TILE_BLOCKS)] for i in range(TOGETHER)]
+
     def jobs_step(step, carry):
-        done = [products(ints_s[0, step * TOGETHER + i]) for i in range(TOGETHER)]
+        later = records(step + 1)
+        done = [products(record) for record in carry]
         for qi, blocks, dq_part, dk_part, dv_part in done:
             dq[qi] += dq_part
             for i, j in enumerate(blocks):
                 part = slice(i * BLOCK, (i + 1) * BLOCK)
                 dk[j] += dk_part[part]
                 dv[j] += dv_part[part]
-        return carry
-
-    lax.fori_loop(0, lax.div(count + TOGETHER - 1, TOGETHER), jobs_step, 0)
+        return later
+
+    lax.fori_loop(0, lax.div(count + TOGETHER - 1, TOGETHER), jobs_step, records(0))
 
     for j in range(KBLOCKS):
         d, to = j % PLANE, slice((j // PLANE) * BLOCK, (j // PLANE + 1) * BLOCK)
@@ -297,9 +309,7 @@
             pltpu.VMEM((KBLOCKS, BLOCK, HEAD), jnp.float32),
             pltpu.VMEM((KBLOCKS, BLOCK, HEAD), jnp.float32),
             pltpu.VMEM((QBLOCKS, HEAD, STACK), jnp.float32),
-            pltpu.VMEM((8, JOBS), jnp.int32),
-            pltpu.SMEM((8, JOBS), jnp.int32),
-            pltpu.SemaphoreType.DMA,
+            pltpu.VMEM((JOBS + 16, ROWS), jnp.int32),
         ],
         compiler_params=pltpu.CompilerParams(vmem_limit_bytes=49 * 1024 * 1024),
         name="grads",

time: 67.8 us -> 68.4 us (level)
  starting transfers between devices: 24.4 us -> 26 us
  waiting for transfers between devices: 28.5 us -> 27.7 us
    all_to_all x2, waiting for transfers between devices: 7.46 us -> 5.77 us  [over_plane(): lax.all_to_all(array, 'inner', 0, 0, axis_index_groups=groups, tiled=True)]
    ppermute x5, starting transfers between devices: 0.75 us -> 2.3 us  [to_partner(): return lax.ppermute(array, AXES, pairs)]
    ppermute x6, starting transfers between devices: 8.5 us -> 9.51 us  [along_z(): return lax.ppermute(array, AXES, pairs)]
    all_to_all x2, starting transfers between devices: 15.2 us -> 14.2 us  [over_plane(): lax.all_to_all(array, 'inner', 0, 0, axis_index_groups=groups, tiled=True)]
    ppermute x6, waiting for transfers between devices: 19.5 us -> 20.4 us  [along_z(): return lax.ppermute(array, AXES, pairs)]
  transfers between devices with their start and end apart: 13 -> 13, of which waited for: 7 -> 6; matrix products, arithmetic and copies ran while one was open for 2% -> 2% of each run, Pallas kernels for 0% -> 0%
where the time goes in v4:
time: 68.4 us; the launch traced here: 67.5 us
  waiting for transfers between devices  27.7 us (40%)
  starting transfers between devices  26 us (38%)
  Pallas kernels  11.1 us (16%)
  other arithmetic  1.01 us (1%)
  local copies, waits for them, and re-layouts  0.93 us (1%)
  between operations  0.73 us (1%)
    ppermute x6, waiting for transfers between devices, along_z(): return lax.ppermute(array, AXES, pairs)  20.4 us
    all_to_all x2, starting transfers between devices, over_plane(): lax.all_to_all(array, 'inner', 0, 0, axis_index_groups=groups, tiled=True)  14.2 us
    ppermute x6, starting transfers between devices, along_z(): return lax.ppermute(array, AXES, pairs)  9.51 us
    pallas_call x1, Pallas kernels, grads(): pl.pallas_call(grad_kernel, out_shape=(jax.ShapeDtypeStruct((PLANE, ROWS,...  8.53 us
    all_to_all x2, waiting for transfers between devices, over_plane(): lax.all_to_all(array, 'inner', 0, 0, axis_index_groups=groups, tiled=True)  5.77 us
    pallas_call x1, Pallas kernels, pack(): pl.pallas_call(pack_kernel, out_shape=(jax.ShapeDtypeStruct((2, STACK + S...  2.58 us
    ppermute x5, starting transfers between devices, to_partner(): return lax.ppermute(array, AXES, pairs)  2.3 us
    ppermute x5, waiting for transfers between devices, to_partner(): return lax.ppermute(array, AXES, pairs)  1.55 us
  transfers between devices with their start and end apart: 13, of which 6 were waited for; matrix products, arithmetic and copies ran while one was open for 2% of the time, Pallas kernels for 0%

profile of v4, /device:TPU:0, one launch (start us, length us, event | category | flops | bytes accessed | tf_op | source)
XLA Modules:
  0.0 67.5 jit_solution(14925139768309821701)
XLA Ops:
  0.6 2.6 %pack.1 = (bf16[2,272,256]{2,1,0:T(8,128)(2,1)}, bf16[16,144,256]{2,1,0:T(8,128)(2,1)}) custom-call(bf16[128,512]{1,0:T(8,128)(2,1)} %q_hbm.1, bf16[128,512]{1,0:T(8,128)(2,1)} %g_hbm.1, bf16[128,512]{1,0:T(8,128)(2,1)} %o_hbm.1, bf16[128,128]{1,0:T(8,128)(2,1)} %k_hbm.1, bf16[128,128]{1,0:T(8,128)(2,1)} %v_hbm.1, f32[4,128]{1,0:T(4,128)} %bitcast.14, ...), custom_call_target="tpu_custom_call" | custom-call | tf_op jit(solution)/shard_map/pack/pallas_call | solution.py:121
  3.2 0.0 copy-start
  3.2 7.3 %all-to-all-start = ((bf16[16,144,256]{2,1,0:T(8,128)(2,1)}), bf16[16,144,256]{2,1,0:T(8,128)(2,1)}, u32[]{:S(2)}, u32[]{:S(2)}) async-start(bf16[16,144,256]{2,1,0:T(8,128)(2,1)} %get-tuple-element.9), calls=%async_computation | async-start | bytes 2359296 | tf_op jit(solution)/shard_map/all_to_all | solution.py:58
  10.5 0.0 copy-done
  10.6 4.1 %collective-permute-start.2 = (bf16[2,272,256]{2,1,0:T(8,128)(2,1)S(1)}, bf16[2,272,256]{2,1,0:T(8,128)(2,1)S(1)}, u32[]{:S(2)}, u32[]{:S(2)}) collective-permute-start(bf16[2,272,256]{2,1,0:T(8,128)(2,1)S(1)} %copy-done), channel_id=1, source_target_pairs={{0,80},{1,81},{2,82},{3,83},{4,84},{5,85},{6,86},{7,87},{8,88},{9,... | collective-permute-start | bytes 835592 | tf_op jit(solution)/shard_map/ppermute | solution.py:45
  14.7 0.0 collective-permute-start.1
  14.7 1.3 %collective-permute-start = (bf16[2,272,256]{2,1,0:T(8,128)(2,1)S(1)}, bf16[2,272,256]{2,1,0:T(8,128)(2,1)S(1)}, u32[]{:S(2)}, u32[]{:S(2)}) collective-permute-start(bf16[2,272,256]{2,1,0:T(8,128)(2,1)S(1)} %copy-done), channel_id=1, source_target_pairs={{0,64},{1,65},{2,66},{3,67},{4,68},{5,69},{6,70},{7,71},{8,72},{9,... | collective-permute-start | bytes 835592 | tf_op jit(solution)/shard_map/ppermute | solution.py:45
  15.9 0.0 collective-permute-start.3
  15.9 10.3 %collective-permute-done.2.refs_3_ = bf16[2,272,256]{2,1,0:T(8,128)(2,1)S(1)} collective-permute-done((bf16[2,272,256]{2,1,0:T(8,128)(2,1)S(1)}, bf16[2,272,256]{2,1,0:T(8,128)(2,1)S(1)}, u32[]{:S(2)}, u32[]{:S(2)}) %collective-permute-start.2) | collective-permute-done | bytes 278560 | tf_op jit(solution)/shard_map/ppermute | solution.py:45
  26.3 0.0 collective-permute-start.6
  26.3 0.0 collective-permute-done.1.refs_2_
  26.3 0.5 collective-permute-start.5
  26.8 2.9 %collective-permute-done.refs_1_ = bf16[2,272,256]{2,1,0:T(8,128)(2,1)S(1)} collective-permute-done((bf16[2,272,256]{2,1,0:T(8,128)(2,1)S(1)}, bf16[2,272,256]{2,1,0:T(8,128)(2,1)S(1)}, u32[]{:S(2)}, u32[]{:S(2)}) %collective-permute-start) | collective-permute-done | bytes 278560 | tf_op jit(solution)/shard_map/ppermute | solution.py:45
  29.7 0.0 collective-permute-start.4
  29.7 0.0 collective-permute-done.3.refs_4_
  29.7 0.0 collective-permute-done.6.refs_7_
  29.7 0.0 collective-permute-done.5.refs_6_
  29.7 1.5 %collective-permute-done.4.refs_5_ = bf16[2,272,256]{2,1,0:T(8,128)(2,1)S(1)} collective-permute-done((bf16[2,272,256]{2,1,0:T(8,128)(2,1)S(1)}, bf16[2,272,256]{2,1,0:T(8,128)(2,1)S(1)}, u32[]{:S(2)}, u32[]{:S(2)}) %collective-permute-start.4) | collective-permute-done | bytes 278560 | tf_op jit(solution)/shard_map/ppermute | solution.py:53
  31.2 0.0 all-to-all-done.refs_8_
  31.2 8.5 %grads.1 = (bf16[16,128,256]{2,1,0:T(8,128)(2,1)}, bf16[8,256,128]{2,1,0:T(8,128)(2,1)S(1)}, bf16[8,256,128]{2,1,0:T(8,128)(2,1)S(1)}) custom-call(bf16[2,272,256]{2,1,0:T(8,128)(2,1)S(1)} %copy-done, bf16[2,272,256]{2,1,0:T(8,128)(2,1)S(1)} %collective-permute-done.refs_1_, bf16[2,272,256]{2,1,0:T(8,128)(2,1)S(1)} %collective-permute-done.1.refs_2_, ...), custom_call_target="tpu_custom_call" | custom-call | tf_op jit(solution)/shard_map/grads/pallas_call | solution.py:297
  39.8 1.8 %collective-permute-start.7 = (bf16[8,256,128]{2,1,0:T(8,128)(2,1)S(1)}, bf16[8,256,128]{2,1,0:T(8,128)(2,1)S(1)}, u32[]{:S(2)}, u32[]{:S(2)}) collective-permute-start(bf16[8,256,128]{2,1,0:T(8,128)(2,1)S(1)} %get-tuple-element.11), channel_id=1, source_target_pairs={{0,32},{1,33},{2,34},{3,35},{4,36},{5,37},{6,38},{7,39},{8,40},{9,... | collective-permute-start | bytes 1572872 | tf_op jit(solution)/shard_map/ppermute | solution.py:53
  41.6 6.9 %all-to-all-start.1 = ((bf16[16,128,256]{2,1,0:T(8,128)(2,1)}), bf16[16,128,256]{2,1,0:T(8,128)(2,1)S(1)}, u32[]{:S(2)}, u32[]{:S(2)}) async-start(bf16[16,128,256]{2,1,0:T(8,128)(2,1)} %get-tuple-element.12), calls=%async_computation.1 | async-start | bytes 2097152 | tf_op jit(solution)/shard_map/all_to_all | solution.py:58
  48.5 0.0 collective-permute-done.7
  48.5 0.2 fusion.2
  48.7 2.5 %collective-permute-start.8 = (bf16[2,256,128]{2,1,0:T(8,128)(2,1)S(1)}, bf16[2,256,128]{2,1,0:T(8,128)(2,1)S(1)}, u32[]{:S(2)}, u32[]{:S(2)}) collective-permute-start(bf16[2,256,128]{2,1,0:T(8,128)(2,1)S(1)} %get-tuple-element.17), channel_id=1, source_target_pairs={{0,80},{1,81},{2,82},{3,83},{4,84},{5,85},{6,86},{7,87},{8,88},{9,... | collective-permute-start | bytes 393224 | tf_op jit(solution)/shard_map/ppermute | solution.py:45
  51.1 0.0 collective-permute-start.10
  51.1 1.7 %collective-permute-start.9 = (bf16[2,256,128]{2,1,0:T(8,128)(2,1)S(1)}, bf16[2,256,128]{2,1,0:T(8,128)(2,1)S(1)}, u32[]{:S(2)}, u32[]{:S(2)}) collective-permute-start(bf16[2,256,128]{2,1,0:T(8,128)(2,1)S(1)} %get-tuple-element.19), channel_id=1, source_target_pairs={{0,16},{1,17},{2,18},{3,19},{4,20},{5,21},{6,22},{7,23},{8,24},{9,... | collective-permute-start | bytes 393224 | tf_op jit(solution)/shard_map/ppermute | solution.py:45
  52.8 1.4 %collective-permute-done.8 = bf16[2,256,128]{2,1,0:T(8,128)(2,1)S(1)} collective-permute-done((bf16[2,256,128]{2,1,0:T(8,128)(2,1)S(1)}, bf16[2,256,128]{2,1,0:T(8,128)(2,1)S(1)}, u32[]{:S(2)}, u32[]{:S(2)}) %collective-permute-start.8) | collective-permute-done | bytes 131104 | tf_op jit(solution)/shard_map/ppermute | solution.py:45
  54.2 5.8 %collective-permute-done.10 = bf16[2,256,128]{2,1,0:T(8,128)(2,1)S(1)} collective-permute-done((bf16[2,256,128]{2,1,0:T(8,128)(2,1)S(1)}, bf16[2,256,128]{2,1,0:T(8,128)(2,1)S(1)}, u32[]{:S(2)}, u32[]{:S(2)}) %collective-permute-start.10) | collective-permute-done | bytes 131104 | tf_op jit(solution)/shard_map/ppermute | solution.py:45
  60.0 0.0 collective-permute-done.9
  60.0 0.1 fusion.1
  60.1 0.2 copy.11
  60.3 0.7 %copy.14 = f32[16,8,4,128]{3,1,2,0:T(8,128)} copy(f32[16,8,4,128]{3,2,1,0:T(4,128)S(1)} %bitcast.12) | data formatting | bytes 524288
  61.0 5.8 %all-to-all-done.1 = bf16[16,128,256]{2,1,0:T(8,128)(2,1)S(1)} async-done(((bf16[16,128,256]{2,1,0:T(8,128)(2,1)}), bf16[16,128,256]{2,1,0:T(8,128)(2,1)S(1)}, u32[]{:S(2)}, u32[]{:S(2)}) %all-to-all-start.1) | async-done | bytes 1048608 | tf_op jit(solution)/shard_map/all_to_all | solution.py:58
  66.7 0.8 %convert_reduce_fusion = (f32[128,128]{1,0:T(8,128)}, f32[128,128]{1,0:T(8,128)}) fusion(bf16[16,128,256]{2,1,0:T(8,128)(2,1)S(1)} %all-to-all-done.1), kind=kLoop, calls=%fused_computation | loop fusion | flops 1015808 | bytes 1179648 | tf_op jit(solution)/shard_map/reduce_sum | solution.py:334
  (1 shorter events, 0.0 us)
Async XLA Ops:
  3.2 7.3 %copy-start = (bf16[2,272,256]{2,1,0:T(8,128)(2,1)S(1)}, bf16[2,272,256]{2,1,0:T(8,128)(2,1)}, u32[]{:S(2)}) copy-start(bf16[2,272,256]{2,1,0:T(8,128)(2,1)} %get-tuple-element.8.refs_0_) | copy-start | bytes 835588
  3.2 28.0 %all-to-all-start = ((bf16[16,144,256]{2,1,0:T(8,128)(2,1)}), bf16[16,144,256]{2,1,0:T(8,128)(2,1)}, u32[]{:S(2)}, u32[]{:S(2)}) async-start(bf16[16,144,256]{2,1,0:T(8,128)(2,1)} %get-tuple-element.9), calls=%async_computation | async-start | bytes 2359296 | tf_op jit(solution)/shard_map/all_to_all | solution.py:58
  10.6 15.7 %collective-permute-start.2 = (bf16[2,272,256]{2,1,0:T(8,128)(2,1)S(1)}, bf16[2,272,256]{2,1,0:T(8,128)(2,1)S(1)}, u32[]{:S(2)}, u32[]{:S(2)}) collective-permute-start(bf16[2,272,256]{2,1,0:T(8,128)(2,1)S(1)} %copy-done), channel_id=1, source_target_pairs={{0,80},{1,81},{2,82},{3,83},{4,84},{5,85},{6,86},{7,87},{8,88},{9,... | collective-permute-start | bytes 835592 | tf_op jit(solution)/shard_map/ppermute | solution.py:45
  14.7 11.6 %collective-permute-start.1 = (bf16[2,272,256]{2,1,0:T(8,128)(2,1)S(1)}, bf16[2,272,256]{2,1,0:T(8,128)(2,1)S(1)}, u32[]{:S(2)}, u32[]{:S(2)}) collective-permute-start(bf16[2,272,256]{2,1,0:T(8,128)(2,1)S(1)} %copy-done), channel_id=1, source_target_pairs={{0,16},{1,17},{2,18},{3,19},{4,20},{5,21},{6,22},{7,23},{8,24},{9,... | collective-permute-start | bytes 835592 | tf_op jit(solution)/shard_map/ppermute | solution.py:45
  14.7 15.0 %collective-permute-start = (bf16[2,272,256]{2,1,0:T(8,128)(2,1)S(1)}, bf16[2,272,256]{2,1,0:T(8,128)(2,1)S(1)}, u32[]{:S(2)}, u32[]{:S(2)}) collective-permute-start(bf16[2,272,256]{2,1,0:T(8,128)(2,1)S(1)} %copy-done), channel_id=1, source_target_pairs={{0,64},{1,65},{2,66},{3,67},{4,68},{5,69},{6,70},{7,71},{8,72},{9,... | collective-permute-start | bytes 835592 | tf_op jit(solution)/shard_map/ppermute | solution.py:45
  15.9 13.8 %collective-permute-start.3 = (bf16[2,272,256]{2,1,0:T(8,128)(2,1)S(1)}, bf16[2,272,256]{2,1,0:T(8,128)(2,1)S(1)}, u32[]{:S(2)}, u32[]{:S(2)}) collective-permute-start(bf16[2,272,256]{2,1,0:T(8,128)(2,1)S(1)} %copy-done), channel_id=1, source_target_pairs={{0,32},{1,33},{2,34},{3,35},{4,36},{5,37},{6,38},{7,39},{8,40},{9,... | collective-permute-start | bytes 835592 | tf_op jit(solution)/shard_map/ppermute | solution.py:53
  26.3 3.4 %collective-permute-start.6 = (bf16[2,272,256]{2,1,0:T(8,128)(2,1)S(1)}, bf16[2,272,256]{2,1,0:T(8,128)(2,1)S(1)}, u32[]{:S(2)}, u32[]{:S(2)}) collective-permute-start(bf16[2,272,256]{2,1,0:T(8,128)(2,1)S(1)} %collective-permute-done.2.refs_3_), channel_id=1, source_target_pairs={{0,32},{1,33},{2,34},{3,35},{4,36},{5,37},{6,38},{7,39},{8,40},{9,... | collective-permute-start | bytes 835592 | tf_op jit(solution)/shard_map/ppermute | solution.py:53
  26.3 3.4 %collective-permute-start.5 = (bf16[2,272,256]{2,1,0:T(8,128)(2,1)S(1)}, bf16[2,272,256]{2,1,0:T(8,128)(2,1)S(1)}, u32[]{:S(2)}, u32[]{:S(2)}) collective-permute-start(bf16[2,272,256]{2,1,0:T(8,128)(2,1)S(1)} %collective-permute-done.1.refs_2_), channel_id=1, source_target_pairs={{0,32},{1,33},{2,34},{3,35},{4,36},{5,37},{6,38},{7,39},{8,40},{9,... | collective-permute-start | bytes 835592 | tf_op jit(solution)/shard_map/ppermute | solution.py:53
  29.7 1.6 %collective-permute-start.4 = (bf16[2,272,256]{2,1,0:T(8,128)(2,1)S(1)}, bf16[2,272,256]{2,1,0:T(8,128)(2,1)S(1)}, u32[]{:S(2)}, u32[]{:S(2)}) collective-permute-start(bf16[2,272,256]{2,1,0:T(8,128)(2,1)S(1)} %collective-permute-done.refs_1_), channel_id=1, source_target_pairs={{0,32},{1,33},{2,34},{3,35},{4,36},{5,37},{6,38},{7,39},{8,40},{9,... | collective-permute-start | bytes 835592 | tf_op jit(solution)/shard_map/ppermute | solution.py:53
  39.8 8.7 %collective-permute-start.7 = (bf16[8,256,128]{2,1,0:T(8,128)(2,1)S(1)}, bf16[8,256,128]{2,1,0:T(8,128)(2,1)S(1)}, u32[]{:S(2)}, u32[]{:S(2)}) collective-permute-start(bf16[8,256,128]{2,1,0:T(8,128)(2,1)S(1)} %get-tuple-element.11), channel_id=1, source_target_pairs={{0,32},{1,33},{2,34},{3,35},{4,36},{5,37},{6,38},{7,39},{8,40},{9,... | collective-permute-start | bytes 1572872 | tf_op jit(solution)/shard_map/ppermute | solution.py:53
  41.6 25.2 %all-to-all-start.1 = ((bf16[16,128,256]{2,1,0:T(8,128)(2,1)}), bf16[16,128,256]{2,1,0:T(8,128)(2,1)S(1)}, u32[]{:S(2)}, u32[]{:S(2)}) async-start(bf16[16,128,256]{2,1,0:T(8,128)(2,1)} %get-tuple-element.12), calls=%async_computation.1 | async-start | bytes 2097152 | tf_op jit(solution)/shard_map/all_to_all | solution.py:58
  48.7 5.5 %collective-permute-start.8 = (bf16[2,256,128]{2,1,0:T(8,128)(2,1)S(1)}, bf16[2,256,128]{2,1,0:T(8,128)(2,1)S(1)}, u32[]{:S(2)}, u32[]{:S(2)}) collective-permute-start(bf16[2,256,128]{2,1,0:T(8,128)(2,1)S(1)} %get-tuple-element.17), channel_id=1, source_target_pairs={{0,80},{1,81},{2,82},{3,83},{4,84},{5,85},{6,86},{7,87},{8,88},{9,... | collective-permute-start | bytes 393224 | tf_op jit(solution)/shard_map/ppermute | solution.py:45
  51.1 8.9 %collective-permute-start.10 = (bf16[2,256,128]{2,1,0:T(8,128)(2,1)S(1)}, bf16[2,256,128]{2,1,0:T(8,128)(2,1)S(1)}, u32[]{:S(2)}, u32[]{:S(2)}) collective-permute-start(bf16[2,256,128]{2,1,0:T(8,128)(2,1)S(1)} %get-tuple-element.18), channel_id=1, source_target_pairs={{0,64},{1,65},{2,66},{3,67},{4,68},{5,69},{6,70},{7,71},{8,72},{9,... | collective-permute-start | bytes 393224 | tf_op jit(solution)/shard_map/ppermute | solution.py:45
  51.1 8.9 %collective-permute-start.9 = (bf16[2,256,128]{2,1,0:T(8,128)(2,1)S(1)}, bf16[2,256,128]{2,1,0:T(8,128)(2,1)S(1)}, u32[]{:S(2)}, u32[]{:S(2)}) collective-permute-start(bf16[2,256,128]{2,1,0:T(8,128)(2,1)S(1)} %get-tuple-element.19), channel_id=1, source_target_pairs={{0,16},{1,17},{2,18},{3,19},{4,20},{5,21},{6,22},{7,23},{8,24},{9,... | collective-permute-start | bytes 393224 | tf_op jit(solution)/shard_map/ppermute | solution.py:45

commit v5 on v4

--- a/solution.py
+++ b/solution.py
@@ -154,7 +154,7 @@
 def grad_kernel(*refs):
     q_refs = refs[:PIECES]
     (kv_ref, dkv_ref, own_ref, other_ref) = refs[PIECES : PIECES + 4]
-    (qs, rows, dk, dv, dq, jobs) = refs[PIECES + 4 :]
+    (qs, rows, dk, dv, dq, jobs, stage, sems) = refs[PIECES + 4 :]
     scale = HEAD ** (-0.5)
     half = QBLOCKS // 2
 
@@ -283,13 +283,17 @@
 
     lax.fori_loop(0, lax.div(count + TOGETHER - 1, TOGETHER), jobs_step, records(0))
 
-    for j in range(KBLOCKS):
-        d, to = j % PLANE, slice((j // PLANE) * BLOCK, (j // PLANE + 1) * BLOCK)
-        dkv_ref[d, to, 0:HEAD] = dk[j].astype(jnp.bfloat16)
-        dkv_ref[d, to, HEAD : 2 * HEAD] = dv[j].astype(jnp.bfloat16)
+    for d in range(PLANE):
+        for b in range(2):
+            to = slice(b * BLOCK, (b + 1) * BLOCK)
+            stage[d, to, 0:HEAD] = dk[b * PLANE + d].astype(jnp.bfloat16)
+            stage[d, to, HEAD : 2 * HEAD] = dv[b * PLANE + d].astype(jnp.bfloat16)
+        pltpu.make_async_copy(stage.at[d], dkv_ref.at[d], sems.at[d]).start()
     for qi in range(half):
         own_ref[qi] = dq[qi].astype(jnp.bfloat16).T
         other_ref[qi] = dq[half + qi].astype(jnp.bfloat16).T
+    for d in range(PLANE):
+        pltpu.make_async_copy(stage.at[d], dkv_ref.at[d], sems.at[d]).wait()
 
 
 def grads(pieces, kv):
@@ -302,7 +306,8 @@
             jax.ShapeDtypeStruct((half, STACK, HEAD), jnp.bfloat16),
         ),
         in_specs=[pl.BlockSpec(memory_space=pltpu.VMEM)] * (PIECES + 1),
-        out_specs=(pl.BlockSpec(memory_space=pltpu.VMEM),) * 3,
+        out_specs=(pl.BlockSpec(memory_space=pl.ANY),)
+        + (pl.BlockSpec(memory_space=pltpu.VMEM),) * 2,
         scratch_shapes=[
             pltpu.VMEM((QBLOCKS, STACK, 2 * HEAD), jnp.bfloat16),
             pltpu.VMEM((QBLOCKS, 8, STACK), jnp.float32),
@@ -310,6 +315,8 @@
             pltpu.VMEM((KBLOCKS, BLOCK, HEAD), jnp.float32),
             pltpu.VMEM((QBLOCKS, HEAD, STACK), jnp.float32),
             pltpu.VMEM((JOBS + 16, ROWS), jnp.int32),
+            pltpu.VMEM((PLANE, ROWS, 2 * HEAD), jnp.bfloat16),
+            pltpu.SemaphoreType.DMA((PLANE,)),
         ],
         compiler_params=pltpu.CompilerParams(vmem_limit_bytes=49 * 1024 * 1024),
         name="grads",

time: 68.4 us -> 69.5 us (1.016)
  starting transfers between devices: 26 us -> 23.6 us
  waiting for transfers between devices: 27.7 us -> 30 us
  Pallas kernels: 11.1 us -> 12.7 us
    ppermute x6, starting transfers between devices: 9.51 us -> 7.46 us  [along_z(): return lax.ppermute(array, AXES, pairs)]
    all_to_all x2, waiting for transfers between devices: 5.77 us -> 7.49 us  [over_plane(): lax.all_to_all(array, 'inner', 0, 0, axis_index_groups=groups, tiled=True)]
    ppermute x5, starting transfers between devices: 2.3 us -> 0.6 us  [to_partner(): return lax.ppermute(array, AXES, pairs)]
    pallas_call x1, Pallas kernels: 8.53 us -> 10.1 us  [grads(): pl.pallas_call(grad_kernel, out_shape=(jax.ShapeDtypeStruct((PLANE, ROWS,...]
    all_to_all x2, starting transfers between devices: 14.2 us -> 15.6 us  [over_plane(): lax.all_to_all(array, 'inner', 0, 0, axis_index_groups=groups, tiled=True)]
where the time goes in v5:
time: 69.5 us; the launch traced here: 69 us
  waiting for transfers between devices  30 us (43%)
  starting transfers between devices  23.6 us (34%)
  Pallas kernels  12.7 us (18%)
  other arithmetic  1.01 us (1%)
  local copies, waits for them, and re-layouts  0.93 us (1%)
  between operations  0.75 us (1%)
    ppermute x6, waiting for transfers between devices, along_z(): return lax.ppermute(array, AXES, pairs)  20.9 us
    all_to_all x2, starting transfers between devices, over_plane(): lax.all_to_all(array, 'inner', 0, 0, axis_index_groups=groups, tiled=True)  15.6 us
    pallas_call x1, Pallas kernels, grads(): pl.pallas_call(grad_kernel, out_shape=(jax.ShapeDtypeStruct((PLANE, ROWS,...  10.1 us
    all_to_all x2, waiting for transfers between devices, over_plane(): lax.all_to_all(array, 'inner', 0, 0, axis_index_groups=groups, tiled=True)  7.49 us
    ppermute x6, starting transfers between devices, along_z(): return lax.ppermute(array, AXES, pairs)  7.46 us
    pallas_call x1, Pallas kernels, pack(): pl.pallas_call(pack_kernel, out_shape=(jax.ShapeDtypeStruct((2, STACK + S...  2.58 us
    ppermute x5, waiting for transfers between devices, to_partner(): return lax.ppermute(array, AXES, pairs)  1.55 us
  transfers between devices with their start and end apart: 13, of which 6 were waited for; matrix products, arithmetic and copies ran while one was open for 2% of the time, Pallas kernels for 0%

profile of v5, /device:TPU:0, one launch (start us, length us, event | category | flops | bytes accessed | tf_op | source)
XLA Modules:
  0.0 69.0 jit_solution(9361258953678091288)
XLA Ops:
  0.6 2.6 %pack.1 = (bf16[2,272,256]{2,1,0:T(8,128)(2,1)}, bf16[16,144,256]{2,1,0:T(8,128)(2,1)}) custom-call(bf16[128,512]{1,0:T(8,128)(2,1)} %q_hbm.1, bf16[128,512]{1,0:T(8,128)(2,1)} %g_hbm.1, bf16[128,512]{1,0:T(8,128)(2,1)} %o_hbm.1, bf16[128,128]{1,0:T(8,128)(2,1)} %k_hbm.1, bf16[128,128]{1,0:T(8,128)(2,1)} %v_hbm.1, f32[4,128]{1,0:T(4,128)} %bitcast.14, ...), custom_call_target="tpu_custom_call" | custom-call | tf_op jit(solution)/shard_map/pack/pallas_call | solution.py:121
  3.2 0.0 copy-start
  3.2 7.3 %all-to-all-start = ((bf16[16,144,256]{2,1,0:T(8,128)(2,1)}), bf16[16,144,256]{2,1,0:T(8,128)(2,1)}, u32[]{:S(2)}, u32[]{:S(2)}) async-start(bf16[16,144,256]{2,1,0:T(8,128)(2,1)} %get-tuple-element.9), calls=%async_computation | async-start | bytes 2359296 | tf_op jit(solution)/shard_map/all_to_all | solution.py:58
  10.5 0.0 copy-done
  10.6 4.1 %collective-permute-start.2 = (bf16[2,272,256]{2,1,0:T(8,128)(2,1)S(1)}, bf16[2,272,256]{2,1,0:T(8,128)(2,1)S(1)}, u32[]{:S(2)}, u32[]{:S(2)}) collective-permute-start(bf16[2,272,256]{2,1,0:T(8,128)(2,1)S(1)} %copy-done), channel_id=1, source_target_pairs={{0,80},{1,81},{2,82},{3,83},{4,84},{5,85},{6,86},{7,87},{8,88},{9,... | collective-permute-start | bytes 835592 | tf_op jit(solution)/shard_map/ppermute | solution.py:45
  14.7 0.0 collective-permute-start.1
  14.7 1.3 %collective-permute-start = (bf16[2,272,256]{2,1,0:T(8,128)(2,1)S(1)}, bf16[2,272,256]{2,1,0:T(8,128)(2,1)S(1)}, u32[]{:S(2)}, u32[]{:S(2)}) collective-permute-start(bf16[2,272,256]{2,1,0:T(8,128)(2,1)S(1)} %copy-done), channel_id=1, source_target_pairs={{0,64},{1,65},{2,66},{3,67},{4,68},{5,69},{6,70},{7,71},{8,72},{9,... | collective-permute-start | bytes 835592 | tf_op jit(solution)/shard_map/ppermute | solution.py:45
  15.9 0.0 collective-permute-start.3
  15.9 10.3 %collective-permute-done.2.refs_3_ = bf16[2,272,256]{2,1,0:T(8,128)(2,1)S(1)} collective-permute-done((bf16[2,272,256]{2,1,0:T(8,128)(2,1)S(1)}, bf16[2,272,256]{2,1,0:T(8,128)(2,1)S(1)}, u32[]{:S(2)}, u32[]{:S(2)}) %collective-permute-start.2) | collective-permute-done | bytes 278560 | tf_op jit(solution)/shard_map/ppermute | solution.py:45
  26.3 0.0 collective-permute-start.6
  26.3 0.0 collective-permute-done.1.refs_2_
  26.3 0.5 collective-permute-start.5
  26.8 2.9 %collective-permute-done.refs_1_ = bf16[2,272,256]{2,1,0:T(8,128)(2,1)S(1)} collective-permute-done((bf16[2,272,256]{2,1,0:T(8,128)(2,1)S(1)}, bf16[2,272,256]{2,1,0:T(8,128)(2,1)S(1)}, u32[]{:S(2)}, u32[]{:S(2)}) %collective-permute-start) | collective-permute-done | bytes 278560 | tf_op jit(solution)/shard_map/ppermute | solution.py:45
  29.7 0.0 collective-permute-start.4
  29.7 0.0 collective-permute-done.3.refs_4_
  29.7 0.0 collective-permute-done.6.refs_7_
  29.7 0.0 collective-permute-done.5.refs_6_
  29.7 1.5 %collective-permute-done.4.refs_5_ = bf16[2,272,256]{2,1,0:T(8,128)(2,1)S(1)} collective-permute-done((bf16[2,272,256]{2,1,0:T(8,128)(2,1)S(1)}, bf16[2,272,256]{2,1,0:T(8,128)(2,1)S(1)}, u32[]{:S(2)}, u32[]{:S(2)}) %collective-permute-start.4) | collective-permute-done | bytes 278560 | tf_op jit(solution)/shard_map/ppermute | solution.py:53
  31.2 0.0 all-to-all-done.refs_8_
  31.2 10.1 %grads.1 = (bf16[16,128,256]{2,1,0:T(8,128)(2,1)}, bf16[8,256,128]{2,1,0:T(8,128)(2,1)S(1)}, bf16[8,256,128]{2,1,0:T(8,128)(2,1)S(1)}) custom-call(bf16[2,272,256]{2,1,0:T(8,128)(2,1)S(1)} %copy-done, bf16[2,272,256]{2,1,0:T(8,128)(2,1)S(1)} %collective-permute-done.refs_1_, bf16[2,272,256]{2,1,0:T(8,128)(2,1)S(1)} %collective-permute-done.1.refs_2_, ...), custom_call_target="tpu_custom_call" | custom-call | tf_op jit(solution)/shard_map/grads/pallas_call | solution.py:301
  41.4 0.1 collective-permute-start.7
  41.5 8.2 %all-to-all-start.1 = ((bf16[16,128,256]{2,1,0:T(8,128)(2,1)}), bf16[16,128,256]{2,1,0:T(8,128)(2,1)S(1)}, u32[]{:S(2)}, u32[]{:S(2)}) async-start(bf16[16,128,256]{2,1,0:T(8,128)(2,1)} %get-tuple-element.12), calls=%async_computation.1 | async-start | bytes 2097152 | tf_op jit(solution)/shard_map/all_to_all | solution.py:58
  49.7 0.0 collective-permute-done.7
  49.7 0.2 fusion.2
  49.9 0.1 collective-permute-start.8
  50.0 2.0 %collective-permute-start.10 = (bf16[2,256,128]{2,1,0:T(8,128)(2,1)S(1)}, bf16[2,256,128]{2,1,0:T(8,128)(2,1)S(1)}, u32[]{:S(2)}, u32[]{:S(2)}) collective-permute-start(bf16[2,256,128]{2,1,0:T(8,128)(2,1)S(1)} %get-tuple-element.18), channel_id=1, source_target_pairs={{0,64},{1,65},{2,66},{3,67},{4,68},{5,69},{6,70},{7,71},{8,72},{9,... | collective-permute-start | bytes 393224 | tf_op jit(solution)/shard_map/ppermute | solution.py:45
  52.0 0.0 collective-permute-start.9
  52.0 4.3 %collective-permute-done.8 = bf16[2,256,128]{2,1,0:T(8,128)(2,1)S(1)} collective-permute-done((bf16[2,256,128]{2,1,0:T(8,128)(2,1)S(1)}, bf16[2,256,128]{2,1,0:T(8,128)(2,1)S(1)}, u32[]{:S(2)}, u32[]{:S(2)}) %collective-permute-start.8) | collective-permute-done | bytes 131104 | tf_op jit(solution)/shard_map/ppermute | solution.py:45
  56.4 3.4 %collective-permute-done.10 = bf16[2,256,128]{2,1,0:T(8,128)(2,1)S(1)} collective-permute-done((bf16[2,256,128]{2,1,0:T(8,128)(2,1)S(1)}, bf16[2,256,128]{2,1,0:T(8,128)(2,1)S(1)}, u32[]{:S(2)}, u32[]{:S(2)}) %collective-permute-start.10) | collective-permute-done | bytes 131104 | tf_op jit(solution)/shard_map/ppermute | solution.py:45
  59.7 0.0 collective-permute-done.9
  59.7 0.1 fusion.1
  59.8 0.2 copy.11
  60.0 0.7 %copy.14 = f32[16,8,4,128]{3,1,2,0:T(8,128)} copy(f32[16,8,4,128]{3,2,1,0:T(4,128)S(1)} %bitcast.12) | data formatting | bytes 524288
  60.7 7.5 %all-to-all-done.1 = bf16[16,128,256]{2,1,0:T(8,128)(2,1)S(1)} async-done(((bf16[16,128,256]{2,1,0:T(8,128)(2,1)}), bf16[16,128,256]{2,1,0:T(8,128)(2,1)S(1)}, u32[]{:S(2)}, u32[]{:S(2)}) %all-to-all-start.1) | async-done | bytes 1048608 | tf_op jit(solution)/shard_map/all_to_all | solution.py:58
  68.2 0.8 %convert_reduce_fusion = (f32[128,128]{1,0:T(8,128)}, f32[128,128]{1,0:T(8,128)}) fusion(bf16[16,128,256]{2,1,0:T(8,128)(2,1)S(1)} %all-to-all-done.1), kind=kLoop, calls=%fused_computation | loop fusion | flops 1015808 | bytes 1179648 | tf_op jit(solution)/shard_map/reduce_sum | solution.py:341
  (1 shorter events, 0.0 us)
Async XLA Ops:
  3.2 7.3 %copy-start = (bf16[2,272,256]{2,1,0:T(8,128)(2,1)S(1)}, bf16[2,272,256]{2,1,0:T(8,128)(2,1)}, u32[]{:S(2)}) copy-start(bf16[2,272,256]{2,1,0:T(8,128)(2,1)} %get-tuple-element.8.refs_0_) | copy-start | bytes 835588
  3.2 28.0 %all-to-all-start = ((bf16[16,144,256]{2,1,0:T(8,128)(2,1)}), bf16[16,144,256]{2,1,0:T(8,128)(2,1)}, u32[]{:S(2)}, u32[]{:S(2)}) async-start(bf16[16,144,256]{2,1,0:T(8,128)(2,1)} %get-tuple-element.9), calls=%async_computation | async-start | bytes 2359296 | tf_op jit(solution)/shard_map/all_to_all | solution.py:58
  10.6 15.7 %collective-permute-start.2 = (bf16[2,272,256]{2,1,0:T(8,128)(2,1)S(1)}, bf16[2,272,256]{2,1,0:T(8,128)(2,1)S(1)}, u32[]{:S(2)}, u32[]{:S(2)}) collective-permute-start(bf16[2,272,256]{2,1,0:T(8,128)(2,1)S(1)} %copy-done), channel_id=1, source_target_pairs={{0,80},{1,81},{2,82},{3,83},{4,84},{5,85},{6,86},{7,87},{8,88},{9,... | collective-permute-start | bytes 835592 | tf_op jit(solution)/shard_map/ppermute | solution.py:45
  14.7 11.6 %collective-permute-start.1 = (bf16[2,272,256]{2,1,0:T(8,128)(2,1)S(1)}, bf16[2,272,256]{2,1,0:T(8,128)(2,1)S(1)}, u32[]{:S(2)}, u32[]{:S(2)}) collective-permute-start(bf16[2,272,256]{2,1,0:T(8,128)(2,1)S(1)} %copy-done), channel_id=1, source_target_pairs={{0,16},{1,17},{2,18},{3,19},{4,20},{5,21},{6,22},{7,23},{8,24},{9,... | collective-permute-start | bytes 835592 | tf_op jit(solution)/shard_map/ppermute | solution.py:45
  14.7 15.0 %collective-permute-start = (bf16[2,272,256]{2,1,0:T(8,128)(2,1)S(1)}, bf16[2,272,256]{2,1,0:T(8,128)(2,1)S(1)}, u32[]{:S(2)}, u32[]{:S(2)}) collective-permute-start(bf16[2,272,256]{2,1,0:T(8,128)(2,1)S(1)} %copy-done), channel_id=1, source_target_pairs={{0,64},{1,65},{2,66},{3,67},{4,68},{5,69},{6,70},{7,71},{8,72},{9,... | collective-permute-start | bytes 835592 | tf_op jit(solution)/shard_map/ppermute | solution.py:45
  15.9 13.8 %collective-permute-start.3 = (bf16[2,272,256]{2,1,0:T(8,128)(2,1)S(1)}, bf16[2,272,256]{2,1,0:T(8,128)(2,1)S(1)}, u32[]{:S(2)}, u32[]{:S(2)}) collective-permute-start(bf16[2,272,256]{2,1,0:T(8,128)(2,1)S(1)} %copy-done), channel_id=1, source_target_pairs={{0,32},{1,33},{2,34},{3,35},{4,36},{5,37},{6,38},{7,39},{8,40},{9,... | collective-permute-start | bytes 835592 | tf_op jit(solution)/shard_map/ppermute | solution.py:53
  26.3 3.4 %collective-permute-start.6 = (bf16[2,272,256]{2,1,0:T(8,128)(2,1)S(1)}, bf16[2,272,256]{2,1,0:T(8,128)(2,1)S(1)}, u32[]{:S(2)}, u32[]{:S(2)}) collective-permute-start(bf16[2,272,256]{2,1,0:T(8,128)(2,1)S(1)} %collective-permute-done.2.refs_3_), channel_id=1, source_target_pairs={{0,32},{1,33},{2,34},{3,35},{4,36},{5,37},{6,38},{7,39},{8,40},{9,... | collective-permute-start | bytes 835592 | tf_op jit(solution)/shard_map/ppermute | solution.py:53
  26.3 3.4 %collective-permute-start.5 = (bf16[2,272,256]{2,1,0:T(8,128)(2,1)S(1)}, bf16[2,272,256]{2,1,0:T(8,128)(2,1)S(1)}, u32[]{:S(2)}, u32[]{:S(2)}) collective-permute-start(bf16[2,272,256]{2,1,0:T(8,128)(2,1)S(1)} %collective-permute-done.1.refs_2_), channel_id=1, source_target_pairs={{0,32},{1,33},{2,34},{3,35},{4,36},{5,37},{6,38},{7,39},{8,40},{9,... | collective-permute-start | bytes 835592 | tf_op jit(solution)/shard_map/ppermute | solution.py:53
  29.7 1.6 %collective-permute-start.4 = (bf16[2,272,256]{2,1,0:T(8,128)(2,1)S(1)}, bf16[2,272,256]{2,1,0:T(8,128)(2,1)S(1)}, u32[]{:S(2)}, u32[]{:S(2)}) collective-permute-start(bf16[2,272,256]{2,1,0:T(8,128)(2,1)S(1)} %collective-permute-done.refs_1_), channel_id=1, source_target_pairs={{0,32},{1,33},{2,34},{3,35},{4,36},{5,37},{6,38},{7,39},{8,40},{9,... | collective-permute-start | bytes 835592 | tf_op jit(solution)/shard_map/ppermute | solution.py:53
  41.4 8.4 %collective-permute-start.7 = (bf16[8,256,128]{2,1,0:T(8,128)(2,1)S(1)}, bf16[8,256,128]{2,1,0:T(8,128)(2,1)S(1)}, u32[]{:S(2)}, u32[]{:S(2)}) collective-permute-start(bf16[8,256,128]{2,1,0:T(8,128)(2,1)S(1)} %get-tuple-element.11), channel_id=1, source_target_pairs={{0,32},{1,33},{2,34},{3,35},{4,36},{5,37},{6,38},{7,39},{8,40},{9,... | collective-permute-start | bytes 1572872 | tf_op jit(solution)/shard_map/ppermute | solution.py:53
  41.5 26.7 %all-to-all-start.1 = ((bf16[16,128,256]{2,1,0:T(8,128)(2,1)}), bf16[16,128,256]{2,1,0:T(8,128)(2,1)S(1)}, u32[]{:S(2)}, u32[]{:S(2)}) async-start(bf16[16,128,256]{2,1,0:T(8,128)(2,1)} %get-tuple-element.12), calls=%async_computation.1 | async-start | bytes 2097152 | tf_op jit(solution)/shard_map/all_to_all | solution.py:58
  49.9 6.4 %collective-permute-start.8 = (bf16[2,256,128]{2,1,0:T(8,128)(2,1)S(1)}, bf16[2,256,128]{2,1,0:T(8,128)(2,1)S(1)}, u32[]{:S(2)}, u32[]{:S(2)}) collective-permute-start(bf16[2,256,128]{2,1,0:T(8,128)(2,1)S(1)} %get-tuple-element.17), channel_id=1, source_target_pairs={{0,80},{1,81},{2,82},{3,83},{4,84},{5,85},{6,86},{7,87},{8,88},{9,... | collective-permute-start | bytes 393224 | tf_op jit(solution)/shard_map/ppermute | solution.py:45
  50.0 9.7 %collective-permute-start.10 = (bf16[2,256,128]{2,1,0:T(8,128)(2,1)S(1)}, bf16[2,256,128]{2,1,0:T(8,128)(2,1)S(1)}, u32[]{:S(2)}, u32[]{:S(2)}) collective-permute-start(bf16[2,256,128]{2,1,0:T(8,128)(2,1)S(1)} %get-tuple-element.18), channel_id=1, source_target_pairs={{0,64},{1,65},{2,66},{3,67},{4,68},{5,69},{6,70},{7,71},{8,72},{9,... | collective-permute-start | bytes 393224 | tf_op jit(solution)/shard_map/ppermute | solution.py:45
  52.0 7.7 %collective-permute-start.9 = (bf16[2,256,128]{2,1,0:T(8,128)(2,1)S(1)}, bf16[2,256,128]{2,1,0:T(8,128)(2,1)S(1)}, u32[]{:S(2)}, u32[]{:S(2)}) collective-permute-start(bf16[2,256,128]{2,1,0:T(8,128)(2,1)S(1)} %get-tuple-element.19), channel_id=1, source_target_pairs={{0,16},{1,17},{2,18},{3,19},{4,20},{5,21},{6,22},{7,23},{8,24},{9,... | collective-permute-start | bytes 393224 | tf_op jit(solution)/shard_map/ppermute | solution.py:45

commit v6 on v5

--- a/solution.py
+++ b/solution.py
@@ -65,7 +65,7 @@
     copies = [pltpu.make_async_copy(s, t, sems.at[i]) for i, (s, t) in enumerate(zip(sources, targets))]
     for copy in copies:
         copy.start()
-    for copy in copies:
+    for copy in copies[:5]:
         copy.wait()
     row = lax.broadcasted_iota(jnp.int32, (8, ROWS), 0)
     lane = lax.broadcasted_iota(jnp.int32, (8, ROWS), 1)
@@ -84,6 +84,10 @@
                 jnp.where(row == 1, dot, jnp.where(row == 2, block, jnp.where(row == 3, seg, 0.0))),
             )
         )
+    for copy in copies[5:]:
+        copy.wait()
+    for h in range(QH):
+        cols = slice(h * HEAD, (h + 1) * HEAD)
         for b in range(2):
             to = slice(h * BLOCK, (h + 1) * BLOCK)
             frm = slice(b * BLOCK, (b + 1) * BLOCK)

time: 69.5 us -> 67.5 us (0.971)
  Pallas kernels: 12.7 us -> 11.1 us
  waiting for transfers between devices: 30 us -> 28.6 us
  starting transfers between devices: 23.6 us -> 24.7 us
    pallas_call x1, Pallas kernels: 10.1 us -> 8.52 us  [grads(): pl.pallas_call(grad_kernel, out_shape=(jax.ShapeDtypeStruct((PLANE, ROWS,...]
    ppermute x6, starting transfers between devices: 7.46 us -> 8.86 us  [along_z(): return lax.ppermute(array, AXES, pairs)]
    all_to_all x2, waiting for transfers between devices: 7.49 us -> 6.43 us  [over_plane(): lax.all_to_all(array, 'inner', 0, 0, axis_index_groups=groups, tiled=True)]
where the time goes in v6:
time: 67.5 us; the launch traced here: 67 us
  waiting for transfers between devices  28.6 us (42%)
  starting transfers between devices  24.7 us (37%)
  Pallas kernels  11.1 us (16%)
  other arithmetic  1.01 us (1%)
  local copies, waits for them, and re-layouts  0.93 us (1%)
  between operations  0.74 us (1%)
    ppermute x6, waiting for transfers between devices, along_z(): return lax.ppermute(array, AXES, pairs)  20.6 us
    all_to_all x2, starting transfers between devices, over_plane(): lax.all_to_all(array, 'inner', 0, 0, axis_index_groups=groups, tiled=True)  15.1 us
    ppermute x6, starting transfers between devices, along_z(): return lax.ppermute(array, AXES, pairs)  8.86 us
    pallas_call x1, Pallas kernels, grads(): pl.pallas_call(grad_kernel, out_shape=(jax.ShapeDtypeStruct((PLANE, ROWS,...  8.52 us
    all_to_all x2, waiting for transfers between devices, over_plane(): lax.all_to_all(array, 'inner', 0, 0, axis_index_groups=groups, tiled=True)  6.43 us
    pallas_call x1, Pallas kernels, pack(): pl.pallas_call(pack_kernel, out_shape=(jax.ShapeDtypeStruct((2, STACK + S...  2.56 us
    ppermute x5, waiting for transfers between devices, to_partner(): return lax.ppermute(array, AXES, pairs)  1.55 us
  transfers between devices with their start and end apart: 13, of which 6 were waited for; matrix products, arithmetic and copies ran while one was open for 2% of the time, Pallas kernels for 0%

profile of v6, /device:TPU:0, one launch (start us, length us, event | category | flops | bytes accessed | tf_op | source)
XLA Modules:
  0.0 67.0 jit_solution(6883572160082308346)
XLA Ops:
  0.6 2.6 %pack.1 = (bf16[2,272,256]{2,1,0:T(8,128)(2,1)}, bf16[16,144,256]{2,1,0:T(8,128)(2,1)}) custom-call(bf16[128,512]{1,0:T(8,128)(2,1)} %q_hbm.1, bf16[128,512]{1,0:T(8,128)(2,1)} %g_hbm.1, bf16[128,512]{1,0:T(8,128)(2,1)} %o_hbm.1, bf16[128,128]{1,0:T(8,128)(2,1)} %k_hbm.1, bf16[128,128]{1,0:T(8,128)(2,1)} %v_hbm.1, f32[4,128]{1,0:T(4,128)} %bitcast.14, ...), custom_call_target="tpu_custom_call" | custom-call | tf_op jit(solution)/shard_map/pack/pallas_call | solution.py:125
  3.2 0.0 copy-start
  3.2 7.3 %all-to-all-start = ((bf16[16,144,256]{2,1,0:T(8,128)(2,1)}), bf16[16,144,256]{2,1,0:T(8,128)(2,1)}, u32[]{:S(2)}, u32[]{:S(2)}) async-start(bf16[16,144,256]{2,1,0:T(8,128)(2,1)} %get-tuple-element.9), calls=%async_computation | async-start | bytes 2359296 | tf_op jit(solution)/shard_map/all_to_all | solution.py:58
  10.5 0.0 copy-done
  10.5 4.1 %collective-permute-start.2 = (bf16[2,272,256]{2,1,0:T(8,128)(2,1)S(1)}, bf16[2,272,256]{2,1,0:T(8,128)(2,1)S(1)}, u32[]{:S(2)}, u32[]{:S(2)}) collective-permute-start(bf16[2,272,256]{2,1,0:T(8,128)(2,1)S(1)} %copy-done), channel_id=1, source_target_pairs={{0,80},{1,81},{2,82},{3,83},{4,84},{5,85},{6,86},{7,87},{8,88},{9,... | collective-permute-start | bytes 835592 | tf_op jit(solution)/shard_map/ppermute | solution.py:45
  14.6 0.0 collective-permute-start.1
  14.6 1.3 %collective-permute-start = (bf16[2,272,256]{2,1,0:T(8,128)(2,1)S(1)}, bf16[2,272,256]{2,1,0:T(8,128)(2,1)S(1)}, u32[]{:S(2)}, u32[]{:S(2)}) collective-permute-start(bf16[2,272,256]{2,1,0:T(8,128)(2,1)S(1)} %copy-done), channel_id=1, source_target_pairs={{0,64},{1,65},{2,66},{3,67},{4,68},{5,69},{6,70},{7,71},{8,72},{9,... | collective-permute-start | bytes 835592 | tf_op jit(solution)/shard_map/ppermute | solution.py:45
  15.9 0.0 collective-permute-start.3
  15.9 10.3 %collective-permute-done.2.refs_3_ = bf16[2,272,256]{2,1,0:T(8,128)(2,1)S(1)} collective-permute-done((bf16[2,272,256]{2,1,0:T(8,128)(2,1)S(1)}, bf16[2,272,256]{2,1,0:T(8,128)(2,1)S(1)}, u32[]{:S(2)}, u32[]{:S(2)}) %collective-permute-start.2) | collective-permute-done | bytes 278560 | tf_op jit(solution)/shard_map/ppermute | solution.py:45
  26.2 0.0 collective-permute-start.6
  26.2 0.0 collective-permute-done.1.refs_2_
  26.3 0.5 collective-permute-start.5
  26.8 2.9 %collective-permute-done.refs_1_ = bf16[2,272,256]{2,1,0:T(8,128)(2,1)S(1)} collective-permute-done((bf16[2,272,256]{2,1,0:T(8,128)(2,1)S(1)}, bf16[2,272,256]{2,1,0:T(8,128)(2,1)S(1)}, u32[]{:S(2)}, u32[]{:S(2)}) %collective-permute-start) | collective-permute-done | bytes 278560 | tf_op jit(solution)/shard_map/ppermute | solution.py:45
  29.7 0.0 collective-permute-start.4
  29.7 0.0 collective-permute-done.3.refs_4_
  29.7 0.0 collective-permute-done.6.refs_7_
  29.7 0.0 collective-permute-done.5.refs_6_
  29.7 1.5 %collective-permute-done.4.refs_5_ = bf16[2,272,256]{2,1,0:T(8,128)(2,1)S(1)} collective-permute-done((bf16[2,272,256]{2,1,0:T(8,128)(2,1)S(1)}, bf16[2,272,256]{2,1,0:T(8,128)(2,1)S(1)}, u32[]{:S(2)}, u32[]{:S(2)}) %collective-permute-start.4) | collective-permute-done | bytes 278560 | tf_op jit(solution)/shard_map/ppermute | solution.py:53
  31.2 0.0 all-to-all-done.refs_8_
  31.2 8.5 %grads.1 = (bf16[16,128,256]{2,1,0:T(8,128)(2,1)}, bf16[8,256,128]{2,1,0:T(8,128)(2,1)S(1)}, bf16[8,256,128]{2,1,0:T(8,128)(2,1)S(1)}) custom-call(bf16[2,272,256]{2,1,0:T(8,128)(2,1)S(1)} %copy-done, bf16[2,272,256]{2,1,0:T(8,128)(2,1)S(1)} %collective-permute-done.refs_1_, bf16[2,272,256]{2,1,0:T(8,128)(2,1)S(1)} %collective-permute-done.1.refs_2_, ...), custom_call_target="tpu_custom_call" | custom-call | tf_op jit(solution)/shard_map/grads/pallas_call | solution.py:305
  39.7 0.2 collective-permute-start.7
  39.9 7.8 %all-to-all-start.1 = ((bf16[16,128,256]{2,1,0:T(8,128)(2,1)}), bf16[16,128,256]{2,1,0:T(8,128)(2,1)S(1)}, u32[]{:S(2)}, u32[]{:S(2)}) async-start(bf16[16,128,256]{2,1,0:T(8,128)(2,1)} %get-tuple-element.12), calls=%async_computation.1 | async-start | bytes 2097152 | tf_op jit(solution)/shard_map/all_to_all | solution.py:58
  47.8 0.0 collective-permute-done.7
  47.8 0.2 fusion.2
  48.0 1.9 %collective-permute-start.8 = (bf16[2,256,128]{2,1,0:T(8,128)(2,1)S(1)}, bf16[2,256,128]{2,1,0:T(8,128)(2,1)S(1)}, u32[]{:S(2)}, u32[]{:S(2)}) collective-permute-start(bf16[2,256,128]{2,1,0:T(8,128)(2,1)S(1)} %get-tuple-element.17), channel_id=1, source_target_pairs={{0,80},{1,81},{2,82},{3,83},{4,84},{5,85},{6,86},{7,87},{8,88},{9,... | collective-permute-start | bytes 393224 | tf_op jit(solution)/shard_map/ppermute | solution.py:45
  49.9 0.1 collective-permute-start.10
  50.1 1.4 %collective-permute-start.9 = (bf16[2,256,128]{2,1,0:T(8,128)(2,1)S(1)}, bf16[2,256,128]{2,1,0:T(8,128)(2,1)S(1)}, u32[]{:S(2)}, u32[]{:S(2)}) collective-permute-start(bf16[2,256,128]{2,1,0:T(8,128)(2,1)S(1)} %get-tuple-element.19), channel_id=1, source_target_pairs={{0,16},{1,17},{2,18},{3,19},{4,20},{5,21},{6,22},{7,23},{8,24},{9,... | collective-permute-start | bytes 393224 | tf_op jit(solution)/shard_map/ppermute | solution.py:45
  51.5 2.2 %collective-permute-done.8 = bf16[2,256,128]{2,1,0:T(8,128)(2,1)S(1)} collective-permute-done((bf16[2,256,128]{2,1,0:T(8,128)(2,1)S(1)}, bf16[2,256,128]{2,1,0:T(8,128)(2,1)S(1)}, u32[]{:S(2)}, u32[]{:S(2)}) %collective-permute-start.8) | collective-permute-done | bytes 131104 | tf_op jit(solution)/shard_map/ppermute | solution.py:45
  53.7 5.2 %collective-permute-done.10 = bf16[2,256,128]{2,1,0:T(8,128)(2,1)S(1)} collective-permute-done((bf16[2,256,128]{2,1,0:T(8,128)(2,1)S(1)}, bf16[2,256,128]{2,1,0:T(8,128)(2,1)S(1)}, u32[]{:S(2)}, u32[]{:S(2)}) %collective-permute-start.10) | collective-permute-done | bytes 131104 | tf_op jit(solution)/shard_map/ppermute | solution.py:45
  58.8 0.0 collective-permute-done.9
  58.8 0.1 fusion.1
  58.9 0.2 copy.11
  59.1 0.7 %copy.14 = f32[16,8,4,128]{3,1,2,0:T(8,128)} copy(f32[16,8,4,128]{3,2,1,0:T(4,128)S(1)} %bitcast.12) | data formatting | bytes 524288
  59.8 6.4 %all-to-all-done.1 = bf16[16,128,256]{2,1,0:T(8,128)(2,1)S(1)} async-done(((bf16[16,128,256]{2,1,0:T(8,128)(2,1)}), bf16[16,128,256]{2,1,0:T(8,128)(2,1)S(1)}, u32[]{:S(2)}, u32[]{:S(2)}) %all-to-all-start.1) | async-done | bytes 1048608 | tf_op jit(solution)/shard_map/all_to_all | solution.py:58
  66.2 0.8 %convert_reduce_fusion = (f32[128,128]{1,0:T(8,128)}, f32[128,128]{1,0:T(8,128)}) fusion(bf16[16,128,256]{2,1,0:T(8,128)(2,1)S(1)} %all-to-all-done.1), kind=kLoop, calls=%fused_computation | loop fusion | flops 1015808 | bytes 1179648 | tf_op jit(solution)/shard_map/reduce_sum | solution.py:345
  (1 shorter events, 0.0 us)
Async XLA Ops:
  3.2 7.3 %copy-start = (bf16[2,272,256]{2,1,0:T(8,128)(2,1)S(1)}, bf16[2,272,256]{2,1,0:T(8,128)(2,1)}, u32[]{:S(2)}) copy-start(bf16[2,272,256]{2,1,0:T(8,128)(2,1)} %get-tuple-element.8.refs_0_) | copy-start | bytes 835588
  3.2 28.0 %all-to-all-start = ((bf16[16,144,256]{2,1,0:T(8,128)(2,1)}), bf16[16,144,256]{2,1,0:T(8,128)(2,1)}, u32[]{:S(2)}, u32[]{:S(2)}) async-start(bf16[16,144,256]{2,1,0:T(8,128)(2,1)} %get-tuple-element.9), calls=%async_computation | async-start | bytes 2359296 | tf_op jit(solution)/shard_map/all_to_all | solution.py:58
  10.5 15.7 %collective-permute-start.2 = (bf16[2,272,256]{2,1,0:T(8,128)(2,1)S(1)}, bf16[2,272,256]{2,1,0:T(8,128)(2,1)S(1)}, u32[]{:S(2)}, u32[]{:S(2)}) collective-permute-start(bf16[2,272,256]{2,1,0:T(8,128)(2,1)S(1)} %copy-done), channel_id=1, source_target_pairs={{0,80},{1,81},{2,82},{3,83},{4,84},{5,85},{6,86},{7,87},{8,88},{9,... | collective-permute-start | bytes 835592 | tf_op jit(solution)/shard_map/ppermute | solution.py:45
  14.6 11.6 %collective-permute-start.1 = (bf16[2,272,256]{2,1,0:T(8,128)(2,1)S(1)}, bf16[2,272,256]{2,1,0:T(8,128)(2,1)S(1)}, u32[]{:S(2)}, u32[]{:S(2)}) collective-permute-start(bf16[2,272,256]{2,1,0:T(8,128)(2,1)S(1)} %copy-done), channel_id=1, source_target_pairs={{0,16},{1,17},{2,18},{3,19},{4,20},{5,21},{6,22},{7,23},{8,24},{9,... | collective-permute-start | bytes 835592 | tf_op jit(solution)/shard_map/ppermute | solution.py:45
  14.6 15.0 %collective-permute-start = (bf16[2,272,256]{2,1,0:T(8,128)(2,1)S(1)}, bf16[2,272,256]{2,1,0:T(8,128)(2,1)S(1)}, u32[]{:S(2)}, u32[]{:S(2)}) collective-permute-start(bf16[2,272,256]{2,1,0:T(8,128)(2,1)S(1)} %copy-done), channel_id=1, source_target_pairs={{0,64},{1,65},{2,66},{3,67},{4,68},{5,69},{6,70},{7,71},{8,72},{9,... | collective-permute-start | bytes 835592 | tf_op jit(solution)/shard_map/ppermute | solution.py:45
  15.9 13.8 %collective-permute-start.3 = (bf16[2,272,256]{2,1,0:T(8,128)(2,1)S(1)}, bf16[2,272,256]{2,1,0:T(8,128)(2,1)S(1)}, u32[]{:S(2)}, u32[]{:S(2)}) collective-permute-start(bf16[2,272,256]{2,1,0:T(8,128)(2,1)S(1)} %copy-done), channel_id=1, source_target_pairs={{0,32},{1,33},{2,34},{3,35},{4,36},{5,37},{6,38},{7,39},{8,40},{9,... | collective-permute-start | bytes 835592 | tf_op jit(solution)/shard_map/ppermute | solution.py:53
  26.2 3.4 %collective-permute-start.6 = (bf16[2,272,256]{2,1,0:T(8,128)(2,1)S(1)}, bf16[2,272,256]{2,1,0:T(8,128)(2,1)S(1)}, u32[]{:S(2)}, u32[]{:S(2)}) collective-permute-start(bf16[2,272,256]{2,1,0:T(8,128)(2,1)S(1)} %collective-permute-done.2.refs_3_), channel_id=1, source_target_pairs={{0,32},{1,33},{2,34},{3,35},{4,36},{5,37},{6,38},{7,39},{8,40},{9,... | collective-permute-start | bytes 835592 | tf_op jit(solution)/shard_map/ppermute | solution.py:53
  26.3 3.4 %collective-permute-start.5 = (bf16[2,272,256]{2,1,0:T(8,128)(2,1)S(1)}, bf16[2,272,256]{2,1,0:T(8,128)(2,1)S(1)}, u32[]{:S(2)}, u32[]{:S(2)}) collective-permute-start(bf16[2,272,256]{2,1,0:T(8,128)(2,1)S(1)} %collective-permute-done.1.refs_2_), channel_id=1, source_target_pairs={{0,32},{1,33},{2,34},{3,35},{4,36},{5,37},{6,38},{7,39},{8,40},{9,... | collective-permute-start | bytes 835592 | tf_op jit(solution)/shard_map/ppermute | solution.py:53
  29.7 1.6 %collective-permute-start.4 = (bf16[2,272,256]{2,1,0:T(8,128)(2,1)S(1)}, bf16[2,272,256]{2,1,0:T(8,128)(2,1)S(1)}, u32[]{:S(2)}, u32[]{:S(2)}) collective-permute-start(bf16[2,272,256]{2,1,0:T(8,128)(2,1)S(1)} %collective-permute-done.refs_1_), channel_id=1, source_target_pairs={{0,32},{1,33},{2,34},{3,35},{4,36},{5,37},{6,38},{7,39},{8,40},{9,... | collective-permute-start | bytes 835592 | tf_op jit(solution)/shard_map/ppermute | solution.py:53
  39.7 8.0 %collective-permute-start.7 = (bf16[8,256,128]{2,1,0:T(8,128)(2,1)S(1)}, bf16[8,256,128]{2,1,0:T(8,128)(2,1)S(1)}, u32[]{:S(2)}, u32[]{:S(2)}) collective-permute-start(bf16[8,256,128]{2,1,0:T(8,128)(2,1)S(1)} %get-tuple-element.11), channel_id=1, source_target_pairs={{0,32},{1,33},{2,34},{3,35},{4,36},{5,37},{6,38},{7,39},{8,40},{9,... | collective-permute-start | bytes 1572872 | tf_op jit(solution)/shard_map/ppermute | solution.py:53
  39.9 26.3 %all-to-all-start.1 = ((bf16[16,128,256]{2,1,0:T(8,128)(2,1)}), bf16[16,128,256]{2,1,0:T(8,128)(2,1)S(1)}, u32[]{:S(2)}, u32[]{:S(2)}) async-start(bf16[16,128,256]{2,1,0:T(8,128)(2,1)} %get-tuple-element.12), calls=%async_computation.1 | async-start | bytes 2097152 | tf_op jit(solution)/shard_map/all_to_all | solution.py:58
  48.0 5.7 %collective-permute-start.8 = (bf16[2,256,128]{2,1,0:T(8,128)(2,1)S(1)}, bf16[2,256,128]{2,1,0:T(8,128)(2,1)S(1)}, u32[]{:S(2)}, u32[]{:S(2)}) collective-permute-start(bf16[2,256,128]{2,1,0:T(8,128)(2,1)S(1)} %get-tuple-element.17), channel_id=1, source_target_pairs={{0,80},{1,81},{2,82},{3,83},{4,84},{5,85},{6,86},{7,87},{8,88},{9,... | collective-permute-start | bytes 393224 | tf_op jit(solution)/shard_map/ppermute | solution.py:45
  49.9 8.9 %collective-permute-start.10 = (bf16[2,256,128]{2,1,0:T(8,128)(2,1)S(1)}, bf16[2,256,128]{2,1,0:T(8,128)(2,1)S(1)}, u32[]{:S(2)}, u32[]{:S(2)}) collective-permute-start(bf16[2,256,128]{2,1,0:T(8,128)(2,1)S(1)} %get-tuple-element.18), channel_id=1, source_target_pairs={{0,64},{1,65},{2,66},{3,67},{4,68},{5,69},{6,70},{7,71},{8,72},{9,... | collective-permute-start | bytes 393224 | tf_op jit(solution)/shard_map/ppermute | solution.py:45
  50.1 8.7 %collective-permute-start.9 = (bf16[2,256,128]{2,1,0:T(8,128)(2,1)S(1)}, bf16[2,256,128]{2,1,0:T(8,128)(2,1)S(1)}, u32[]{:S(2)}, u32[]{:S(2)}) collective-permute-start(bf16[2,256,128]{2,1,0:T(8,128)(2,1)S(1)} %get-tuple-element.19), channel_id=1, source_target_pairs={{0,16},{1,17},{2,18},{3,19},{4,20},{5,21},{6,22},{7,23},{8,24},{9,... | collective-permute-start | bytes 393224 | tf_op jit(solution)/shard_map/ppermute | solution.py:45
